TPU v7x, 256 devices: a whole 4x4x8 slice. The times are simulated.
256 devices in a mesh: lat: 32 (over y, x, core), lon: 8 (over z).
Axes of the slice: x: 4, y: 4, z: 8, core: 2. Of those that a mesh axis runs over, the one named last changes fastest.
Arguments:
- snapshots: float32 [1024, 512, 1024], P(None, 'lat', 'lon'), may hold values from -60 to 60
- land_sea: int32 [512, 1024], P('lat', 'lon'), may hold values 0 or 1
- penalty: float32 [512, 1024], P('lat', 'lon'), may hold values from 0.003 to 0.03
- initial_basis: float32 [64, 512, 1024], P(None, 'lat', 'lon'), may hold values from -6 to 6
Outputs:
- leading_basis: float32 [64, 512, 1024], P(None, 'lat', 'lon')
- rayleigh_matrix: float32 [64, 64], replicated
All inputs are finite; a program needn't handle non-finite values. No bound on the sum of `land_sea` on one device may be relied on, other than what follows from the above.
Results may differ from a plain program's by a relative error of at most 0.0003.
Values sent between devices are 32-bit elements; how exact they have to be, the bound alone decides.
No kernel may reach another device: no remote copies, remote signals or barrier semaphores. Data moves between devices by JAX's collectives and lax.ppermute only.
A program may use at most 64 MiB of HBM per device.

v0:
```python
import jax
import jax.numpy as jnp
from jax import lax
from jax.experimental import pallas as pl
from jax.experimental.pallas import tpu as pltpu
from jax.sharding import Mesh, PartitionSpec as P

K = 64
NSNAP = 1024
NPTS = 524288
ROWS = 16
LANES = 128
PTS = ROWS * LANES
BLOCK = 256
NBLOCK = NSNAP // BLOCK
SHARD = 24
F32 = jnp.float32
BF16 = jnp.bfloat16
HIGHEST = lax.Precision.HIGHEST
CHIPS = ("y", "x")
LAT = ("y", "x", "core")
SWAP = [(0, 1), (1, 0)]
VMEM_LIMIT = 40 * 1024 * 1024


def parts(value):
    high = value.astype(BF16)
    return high, (value - high.astype(F32)).astype(BF16)


def dot_nt(left, right, precision=None):
    return lax.dot_general(
        left, right, (((1,), (1,)), ((), ())), precision=precision, preferred_element_type=F32
    )


def dot_nn(left, right, precision=None):
    return lax.dot_general(
        left, right, (((1,), (0,)), ((), ())), precision=precision, preferred_element_type=F32
    )


def lane_of(shape):
    return lax.broadcasted_iota(jnp.int32, shape, len(shape) - 1)


def cols(a):
    return slice(a * LANES, (a + 1) * LANES)


def store_split(split_ref, a, value):
    high, low = parts(value)
    split_ref[0:K, cols(a)] = high
    split_ref[K : 2 * K, cols(a)] = low


def edge_columns(field_ref):
    lane = lane_of((K, LANES))
    first = jnp.zeros((K, LANES), F32)
    last = jnp.zeros((K, LANES), F32)
    for a in range(ROWS):
        block = field_ref[:, cols(a)]
        first = jnp.where(lane == a, block[:, 0:1], first)
        last = jnp.where(lane == a, block[:, LANES - 1 : LANES], last)
    return first, last


def smooth(field_ref, a, north, south, west, east):
    lane = lane_of((K, LANES))
    here = field_ref[:, cols(a)]
    up = field_ref[:, cols(a - 1)] if a > 0 else north
    down = field_ref[:, cols(a + 1)] if a < ROWS - 1 else south
    left = pltpu.roll(here, 1, 1)
    right = pltpu.roll(here, LANES - 1, 1)
    left = jnp.where(lane == 0, 0.0 if west is None else west[:, a : a + 1], left)
    right = jnp.where(lane == LANES - 1, 0.0 if east is None else east[:, a : a + 1], right)
    total = left + right
    if up is not None:
        total = total + up
    if down is not None:
        total = total + down
    return total - 4.0 * here


def hand_out(pay, mine, other):
    me = lax.axis_index("core")
    mine[...] = pay[me]
    other[...] = pay[1 - me]


def take_in(mine, other, full):
    me = lax.axis_index("core")
    full[me] = mine[...]
    full[1 - me] = other[...]


def row_of_shards(full, row):
    return jnp.concatenate(
        [full[half, chip, row : row + 1, :] for half in range(2) for chip in range(16)], axis=0
    )


def put_square(pay, row, doubled):
    packed = jnp.where(lane_of((K // 2, LANES)) < K, doubled[0 : K // 2], doubled[K // 2 : K])
    for half in range(2):
        for chip in range(16):
            at = half * 16 + chip
            pay[half, chip, row : row + 1, :] = packed[at : at + 1]


def square_of(full, row):
    packed = row_of_shards(full, row)
    return jnp.concatenate([packed, pltpu.roll(packed, K, 1)], axis=0)


def folded(product):
    rows = product[0:K] + product[K : 2 * K]
    return rows + pltpu.roll(rows, K, 1)


def inverse_factor(square):
    lane = lane_of((8, LANES))
    sub = lax.broadcasted_iota(jnp.int32, (8, LANES), 0)
    blocks = []
    for b in range(K // 8):
        unit = jnp.where(lane - K == sub + 8 * b, 1.0, 0.0)
        blocks.append(jnp.where(lane < K, square[8 * b : 8 * b + 8] * (1.0 / NPTS), unit))
    for j in range(K):
        home, inner = j // 8, j % 8
        row = blocks[home][inner : inner + 1, :]
        scaled = row / blocks[home][inner : inner + 1, j : j + 1]
        for b in range(home, K // 8):
            column = blocks[b][:, j : j + 1]
            if b == home:
                if inner == 7:
                    continue
                column = jnp.where(sub > inner, column, 0.0)
            blocks[b] = blocks[b] - column * scaled
    done = []
    for b in range(K // 8):
        diagonal = jnp.sum(jnp.where(lane == sub + 8 * b, blocks[b], 0.0), axis=1, keepdims=True)
        done.append(blocks[b] * lax.rsqrt(diagonal))
    return pltpu.roll(jnp.concatenate(done, axis=0), K, 1)[:, 0:K]


def put_coefficients(pay, block, both):
    half = block % 2
    summed = both + pltpu.roll(both, K, 1)
    summed = summed.reshape(16, 16, LANES)
    if block < 2:
        pay[half, :, 0:16, :] = summed
    else:
        old = pay[half, :, 0:16, :]
        pay[half, :, 0:16, :] = jnp.where(lane_of(old.shape) < K, old, summed)


def coefficients_of(full, spread):
    packed = full[:, :, 0:16, :].reshape(NSNAP // 2, LANES)
    turned = packed.T
    if spread is not None:
        for block in range(NBLOCK):
            top = (block // 2) * K
            left = (block % 2) * BLOCK
            high, low = parts(turned[top : top + K, left : left + BLOCK])
            spread[block, 0:K, :] = high
            spread[block, K : 2 * K, :] = low
    return turned


def begin_kernel(
    snap, basis, sea, split_out, flat, top, bottom, first, last, mine, other, split, pay
):
    step = pl.program_id(0)

    @pl.when(step == 0)
    def _():
        pay[...] = jnp.zeros_like(pay)
        for a in range(ROWS):
            value = basis[pl.ds(a, K, stride=ROWS), :] * sea[a : a + 1, :].astype(F32)
            flat[:, cols(a)] = value
            store_split(split, a, value)
        top[...] = flat[:, cols(0)]
        bottom[...] = flat[:, cols(ROWS - 1)]
        first[...], last[...] = edge_columns(flat)

    depth = BLOCK // 2
    for a in range(ROWS):
        high, low = parts(snap[pl.ds(a, depth, stride=ROWS), :])
        split_out[0, 0, :, cols(a)] = high
        split_out[0, 1, :, cols(a)] = low
    both = dot_nt(split_out[0, 0], split[...]) + dot_nt(split_out[0, 1], split[...])
    summed = (both + pltpu.roll(both, K, 1)).reshape(8, 16, LANES)
    half = (step // 2) % 2
    at = pl.ds((step % 2) * 8, 8)
    keep = (lane_of(summed.shape) < K) & (step >= 4)
    pay[half, at, 0:16, :] = jnp.where(keep, pay[half, at, 0:16, :], summed)

    @pl.when(step == pl.num_programs(0) - 1)
    def _():
        hand_out(pay, mine, other)


def whole(shape):
    return pl.BlockSpec(shape, lambda i: (0,) * len(shape))


def begin(snapshots, basis, sea):
    depth = BLOCK // 2
    halo = jax.ShapeDtypeStruct((K, LANES), F32)
    share = jax.ShapeDtypeStruct((16, SHARD, LANES), F32)
    return pl.pallas_call(
        begin_kernel,
        grid=(NSNAP // depth,),
        in_specs=[
            pl.BlockSpec((depth * ROWS, LANES), lambda i: (i, 0)),
            whole((K * ROWS, LANES)),
            whole((ROWS, LANES)),
        ],
        out_specs=[
            pl.BlockSpec((1, 2, depth, PTS), lambda i: (i // 2, 0, i % 2, 0)),
            whole((K, PTS)),
            *[whole((K, LANES))] * 4,
            *[whole((16, SHARD, LANES))] * 2,
        ],
        out_shape=[
            jax.ShapeDtypeStruct((NBLOCK, 2, BLOCK, PTS), BF16),
            jax.ShapeDtypeStruct((K, PTS), F32),
            halo,
            halo,
            halo,
            halo,
            share,
            share,
        ],
        scratch_shapes=[
            pltpu.VMEM((2 * K, PTS), BF16),
            pltpu.VMEM((2, 16, SHARD, LANES), F32),
        ],
        compiler_params=pltpu.CompilerParams(vmem_limit_bytes=VMEM_LIMIT),
        name="split_and_project",
    )(snapshots.reshape(NSNAP * ROWS, LANES), basis.reshape(K * ROWS, LANES), sea)


def copy_of(snap, held, sems, block):
    return pltpu.make_async_copy(snap.at[block], held.at[block], sems.at[block])


def expand(spread, snap, held, sems, total):
    width = 512
    for block in range(NBLOCK):
        copy_of(snap, held, sems, block).wait()
        for left in range(0, PTS, width):
            at = slice(left, left + width)
            both = dot_nn(spread[block], held[block, 0, :, at]) + dot_nn(
                spread[block], held[block, 1, :, at]
            )
            piece = both[0:K] + both[K : 2 * K]
            total[:, at] = piece if block == 0 else total[:, at] + piece


def project(held, split, pay):
    for block in range(NBLOCK):
        both = dot_nt(held[block, 0], split[...]) + dot_nt(held[block, 1], split[...])
        put_coefficients(pay, block, both)


def applied_field(total, prev, sides, sea, pen, out):
    north, south, west, east = (side[...] for side in sides)
    for a in range(ROWS):
        lap = smooth(prev, a, north, south, west, east)
        mask = sea[a : a + 1, :].astype(F32)
        out[:, cols(a)] = mask * (total[:, cols(a)] * (1.0 / NPTS) + pen[a : a + 1, :] * lap)


def first_kernel(
    got_mine, got_other, snap, prev, north, south, west, east, sea, pen,
    field, top, bottom, first, last, mine, other,
    full, held, spread, total, split, pay, sems,
):
    for block in range(NBLOCK):
        copy_of(snap, held, sems, block).start()
    take_in(got_mine, got_other, full)
    coefficients_of(full, spread)
    expand(spread, snap, held, sems, total)
    applied_field(total, prev, (north, south, west, east), sea, pen, field)
    for a in range(ROWS):
        store_split(split, a, field[:, cols(a)])
    top[...] = field[:, cols(0)]
    bottom[...] = field[:, cols(ROWS - 1)]
    first[...], last[...] = edge_columns(field)
    pay[...] = jnp.zeros_like(pay)
    put_square(pay, 16, folded(dot_nt(split[...], split[...])))
    project(held, split, pay)
    hand_out(pay, mine, other)


def scratch_for_expand():
    return [
        pltpu.VMEM((2, 16, SHARD, LANES), F32),
        pltpu.VMEM((NBLOCK, 2, BLOCK, PTS), BF16),
        pltpu.VMEM((NBLOCK, 2 * K, BLOCK), BF16),
        pltpu.VMEM((K, PTS), F32),
    ]


VM = pl.BlockSpec(memory_space=pltpu.VMEM)
HB = pl.BlockSpec(memory_space=pl.ANY)


def first_step(got, snap, prev, sides, sea, pen):
    halo = jax.ShapeDtypeStruct((K, LANES), F32)
    share = jax.ShapeDtypeStruct((16, SHARD, LANES), F32)
    return pl.pallas_call(
        first_kernel,
        in_specs=[VM, VM, HB, *[VM] * 7],
        out_specs=[VM] * 7,
        out_shape=[jax.ShapeDtypeStruct((K, PTS), F32), halo, halo, halo, halo, share, share],
        scratch_shapes=[
            *scratch_for_expand(),
            pltpu.VMEM((2 * K, PTS), BF16),
            pltpu.VMEM((2, 16, SHARD, LANES), F32),
            pltpu.SemaphoreType.DMA((NBLOCK,)),
        ],
        compiler_params=pltpu.CompilerParams(vmem_limit_bytes=VMEM_LIMIT),
        name="expand_and_project",
    )(*got, snap, prev, *sides, sea, pen)


def second_kernel(
    got_mine, got_other, snap, prev, north, south, west, east, sea, pen,
    field, bottom, last,
    full, held, spread, total, raw, sems,
):
    for block in range(NBLOCK):
        copy_of(snap, held, sems, block).start()
    take_in(got_mine, got_other, full)
    coefficients_of(full, spread)
    inverse = inverse_factor(square_of(full, 16))
    expand(spread, snap, held, sems, total)
    applied_field(total, prev, (north, south, west, east), sea, pen, raw)
    field[...] = dot_nn(inverse, raw[...], HIGHEST)
    bottom[0:K, :] = field[:, cols(ROWS - 1)]
    bottom[K : 2 * K, :] = field[:, cols(ROWS - 1)] * pen[ROWS - 1 : ROWS, :]
    _, last[0:K, :] = edge_columns(field)
    for a in range(ROWS):
        raw[:, cols(a)] = field[:, cols(a)] * pen[a : a + 1, :]
    _, last[K : 2 * K, :] = edge_columns(raw)


def second_step(got, snap, prev, sides, sea, pen):
    halo = jax.ShapeDtypeStruct((2 * K, LANES), F32)
    return pl.pallas_call(
        second_kernel,
        in_specs=[VM, VM, HB, *[VM] * 7],
        out_specs=[VM] * 3,
        out_shape=[jax.ShapeDtypeStruct((K, PTS), F32), halo, halo],
        scratch_shapes=[
            *scratch_for_expand(),
            pltpu.VMEM((K, PTS), F32),
            pltpu.SemaphoreType.DMA((NBLOCK,)),
        ],
        compiler_params=pltpu.CompilerParams(vmem_limit_bytes=VMEM_LIMIT),
        name="factor_and_expand",
    )(*got, snap, prev, *sides, sea, pen)


def project_kernel(snap, field, pay, held, split, sems):
    for block in range(NBLOCK):
        copy_of(snap, held, sems, block).start()
    for a in range(ROWS):
        store_split(split, a, field[:, cols(a)])
    pay[...] = jnp.zeros_like(pay)
    put_square(pay, 16, folded(dot_nt(split[...], split[...])))
    for block in range(NBLOCK):
        copy_of(snap, held, sems, block).wait()
        both = dot_nt(held[block, 0], split[...]) + dot_nt(held[block, 1], split[...])
        put_coefficients(pay, block, both)


def project_step(snap, field):
    return pl.pallas_call(
        project_kernel,
        in_specs=[HB, VM],
        out_specs=VM,
        out_shape=jax.ShapeDtypeStruct((2, 16, SHARD, LANES), F32),
        scratch_shapes=[
            pltpu.VMEM((NBLOCK, 2, BLOCK, PTS), BF16),
            pltpu.VMEM((2 * K, PTS), BF16),
            pltpu.SemaphoreType.DMA((NBLOCK,)),
        ],
        compiler_params=pltpu.CompilerParams(vmem_limit_bytes=VMEM_LIMIT),
        name="project",
    )(snap, field)


def rough_kernel(field, north, west, pen, base, mine, other, left, right, pay):
    def put(at, first, second):
        high, low = parts(first)
        left[0:K, cols(at)] = high
        left[K : 2 * K, cols(at)] = low
        high, low = parts(second)
        right[0:K, cols(at)] = high
        right[K : 2 * K, cols(at)] = low

    first = jnp.zeros((K, LANES), F32)
    first_weighted = jnp.zeros((K, LANES), F32)
    lane = lane_of((K, LANES))
    for a in range(ROWS):
        here = field[:, cols(a)]
        weighted = here * pen[a : a + 1, :]
        put(a, weighted, smooth(field, a, None, None, None, None))
        first = jnp.where(lane == a, here[:, 0:1], first)
        first_weighted = jnp.where(lane == a, weighted[:, 0:1], first_weighted)
        if a == 0:
            put(ROWS, weighted, north[0:K, :])
            put(ROWS + 1, north[K : 2 * K, :], here)
    put(ROWS + 2, first_weighted, west[0:K, :])
    put(ROWS + 3, west[K : 2 * K, :], first)
    pay[...] = base[...]
    put_square(pay, 17, folded(dot_nt(left[...], right[...])))
    hand_out(pay, mine, other)


def rough_step(field, north, west, pen, base):
    share = jax.ShapeDtypeStruct((16, SHARD, LANES), F32)
    return pl.pallas_call(
        rough_kernel,
        in_specs=[VM] * 5,
        out_specs=[VM] * 2,
        out_shape=[share, share],
        scratch_shapes=[
            pltpu.VMEM((2 * K, PTS + 4 * LANES), BF16),
            pltpu.VMEM((2 * K, PTS + 4 * LANES), BF16),
            pltpu.VMEM((2, 16, SHARD, LANES), F32),
        ],
        compiler_params=pltpu.CompilerParams(vmem_limit_bytes=VMEM_LIMIT),
        name="roughness_products",
    )(field, north, west, pen, base)


def last_kernel(got_mine, got_other, field, basis, matrix, full):
    take_in(got_mine, got_other, full)
    inverse = inverse_factor(square_of(full, 16))
    solved = dot_nn(inverse, field[...], HIGHEST)
    for a in range(ROWS):
        basis[pl.ds(a, K, stride=ROWS), :] = solved[:, cols(a)]
    turned = coefficients_of(full, None)
    rough = square_of(full, 17)[:, 0:K]
    low, high = turned[0:K], turned[K : 2 * K]
    gram = dot_nt(low, low, HIGHEST) + dot_nt(high, high, HIGHEST)
    middle = (gram * (1.0 / NPTS) + rough) * (1.0 / NPTS)
    matrix[...] = dot_nt(dot_nn(inverse, middle, HIGHEST), inverse, HIGHEST)


def last_step(got, field):
    basis, matrix = pl.pallas_call(
        last_kernel,
        in_specs=[VM] * 3,
        out_specs=[VM] * 2,
        out_shape=[
            jax.ShapeDtypeStruct((K * ROWS, LANES), F32),
            jax.ShapeDtypeStruct((K, K), F32),
        ],
        scratch_shapes=[pltpu.VMEM((2, 16, SHARD, LANES), F32)],
        compiler_params=pltpu.CompilerParams(vmem_limit_bytes=VMEM_LIMIT),
        name="factor_and_finish",
    )(*got, field)
    return basis.reshape(K, ROWS, LANES), matrix


def to_each(value, axis, count):
    return lax.all_to_all(
        jnp.broadcast_to(value[None], (count, *value.shape)), axis, 0, 0, tiled=True
    )


def summed_everywhere(mine, other):
    pair = mine + lax.ppermute(other, "core", SWAP)
    share = lax.all_to_all(pair, CHIPS, 0, 0, tiled=True).sum(axis=0)
    share = to_each(share, "z", 8).sum(axis=0)
    half = to_each(share, CHIPS, 16)
    return half, lax.ppermute(half, "core", SWAP)


def from_below(value, axis, count):
    return lax.ppermute(value, axis, [(i, i + 1) for i in range(count - 1)])


def from_above(value, axis, count):
    return lax.ppermute(value, axis, [(i + 1, i) for i in range(count - 1)])


def sides_of(top, bottom, first, last):
    return (
        from_below(bottom, LAT, 32),
        from_above(top, LAT, 32),
        from_below(last, "z", 8),
        from_above(first, "z", 8),
    )


def local(snapshots, land_sea, penalty, initial_basis):
    snap, start, *edges, mine, other = begin(snapshots, initial_basis, land_sea)
    sides = sides_of(*edges)
    got = summed_everywhere(mine, other)
    applied, *edges, mine, other = first_step(got, snap, start, sides, land_sea, penalty)
    sides = sides_of(*edges)
    got = summed_everywhere(mine, other)
    applied, bottom, last = second_step(got, snap, applied, sides, land_sea, penalty)
    north = from_below(bottom, LAT, 32)
    west = from_below(last, "z", 8)
    base = project_step(snap, applied)
    mine, other = rough_step(applied, north, west, penalty, base)
    got = summed_everywhere(mine, other)
    return last_step(got, applied)


def solution(mesh):
    split_mesh = Mesh(mesh.devices.reshape(4, 4, 2, 8), ("y", "x", "core", "z"))
    flat = P(LAT, "z")
    deep = P(None, LAT, "z")
    return jax.shard_map(
        local,
        mesh=split_mesh,
        in_specs=(deep, flat, flat, deep),
        out_specs=(deep, P()),
        check_vma=False,
    )
```

profile of v0, /device:TPU:1, one launch (start us, length us, event | category | flops | bytes accessed | tf_op | source)
XLA Modules:
  0.0 207.0 jit_solution(18389428274386331764)
XLA Ops:
  2.4 9.7 %split_and_project.1 = (bf16[4,2,256,2048]{3,2,1,0:T(8,128)(2,1)S(1)}, f32[64,2048]{1,0:T(8,128)S(1)}, f32[64,128]{1,0:T(8,128)S(1)}, f32[64,128]{1,0:T(8,128)S(...) custom-call(f32[16384,128]{1,0:T(8,128)} %bitcast.4, ...), custom_call_target="tpu_custom_call" | custom-call | tf_op jit(solution)/shard_map/split_and_project/pallas_call | solution.py:211
  12.1 3.2 %copy-done = bf16[4,2,256,2048]{3,2,1,0:T(8,128)(2,1)} copy-done((bf16[4,2,256,2048]{3,2,1,0:T(8,128)(2,1)}, bf16[4,2,256,2048]{3,2,1,0:T(8,128)(2,1)S(1)}, u32[]{:S(2)}) %copy-start) | copy-done | bytes 8388632
  15.3 3.2 %collective-permute-start = (f32[16,24,128]{2,1,0:T(8,128)S(1)}, f32[16,24,128]{2,1,0:T(8,128)S(1)}, u32[]{:S(2)}, u32[]{:S(2)}) collective-permute-start(f32[16,24,128]{2,1,0:T(8,128)S(1)} %get-tuple-element.25), channel_id=1, source_target_pairs={{0,8},{8,0},{1,9},{9,1},{2,10},{10,2},{3,11},{11,3},{4,12},{12,4},... | collective-permute-start | bytes 589832 | tf_op jit(solution)/shard_map/ppermute | solution.py:478
  19.7 12.0 %all_to_all.45 = f32[16,24,128]{2,1,0:T(8,128)S(1)} all-to-all(f32[16,24,128]{2,1,0:T(8,128)S(1)} %add.9), channel_id=1, replica_groups=mesh['y'=4,'x'=4,'core'=2,'z'=8] {'y','x'}, dimensions={0} | all-to-all | bytes 393216 | tf_op jit(solution)/shard_map/all_to_all | solution.py:479
  31.7 15.7 %all_to_all.46 = f32[8,24,128]{2,1,0:T(8,128)S(1)} all-to-all(f32[8,24,128]{2,1,0:T(8,128)S(1)} %broadcast_in_dim.12), channel_id=1, replica_groups=mesh['y'=4,'x'=4,'core'=2,'z'=8] {'z'}, dimensions={0} | all-to-all | bytes 196608 | tf_op jit(solution)/shard_map/all_to_all | solution.py:472
  47.4 10.1 %all_to_all.47.got_mine = f32[16,24,128]{2,1,0:T(8,128)S(1)} all-to-all(f32[16,24,128]{2,1,0:T(8,128)S(1)} %broadcast_in_dim.13), channel_id=1, replica_groups=mesh['y'=4,'x'=4,'core'=2,'z'=8] {'y','x'}, dimensions={0} | all-to-all | bytes 393216 | tf_op jit(solution)/shard_map/all_to_all | solution.py:472
  57.6 4.3 %collective-permute-start.1 = (f32[16,24,128]{2,1,0:T(8,128)S(1)}, f32[16,24,128]{2,1,0:T(8,128)S(1)}, u32[]{:S(2)}, u32[]{:S(2)}) collective-permute-start(f32[16,24,128]{2,1,0:T(8,128)S(1)} %all_to_all.47.got_mine), channel_id=1, source_target_pairs={{0,8},{8,0},{1,9},{9,1},{2,10},{10,2},{3,11},{11,3},{4,12},{12,4},... | collective-permute-start | bytes 589832 | tf_op jit(solution)/shard_map/ppermute | solution.py:482
  61.9 2.1 collective-permute-start.2
  64.0 2.2 %collective-permute-start.3 = (f32[64,128]{1,0:T(8,128)S(1)}, f32[64,128]{1,0:T(8,128)S(1)}, u32[]{:S(2)}, u32[]{:S(2)}) collective-permute-start(f32[64,128]{1,0:T(8,128)S(1)} %get-tuple-element.29), channel_id=1, source_target_pairs={{8,0},{16,8},{24,16},{32,24},{40,32},{48,40},{56,48},{64,56},{72,6... | collective-permute-start | bytes 98312 | tf_op jit(solution)/shard_map/ppermute | solution.py:490
  66.2 2.2 %collective-permute-start.4 = (f32[64,128]{1,0:T(8,128)S(1)}, f32[64,128]{1,0:T(8,128)S(1)}, u32[]{:S(2)}, u32[]{:S(2)}) collective-permute-start(f32[64,128]{1,0:T(8,128)S(1)} %get-tuple-element.30), channel_id=1, source_target_pairs={{0,1},{1,2},{2,3},{3,4},{4,5},{5,6},{6,7},{8,9},{9,10},{10,11},{11... | collective-permute-start | bytes 98312 | tf_op jit(solution)/shard_map/ppermute | solution.py:486
  69.7 3.8 %collective-permute-done.5.east = f32[64,128]{1,0:T(8,128)S(1)} collective-permute-done((f32[64,128]{1,0:T(8,128)S(1)}, f32[64,128]{1,0:T(8,128)S(1)}, u32[]{:S(2)}, u32[]{:S(2)}) %collective-permute-start.5) | collective-permute-done | bytes 32800 | tf_op jit(solution)/shard_map/ppermute | solution.py:490
  73.6 3.4 %copy-done.1 = bf16[4,2,256,2048]{3,2,1,0:T(8,128)(2,1)S(1)} copy-done((bf16[4,2,256,2048]{3,2,1,0:T(8,128)(2,1)S(1)}, bf16[4,2,256,2048]{3,2,1,0:T(8,128)(2,1)}, u32[]{:S(2)}) %copy-start.1) | copy-done | bytes 8388632
  77.0 5.0 %expand_and_project.1 = (f32[64,2048]{1,0:T(8,128)S(1)}, f32[64,128]{1,0:T(8,128)S(1)}, f32[64,128]{1,0:T(8,128)S(1)}, f32[64,128]{1,0:T(8,128)S(1)}, f32[64,128...) custom-call(f32[16,24,128]{2,1,0:T(8,128)S(1)} %all_to_all.47.got_mine, ...), custom_call_target="tpu_custom_call" | custom-call | tf_op jit(solution)/shard_map/expand_and_project/pallas_call | solution.py:313
  83.7 12.7 %all_to_all.48 = f32[16,24,128]{2,1,0:T(8,128)S(1)} all-to-all(f32[16,24,128]{2,1,0:T(8,128)S(1)} %add.10), channel_id=1, replica_groups=mesh['y'=4,'x'=4,'core'=2,'z'=8] {'y','x'}, dimensions={0} | all-to-all | bytes 393216 | tf_op jit(solution)/shard_map/all_to_all | solution.py:479
  96.4 10.1 %all_to_all.49 = f32[8,24,128]{2,1,0:T(8,128)S(1)} all-to-all(f32[8,24,128]{2,1,0:T(8,128)S(1)} %broadcast_in_dim.14), channel_id=1, replica_groups=mesh['y'=4,'x'=4,'core'=2,'z'=8] {'z'}, dimensions={0} | all-to-all | bytes 196608 | tf_op jit(solution)/shard_map/all_to_all | solution.py:472
  106.6 10.1 %all_to_all.50.got_mine = f32[16,24,128]{2,1,0:T(8,128)S(1)} all-to-all(f32[16,24,128]{2,1,0:T(8,128)S(1)} %broadcast_in_dim.15), channel_id=1, replica_groups=mesh['y'=4,'x'=4,'core'=2,'z'=8] {'y','x'}, dimensions={0} | all-to-all | bytes 393216 | tf_op jit(solution)/shard_map/all_to_all | solution.py:472
  116.7 4.3 %collective-permute-start.7 = (f32[16,24,128]{2,1,0:T(8,128)S(1)}, f32[16,24,128]{2,1,0:T(8,128)S(1)}, u32[]{:S(2)}, u32[]{:S(2)}) collective-permute-start(f32[16,24,128]{2,1,0:T(8,128)S(1)} %all_to_all.50.got_mine), channel_id=1, source_target_pairs={{0,8},{8,0},{1,9},{9,1},{2,10},{10,2},{3,11},{11,3},{4,12},{12,4},... | collective-permute-start | bytes 589832 | tf_op jit(solution)/shard_map/ppermute | solution.py:482
  121.0 2.1 collective-permute-start.8
  123.1 2.2 %collective-permute-start.9 = (f32[64,128]{1,0:T(8,128)S(1)}, f32[64,128]{1,0:T(8,128)S(1)}, u32[]{:S(2)}, u32[]{:S(2)}) collective-permute-start(f32[64,128]{1,0:T(8,128)S(1)} %get-tuple-element.36), channel_id=1, source_target_pairs={{8,0},{16,8},{24,16},{32,24},{40,32},{48,40},{56,48},{64,56},{72,6... | collective-permute-start | bytes 98312 | tf_op jit(solution)/shard_map/ppermute | solution.py:490
  125.4 2.2 %collective-permute-start.10 = (f32[64,128]{1,0:T(8,128)S(1)}, f32[64,128]{1,0:T(8,128)S(1)}, u32[]{:S(2)}, u32[]{:S(2)}) collective-permute-start(f32[64,128]{1,0:T(8,128)S(1)} %get-tuple-element.37), channel_id=1, source_target_pairs={{0,1},{1,2},{2,3},{3,4},{4,5},{5,6},{6,7},{8,9},{9,10},{10,11},{11... | collective-permute-start | bytes 98312 | tf_op jit(solution)/shard_map/ppermute | solution.py:486
  127.6 1.5 collective-permute-start.11
  129.1 3.7 %collective-permute-done.11.east = f32[64,128]{1,0:T(8,128)S(1)} collective-permute-done((f32[64,128]{1,0:T(8,128)S(1)}, f32[64,128]{1,0:T(8,128)S(1)}, u32[]{:S(2)}, u32[]{:S(2)}) %collective-permute-start.11) | collective-permute-done | bytes 32800 | tf_op jit(solution)/shard_map/ppermute | solution.py:490
  132.8 3.4 %copy-done.2 = bf16[4,2,256,2048]{3,2,1,0:T(8,128)(2,1)S(1)} copy-done((bf16[4,2,256,2048]{3,2,1,0:T(8,128)(2,1)S(1)}, bf16[4,2,256,2048]{3,2,1,0:T(8,128)(2,1)}, u32[]{:S(2)}) %copy-start.2) | copy-done | bytes 8388632
  136.1 8.1 %factor_and_expand.1 = (f32[64,2048]{1,0:T(8,128)S(1)}, f32[128,128]{1,0:T(8,128)S(1)}, f32[128,128]{1,0:T(8,128)S(1)}) custom-call(f32[16,24,128]{2,1,0:T(8,128)S(1)} %all_to_all.50.got_mine, f32[16,24,128]{2,1,0:T(8,128)S(1)} %collective-permute-done.7.got_other, bf16[4,2,256,2048]{3,2,1,0:T(8,128)(2,1)S(1)} %copy-done.2, ...), custom_call_target="tpu_custom_call" | custom-call | tf_op jit(solution)/shard_map/factor_and_expand/pallas_call | solution.py:352
  144.3 4.2 %collective-permute-start.12 = (f32[128,128]{1,0:T(8,128)S(1)}, f32[128,128]{1,0:T(8,128)S(1)}, u32[]{:S(2)}, u32[]{:S(2)}) collective-permute-start(f32[128,128]{1,0:T(8,128)S(1)} %get-tuple-element.40), channel_id=1, source_target_pairs={{0,8},{8,16},{16,24},{24,32},{32,40},{40,48},{48,56},{56,64},{64,7... | collective-permute-start | bytes 196616 | tf_op jit(solution)/shard_map/ppermute | solution.py:486
  148.5 2.1 collective-permute-start.13
  150.6 6.2 %project.1.base = f32[2,16,24,128]{3,2,1,0:T(8,128)S(1)} custom-call(bf16[4,2,256,2048]{3,2,1,0:T(8,128)(2,1)S(1)} %copy-done.3, f32[64,2048]{1,0:T(8,128)S(1)} %get-tuple-element.39.field), custom_call_target="tpu_custom_call" | custom-call | tf_op jit(solution)/shard_map/project/pallas_call | solution.py:381
  159.2 14.5 %all_to_all.51 = f32[16,24,128]{2,1,0:T(8,128)S(1)} all-to-all(f32[16,24,128]{2,1,0:T(8,128)S(1)} %add.11), channel_id=1, replica_groups=mesh['y'=4,'x'=4,'core'=2,'z'=8] {'y','x'}, dimensions={0} | all-to-all | bytes 393216 | tf_op jit(solution)/shard_map/all_to_all | solution.py:479
  173.8 10.9 %all_to_all.52 = f32[8,24,128]{2,1,0:T(8,128)S(1)} all-to-all(f32[8,24,128]{2,1,0:T(8,128)S(1)} %broadcast_in_dim.16), channel_id=1, replica_groups=mesh['y'=4,'x'=4,'core'=2,'z'=8] {'z'}, dimensions={0} | all-to-all | bytes 196608 | tf_op jit(solution)/shard_map/all_to_all | solution.py:472
  184.7 9.8 %all_to_all.53.got_mine = f32[16,24,128]{2,1,0:T(8,128)S(1)} all-to-all(f32[16,24,128]{2,1,0:T(8,128)S(1)} %broadcast_in_dim.17), channel_id=1, replica_groups=mesh['y'=4,'x'=4,'core'=2,'z'=8] {'y','x'}, dimensions={0} | all-to-all | bytes 393216 | tf_op jit(solution)/shard_map/all_to_all | solution.py:472
  194.5 4.2 %collective-permute-start.15 = (f32[16,24,128]{2,1,0:T(8,128)S(1)}, f32[16,24,128]{2,1,0:T(8,128)S(1)}, u32[]{:S(2)}, u32[]{:S(2)}) collective-permute-start(f32[16,24,128]{2,1,0:T(8,128)S(1)} %all_to_all.53.got_mine), channel_id=1, source_target_pairs={{0,8},{8,0},{1,9},{9,1},{2,10},{10,2},{3,11},{11,3},{4,12},{12,4},... | collective-permute-start | bytes 589832 | tf_op jit(solution)/shard_map/ppermute | solution.py:482
  199.8 7.2 %factor_and_finish.1 = (f32[1024,128]{1,0:T(8,128)}, f32[64,64]{1,0:T(8,128)}) custom-call(f32[16,24,128]{2,1,0:T(8,128)S(1)} %all_to_all.53.got_mine, f32[16,24,128]{2,1,0:T(8,128)S(1)} %collective-permute-done.15.got_other, f32[64,2048]{1,0:T(8,128)S(1)} %get-tuple-element.39.field), custom_call_target="tpu_custom_call" | custom-call | tf_op jit(solution)/shard_map/factor_and_finish/pallas_call | solution.py:456
  (46 shorter events, 9.5 us)
Async XLA Ops:
  0.6 1.0 copy-start.4
  1.7 0.7 copy-start.5
  2.4 71.2 %copy-start.6 = (s32[16,128]{1,0:T(8,128)S(1)}, s32[16,128]{1,0:T(8,128)}, u32[]{:S(2)}) copy-start(s32[16,128]{1,0:T(8,128)} %sea.5) | copy-start | bytes 24580
  2.4 71.2 %copy-start.7 = (f32[16,128]{1,0:T(8,128)S(1)}, f32[16,128]{1,0:T(8,128)}, u32[]{:S(2)}) copy-start(f32[16,128]{1,0:T(8,128)} %pen.5) | copy-start | bytes 24580
  12.1 3.2 %copy-start = (bf16[4,2,256,2048]{3,2,1,0:T(8,128)(2,1)}, bf16[4,2,256,2048]{3,2,1,0:T(8,128)(2,1)S(1)}, u32[]{:S(2)}) copy-start(bf16[4,2,256,2048]{3,2,1,0:T(8,128)(2,1)S(1)} %get-tuple-element.26.snap) | copy-start | bytes 25165828
  15.3 4.3 %collective-permute-start = (f32[16,24,128]{2,1,0:T(8,128)S(1)}, f32[16,24,128]{2,1,0:T(8,128)S(1)}, u32[]{:S(2)}, u32[]{:S(2)}) collective-permute-start(f32[16,24,128]{2,1,0:T(8,128)S(1)} %get-tuple-element.25), channel_id=1, source_target_pairs={{0,8},{8,0},{1,9},{9,1},{2,10},{10,2},{3,11},{11,3},{4,12},{12,4},... | collective-permute-start | bytes 589832 | tf_op jit(solution)/shard_map/ppermute | solution.py:478
  57.6 16.0 %collective-permute-start.1 = (f32[16,24,128]{2,1,0:T(8,128)S(1)}, f32[16,24,128]{2,1,0:T(8,128)S(1)}, u32[]{:S(2)}, u32[]{:S(2)}) collective-permute-start(f32[16,24,128]{2,1,0:T(8,128)S(1)} %all_to_all.47.got_mine), channel_id=1, source_target_pairs={{0,8},{8,0},{1,9},{9,1},{2,10},{10,2},{3,11},{11,3},{4,12},{12,4},... | collective-permute-start | bytes 589832 | tf_op jit(solution)/shard_map/ppermute | solution.py:482
  61.9 7.8 %collective-permute-start.2 = (f32[64,128]{1,0:T(8,128)S(1)}, f32[64,128]{1,0:T(8,128)S(1)}, u32[]{:S(2)}, u32[]{:S(2)}) collective-permute-start(f32[64,128]{1,0:T(8,128)S(1)} %get-tuple-element.28), channel_id=1, source_target_pairs={{0,8},{8,16},{16,24},{24,32},{32,40},{40,48},{48,56},{56,64},{64,7... | collective-permute-start | bytes 98312 | tf_op jit(solution)/shard_map/ppermute | solution.py:486
  64.0 5.8 %collective-permute-start.3 = (f32[64,128]{1,0:T(8,128)S(1)}, f32[64,128]{1,0:T(8,128)S(1)}, u32[]{:S(2)}, u32[]{:S(2)}) collective-permute-start(f32[64,128]{1,0:T(8,128)S(1)} %get-tuple-element.29), channel_id=1, source_target_pairs={{8,0},{16,8},{24,16},{32,24},{40,32},{48,40},{56,48},{64,56},{72,6... | collective-permute-start | bytes 98312 | tf_op jit(solution)/shard_map/ppermute | solution.py:490
  66.2 3.5 %collective-permute-start.4 = (f32[64,128]{1,0:T(8,128)S(1)}, f32[64,128]{1,0:T(8,128)S(1)}, u32[]{:S(2)}, u32[]{:S(2)}) collective-permute-start(f32[64,128]{1,0:T(8,128)S(1)} %get-tuple-element.30), channel_id=1, source_target_pairs={{0,1},{1,2},{2,3},{3,4},{4,5},{5,6},{6,7},{8,9},{9,10},{10,11},{11... | collective-permute-start | bytes 98312 | tf_op jit(solution)/shard_map/ppermute | solution.py:486
  68.4 5.2 %collective-permute-start.5 = (f32[64,128]{1,0:T(8,128)S(1)}, f32[64,128]{1,0:T(8,128)S(1)}, u32[]{:S(2)}, u32[]{:S(2)}) collective-permute-start(f32[64,128]{1,0:T(8,128)S(1)} %get-tuple-element.31), channel_id=1, source_target_pairs={{1,0},{2,1},{3,2},{4,3},{5,4},{6,5},{7,6},{9,8},{10,9},{11,10},{12... | collective-permute-start | bytes 98312 | tf_op jit(solution)/shard_map/ppermute | solution.py:490
  73.6 3.4 %copy-start.1 = (bf16[4,2,256,2048]{3,2,1,0:T(8,128)(2,1)S(1)}, bf16[4,2,256,2048]{3,2,1,0:T(8,128)(2,1)}, u32[]{:S(2)}) copy-start(bf16[4,2,256,2048]{3,2,1,0:T(8,128)(2,1)} %copy-done) | copy-start | bytes 25165828
  82.0 1.7 collective-permute-start.6
  116.7 16.0 %collective-permute-start.7 = (f32[16,24,128]{2,1,0:T(8,128)S(1)}, f32[16,24,128]{2,1,0:T(8,128)S(1)}, u32[]{:S(2)}, u32[]{:S(2)}) collective-permute-start(f32[16,24,128]{2,1,0:T(8,128)S(1)} %all_to_all.50.got_mine), channel_id=1, source_target_pairs={{0,8},{8,0},{1,9},{9,1},{2,10},{10,2},{3,11},{11,3},{4,12},{12,4},... | collective-permute-start | bytes 589832 | tf_op jit(solution)/shard_map/ppermute | solution.py:482
  121.0 8.0 %collective-permute-start.8 = (f32[64,128]{1,0:T(8,128)S(1)}, f32[64,128]{1,0:T(8,128)S(1)}, u32[]{:S(2)}, u32[]{:S(2)}) collective-permute-start(f32[64,128]{1,0:T(8,128)S(1)} %get-tuple-element.35), channel_id=1, source_target_pairs={{0,8},{8,16},{16,24},{24,32},{32,40},{40,48},{48,56},{56,64},{64,7... | collective-permute-start | bytes 98312 | tf_op jit(solution)/shard_map/ppermute | solution.py:486
  123.1 5.9 %collective-permute-start.9 = (f32[64,128]{1,0:T(8,128)S(1)}, f32[64,128]{1,0:T(8,128)S(1)}, u32[]{:S(2)}, u32[]{:S(2)}) collective-permute-start(f32[64,128]{1,0:T(8,128)S(1)} %get-tuple-element.36), channel_id=1, source_target_pairs={{8,0},{16,8},{24,16},{32,24},{40,32},{48,40},{56,48},{64,56},{72,6... | collective-permute-start | bytes 98312 | tf_op jit(solution)/shard_map/ppermute | solution.py:490
  125.4 3.7 %collective-permute-start.10 = (f32[64,128]{1,0:T(8,128)S(1)}, f32[64,128]{1,0:T(8,128)S(1)}, u32[]{:S(2)}, u32[]{:S(2)}) collective-permute-start(f32[64,128]{1,0:T(8,128)S(1)} %get-tuple-element.37), channel_id=1, source_target_pairs={{0,1},{1,2},{2,3},{3,4},{4,5},{5,6},{6,7},{8,9},{9,10},{10,11},{11... | collective-permute-start | bytes 98312 | tf_op jit(solution)/shard_map/ppermute | solution.py:486
  127.6 5.2 %collective-permute-start.11 = (f32[64,128]{1,0:T(8,128)S(1)}, f32[64,128]{1,0:T(8,128)S(1)}, u32[]{:S(2)}, u32[]{:S(2)}) collective-permute-start(f32[64,128]{1,0:T(8,128)S(1)} %get-tuple-element.38), channel_id=1, source_target_pairs={{1,0},{2,1},{3,2},{4,3},{5,4},{6,5},{7,6},{9,8},{10,9},{11,10},{12... | collective-permute-start | bytes 98312 | tf_op jit(solution)/shard_map/ppermute | solution.py:490
  132.8 3.4 %copy-start.2 = (bf16[4,2,256,2048]{3,2,1,0:T(8,128)(2,1)S(1)}, bf16[4,2,256,2048]{3,2,1,0:T(8,128)(2,1)}, u32[]{:S(2)}) copy-start(bf16[4,2,256,2048]{3,2,1,0:T(8,128)(2,1)} %copy-done) | copy-start | bytes 25165828
  136.1 14.4 %copy-start.3 = (bf16[4,2,256,2048]{3,2,1,0:T(8,128)(2,1)S(1)}, bf16[4,2,256,2048]{3,2,1,0:T(8,128)(2,1)}, u32[]{:S(2)}) copy-start(bf16[4,2,256,2048]{3,2,1,0:T(8,128)(2,1)} %copy-done) | copy-start | bytes 25165828
  144.3 12.5 %collective-permute-start.12 = (f32[128,128]{1,0:T(8,128)S(1)}, f32[128,128]{1,0:T(8,128)S(1)}, u32[]{:S(2)}, u32[]{:S(2)}) collective-permute-start(f32[128,128]{1,0:T(8,128)S(1)} %get-tuple-element.40), channel_id=1, source_target_pairs={{0,8},{8,16},{16,24},{24,32},{32,40},{40,48},{48,56},{56,64},{64,7... | collective-permute-start | bytes 196616 | tf_op jit(solution)/shard_map/ppermute | solution.py:486
  148.5 8.3 %collective-permute-start.13 = (f32[128,128]{1,0:T(8,128)S(1)}, f32[128,128]{1,0:T(8,128)S(1)}, u32[]{:S(2)}, u32[]{:S(2)}) collective-permute-start(f32[128,128]{1,0:T(8,128)S(1)} %get-tuple-element.41), channel_id=1, source_target_pairs={{0,1},{1,2},{2,3},{3,4},{4,5},{5,6},{6,7},{8,9},{9,10},{10,11},{11... | collective-permute-start | bytes 196616 | tf_op jit(solution)/shard_map/ppermute | solution.py:486
  157.7 1.5 collective-permute-start.14
  194.5 5.3 %collective-permute-start.15 = (f32[16,24,128]{2,1,0:T(8,128)S(1)}, f32[16,24,128]{2,1,0:T(8,128)S(1)}, u32[]{:S(2)}, u32[]{:S(2)}) collective-permute-start(f32[16,24,128]{2,1,0:T(8,128)S(1)} %all_to_all.53.got_mine), channel_id=1, source_target_pairs={{0,8},{8,0},{1,9},{9,1},{2,10},{10,2},{3,11},{11,3},{4,12},{12,4},... | collective-permute-start | bytes 589832 | tf_op jit(solution)/shard_map/ppermute | solution.py:482
where the time goes:
time: 208 us; the launch traced here: 207 us
  blocking collectives  106 us (51%)
  starting transfers between devices  38.9 us (19%)
  Pallas kernels  37.1 us (18%)
  waiting for transfers between devices  12.2 us (6%)
  local copies, waits for them, and re-layouts  11.8 us (6%)
    all_to_all x6, blocking collectives, to_each(): lax.all_to_all(jnp.broadcast_to(value[None], (count, *value.shape)), axis...  66.7 us
    all_to_all x3, blocking collectives, summed_everywhere(): share = lax.all_to_all(pair, CHIPS, 0, 0, tiled=True).sum(axis=0)  39.3 us
    ppermute x6, starting transfers between devices, from_below(): return lax.ppermute(value, axis, [(i, i + 1) for i in range(count - 1)])  14.8 us
    ppermute x3, starting transfers between devices, summed_everywhere(): return (half, lax.ppermute(half, 'core', SWAP))  12.9 us
    unnamed x16, local copies, waits for them, and re-layouts  11.7 us
    pallas_call x1, Pallas kernels, begin(): pl.pallas_call(begin_kernel, grid=(NSNAP // depth,), in_specs=[pl.BlockSp...  9.73 us
    pallas_call x1, Pallas kernels, second_step(): pl.pallas_call(second_kernel, in_specs=[VM, VM, HB, *[VM] * 7], out_specs...  8.11 us
    ppermute x4, waiting for transfers between devices, from_above(): return lax.ppermute(value, axis, [(i + 1, i) for i in range(count - 1)])  7.52 us
  transfers between devices with their start and end apart: 16, of which 6 were waited for; matrix products, arithmetic and copies ran while one was open for 0% of the time, Pallas kernels for 3%

commit v1 on v0

--- a/solution.py
+++ b/solution.py
@@ -14,13 +14,15 @@
 BLOCK = 256
 NBLOCK = NSNAP // BLOCK
 SHARD = 24
+DEPTH = 16
 F32 = jnp.float32
 BF16 = jnp.bfloat16
 HIGHEST = lax.Precision.HIGHEST
 CHIPS = ("y", "x")
 LAT = ("y", "x", "core")
 SWAP = [(0, 1), (1, 0)]
-VMEM_LIMIT = 40 * 1024 * 1024
+VMEM_LIMIT = 50 * 1024 * 1024
+SMALL_LIMIT = 20 * 1024 * 1024
 
 
 def parts(value):
@@ -183,17 +185,16 @@
         bottom[...] = flat[:, cols(ROWS - 1)]
         first[...], last[...] = edge_columns(flat)
 
-    depth = BLOCK // 2
-    for a in range(ROWS):
-        high, low = parts(snap[pl.ds(a, depth, stride=ROWS), :])
+    for a in range(ROWS):
+        high, low = parts(snap[pl.ds(a, BLOCK, stride=ROWS), :])
         split_out[0, 0, :, cols(a)] = high
         split_out[0, 1, :, cols(a)] = low
-    both = dot_nt(split_out[0, 0], split[...]) + dot_nt(split_out[0, 1], split[...])
-    summed = (both + pltpu.roll(both, K, 1)).reshape(8, 16, LANES)
-    half = (step // 2) % 2
-    at = pl.ds((step % 2) * 8, 8)
-    keep = (lane_of(summed.shape) < K) & (step >= 4)
-    pay[half, at, 0:16, :] = jnp.where(keep, pay[half, at, 0:16, :], summed)
+    both = dot_nt(split_out[0].reshape(2 * BLOCK, PTS), split[...])
+    both = both[0:BLOCK] + both[BLOCK : 2 * BLOCK]
+    summed = (both + pltpu.roll(both, K, 1)).reshape(16, 16, LANES)
+    half = step % 2
+    keep = (lane_of(summed.shape) < K) & (step >= 2)
+    pay[half, :, 0:16, :] = jnp.where(keep, pay[half, :, 0:16, :], summed)
 
     @pl.when(step == pl.num_programs(0) - 1)
     def _():
@@ -205,22 +206,21 @@
 
 
 def begin(snapshots, basis, sea):
-    depth = BLOCK // 2
     halo = jax.ShapeDtypeStruct((K, LANES), F32)
-    share = jax.ShapeDtypeStruct((16, SHARD, LANES), F32)
+    share = jax.ShapeDtypeStruct((16, DEPTH, LANES), F32)
     return pl.pallas_call(
         begin_kernel,
-        grid=(NSNAP // depth,),
+        grid=(NBLOCK,),
         in_specs=[
-            pl.BlockSpec((depth * ROWS, LANES), lambda i: (i, 0)),
+            pl.BlockSpec((BLOCK * ROWS, LANES), lambda i: (i, 0)),
             whole((K * ROWS, LANES)),
             whole((ROWS, LANES)),
         ],
         out_specs=[
-            pl.BlockSpec((1, 2, depth, PTS), lambda i: (i // 2, 0, i % 2, 0)),
+            pl.BlockSpec((1, 2, BLOCK, PTS), lambda i: (i, 0, 0, 0)),
             whole((K, PTS)),
             *[whole((K, LANES))] * 4,
-            *[whole((16, SHARD, LANES))] * 2,
+            *[whole((16, DEPTH, LANES))] * 2,
         ],
         out_shape=[
             jax.ShapeDtypeStruct((NBLOCK, 2, BLOCK, PTS), BF16),
@@ -234,7 +234,7 @@
         ],
         scratch_shapes=[
             pltpu.VMEM((2 * K, PTS), BF16),
-            pltpu.VMEM((2, 16, SHARD, LANES), F32),
+            pltpu.VMEM((2, 16, DEPTH, LANES), F32),
         ],
         compiler_params=pltpu.CompilerParams(vmem_limit_bytes=VMEM_LIMIT),
         name="split_and_project",
@@ -243,6 +243,11 @@
 
 def copy_of(snap, held, sems, block):
     return pltpu.make_async_copy(snap.at[block], held.at[block], sems.at[block])
+
+
+def begin_copies(snap, held, sems):
+    for block in range(NBLOCK):
+        copy_of(snap, held, sems, block).start()
 
 
 def expand(spread, snap, held, sems, total):
@@ -258,10 +263,12 @@
             total[:, at] = piece if block == 0 else total[:, at] + piece
 
 
-def project(held, split, pay):
+def project(held, split, pay, arrive=None):
     for block in range(NBLOCK):
-        both = dot_nt(held[block, 0], split[...]) + dot_nt(held[block, 1], split[...])
-        put_coefficients(pay, block, both)
+        if arrive is not None:
+            arrive(block)
+        both = dot_nt(held[block].reshape(2 * BLOCK, PTS), split[...])
+        put_coefficients(pay, block, both[0:BLOCK] + both[BLOCK : 2 * BLOCK])
 
 
 def applied_field(total, prev, sides, sea, pen, out):
@@ -277,8 +284,7 @@
     field, top, bottom, first, last, mine, other,
     full, held, spread, total, split, pay, sems,
 ):
-    for block in range(NBLOCK):
-        copy_of(snap, held, sems, block).start()
+    begin_copies(snap, held, sems)
     take_in(got_mine, got_other, full)
     coefficients_of(full, spread)
     expand(spread, snap, held, sems, total)
@@ -294,9 +300,9 @@
     hand_out(pay, mine, other)
 
 
-def scratch_for_expand():
+def scratch_for_expand(depth):
     return [
-        pltpu.VMEM((2, 16, SHARD, LANES), F32),
+        pltpu.VMEM((2, 16, depth, LANES), F32),
         pltpu.VMEM((NBLOCK, 2, BLOCK, PTS), BF16),
         pltpu.VMEM((NBLOCK, 2 * K, BLOCK), BF16),
         pltpu.VMEM((K, PTS), F32),
@@ -316,7 +322,7 @@
         out_specs=[VM] * 7,
         out_shape=[jax.ShapeDtypeStruct((K, PTS), F32), halo, halo, halo, halo, share, share],
         scratch_shapes=[
-            *scratch_for_expand(),
+            *scratch_for_expand(DEPTH),
             pltpu.VMEM((2 * K, PTS), BF16),
             pltpu.VMEM((2, 16, SHARD, LANES), F32),
             pltpu.SemaphoreType.DMA((NBLOCK,)),
@@ -331,8 +337,7 @@
     field, bottom, last,
     full, held, spread, total, raw, sems,
 ):
-    for block in range(NBLOCK):
-        copy_of(snap, held, sems, block).start()
+    begin_copies(snap, held, sems)
     take_in(got_mine, got_other, full)
     coefficients_of(full, spread)
     inverse = inverse_factor(square_of(full, 16))
@@ -355,7 +360,7 @@
         out_specs=[VM] * 3,
         out_shape=[jax.ShapeDtypeStruct((K, PTS), F32), halo, halo],
         scratch_shapes=[
-            *scratch_for_expand(),
+            *scratch_for_expand(SHARD),
             pltpu.VMEM((K, PTS), F32),
             pltpu.SemaphoreType.DMA((NBLOCK,)),
         ],
@@ -365,16 +370,12 @@
 
 
 def project_kernel(snap, field, pay, held, split, sems):
-    for block in range(NBLOCK):
-        copy_of(snap, held, sems, block).start()
+    begin_copies(snap, held, sems)
     for a in range(ROWS):
         store_split(split, a, field[:, cols(a)])
     pay[...] = jnp.zeros_like(pay)
     put_square(pay, 16, folded(dot_nt(split[...], split[...])))
-    for block in range(NBLOCK):
-        copy_of(snap, held, sems, block).wait()
-        both = dot_nt(held[block, 0], split[...]) + dot_nt(held[block, 1], split[...])
-        put_coefficients(pay, block, both)
+    project(held, split, pay, lambda block: copy_of(snap, held, sems, block).wait())
 
 
 def project_step(snap, field):
@@ -433,7 +434,7 @@
             pltpu.VMEM((2 * K, PTS + 4 * LANES), BF16),
             pltpu.VMEM((2, 16, SHARD, LANES), F32),
         ],
-        compiler_params=pltpu.CompilerParams(vmem_limit_bytes=VMEM_LIMIT),
+        compiler_params=pltpu.CompilerParams(vmem_limit_bytes=SMALL_LIMIT),
         name="roughness_products",
     )(field, north, west, pen, base)
 
@@ -462,24 +463,32 @@
             jax.ShapeDtypeStruct((K, K), F32),
         ],
         scratch_shapes=[pltpu.VMEM((2, 16, SHARD, LANES), F32)],
-        compiler_params=pltpu.CompilerParams(vmem_limit_bytes=VMEM_LIMIT),
+        compiler_params=pltpu.CompilerParams(vmem_limit_bytes=SMALL_LIMIT),
         name="factor_and_finish",
     )(*got, field)
     return basis.reshape(K, ROWS, LANES), matrix
 
 
-def to_each(value, axis, count):
-    return lax.all_to_all(
-        jnp.broadcast_to(value[None], (count, *value.shape)), axis, 0, 0, tiled=True
-    )
-
-
-def summed_everywhere(mine, other):
+def exchange(value, axis):
+    return lax.all_to_all(value, axis, 0, 0, tiled=True)
+
+
+def copies(value, count):
+    return jnp.broadcast_to(value[None], (count, *value.shape))
+
+
+def summed_everywhere(mine, other, edges=None):
+    sides = None
     pair = mine + lax.ppermute(other, "core", SWAP)
-    share = lax.all_to_all(pair, CHIPS, 0, 0, tiled=True).sum(axis=0)
-    share = to_each(share, "z", 8).sum(axis=0)
-    half = to_each(share, CHIPS, 16)
-    return half, lax.ppermute(half, "core", SWAP)
+    if edges is not None:
+        pair, edges = lax.optimization_barrier((pair, edges))
+        sides = sides_of(*edges)
+    shares = exchange(pair, CHIPS)
+    if edges is not None:
+        shares, sides = lax.optimization_barrier((shares, sides))
+    shares = exchange(copies(shares.sum(axis=0), 8), "z")
+    half = exchange(copies(shares.sum(axis=0), 16), CHIPS)
+    return (half, lax.ppermute(half, "core", SWAP)), sides
 
 
 def from_below(value, axis, count):
@@ -501,17 +510,15 @@
 
 def local(snapshots, land_sea, penalty, initial_basis):
     snap, start, *edges, mine, other = begin(snapshots, initial_basis, land_sea)
-    sides = sides_of(*edges)
-    got = summed_everywhere(mine, other)
+    got, sides = summed_everywhere(mine, other, edges)
     applied, *edges, mine, other = first_step(got, snap, start, sides, land_sea, penalty)
-    sides = sides_of(*edges)
-    got = summed_everywhere(mine, other)
+    got, sides = summed_everywhere(mine, other, edges)
     applied, bottom, last = second_step(got, snap, applied, sides, land_sea, penalty)
     north = from_below(bottom, LAT, 32)
     west = from_below(last, "z", 8)
     base = project_step(snap, applied)
     mine, other = rough_step(applied, north, west, penalty, base)
-    got = summed_everywhere(mine, other)
+    got, _ = summed_everywhere(mine, other)
     return last_step(got, applied)
 
 

time: 208 us -> 194 us (0.933)
  blocking collectives: 106 us -> 83.4 us
  starting transfers between devices: 38.9 us -> 51.4 us
  local copies, waits for them, and re-layouts: 11.8 us -> 1.8 us
  Pallas kernels: 37.1 us -> 41.2 us
    all_to_all x9 -> x7, blocking collectives: 106 us -> 83.4 us  [exchange(): return lax.all_to_all(value, axis, 0, 0, tiled=True)]
    unnamed x16 -> x8, local copies, waits for them, and re-layouts: 11.7 us -> 1.74 us
    all_to_all x0 -> x2, starting transfers between devices: none -> 8.54 us  [exchange(): return lax.all_to_all(value, axis, 0, 0, tiled=True)]
    ppermute x6, starting transfers between devices: 14.8 us -> 18.1 us  [from_below(): return lax.ppermute(value, axis, [(i, i + 1) for i in range(count - 1)])]
  transfers between devices with their start and end apart: 16 -> 18, of which waited for: 6 -> 8; matrix products, arithmetic and copies ran while one was open for 0% -> 0% of each run, Pallas kernels for 3% -> 3%
where the time goes in v1:
time: 194 us; the launch traced here: 193 us
  blocking collectives  83.4 us (43%)
  starting transfers between devices  51.4 us (26%)
  Pallas kernels  41.2 us (21%)
  waiting for transfers between devices  13.3 us (7%)
    all_to_all x7, blocking collectives, exchange(): return lax.all_to_all(value, axis, 0, 0, tiled=True)  83.4 us
    ppermute x6, starting transfers between devices, from_below(): return lax.ppermute(value, axis, [(i, i + 1) for i in range(count - 1)])  18.1 us
    ppermute x3, starting transfers between devices, summed_everywhere(): return ((half, lax.ppermute(half, 'core', SWAP)), sides)  14.3 us
    pallas_call x1, Pallas kernels, begin(): pl.pallas_call(begin_kernel, grid=(NBLOCK,), in_specs=[pl.BlockSpec((BLOC...  9.98 us
    pallas_call x1, Pallas kernels, second_step(): pl.pallas_call(second_kernel, in_specs=[VM, VM, HB, *[VM] * 7], out_specs...  9.71 us
    all_to_all x2, starting transfers between devices, exchange(): return lax.all_to_all(value, axis, 0, 0, tiled=True)  8.54 us
    pallas_call x1, Pallas kernels, last_step(): pl.pallas_call(last_kernel, in_specs=[VM] * 3, out_specs=[VM] * 2, out_sh...  7.25 us
    ppermute x4, waiting for transfers between devices, from_above(): return lax.ppermute(value, axis, [(i + 1, i) for i in range(count - 1)])  6.84 us
  transfers between devices with their start and end apart: 18, of which 8 were waited for; matrix products, arithmetic and copies ran while one was open for 0% of the time, Pallas kernels for 3%

profile of v1, /device:TPU:1, one launch (start us, length us, event | category | flops | bytes accessed | tf_op | source)
XLA Modules:
  0.0 193.5 jit_solution(18335798655931201583)
XLA Ops:
  2.4 10.0 %split_and_project.1 = (bf16[4,2,256,2048]{3,2,1,0:T(8,128)(2,1)}, f32[64,2048]{1,0:T(8,128)S(1)}, f32[64,128]{1,0:T(8,128)S(1)}, f32[64,128]{1,0:T(8,128)S(1)},...) custom-call(f32[16384,128]{1,0:T(8,128)} %bitcast.4, ...), custom_call_target="tpu_custom_call" | custom-call | tf_op jit(solution)/shard_map/split_and_project/pallas_call | solution.py:211
  12.4 3.2 %collective-permute-start = (f32[16,16,128]{2,1,0:T(8,128)S(1)}, f32[16,16,128]{2,1,0:T(8,128)S(1)}, u32[]{:S(2)}, u32[]{:S(2)}) collective-permute-start(f32[16,16,128]{2,1,0:T(8,128)S(1)} %get-tuple-element.45), channel_id=1, source_target_pairs={{0,8},{8,0},{1,9},{9,1},{2,10},{10,2},{3,11},{11,3},{4,12},{12,4},... | collective-permute-start | bytes 393224 | tf_op jit(solution)/shard_map/ppermute | solution.py:482
  17.3 5.0 %all-to-all-start = ((f32[16,16,128]{2,1,0:T(8,128)}), f32[16,16,128]{2,1,0:T(8,128)S(1)}, u32[]{:S(2)}, u32[]{:S(2)}) async-start(f32[16,16,128]{2,1,0:T(8,128)} %add.9), calls=%async_computation | async-start | bytes 262144 | tf_op jit(solution)/shard_map/all_to_all | solution.py:473
  22.3 4.1 %collective-permute-start.1 = (f32[64,128]{1,0:T(8,128)S(1)}, f32[64,128]{1,0:T(8,128)S(1)}, u32[]{:S(2)}, u32[]{:S(2)}) collective-permute-start(f32[64,128]{1,0:T(8,128)S(1)} %get-tuple-element.51), channel_id=1, source_target_pairs={{0,8},{8,16},{16,24},{24,32},{32,40},{40,48},{48,56},{56,64},{64,7... | collective-permute-start | bytes 98312 | tf_op jit(solution)/shard_map/ppermute | solution.py:495
  26.4 1.9 collective-permute-start.2
  28.3 3.5 %collective-permute-start.3 = (f32[64,128]{1,0:T(8,128)S(1)}, f32[64,128]{1,0:T(8,128)S(1)}, u32[]{:S(2)}, u32[]{:S(2)}) collective-permute-start(f32[64,128]{1,0:T(8,128)S(1)} %get-tuple-element.53), channel_id=1, source_target_pairs={{0,1},{1,2},{2,3},{3,4},{4,5},{5,6},{6,7},{8,9},{9,10},{10,11},{11... | collective-permute-start | bytes 98312 | tf_op jit(solution)/shard_map/ppermute | solution.py:495
  31.8 1.3 collective-permute-start.4
  33.2 3.5 %collective-permute-done.4.east = f32[64,128]{1,0:T(8,128)S(1)} collective-permute-done((f32[64,128]{1,0:T(8,128)S(1)}, f32[64,128]{1,0:T(8,128)S(1)}, u32[]{:S(2)}, u32[]{:S(2)}) %collective-permute-start.4) | collective-permute-done | bytes 32800 | tf_op jit(solution)/shard_map/ppermute | solution.py:499
  36.7 15.7 %all_to_all.45 = f32[8,16,128]{2,1,0:T(8,128)S(1)} all-to-all(f32[8,16,128]{2,1,0:T(8,128)S(1)} %broadcast_in_dim.12), channel_id=1, replica_groups=mesh['y'=4,'x'=4,'core'=2,'z'=8] {'z'}, dimensions={0} | all-to-all | bytes 131072 | tf_op jit(solution)/shard_map/all_to_all | solution.py:473
  52.4 12.1 %all_to_all.46.got_mine = f32[16,16,128]{2,1,0:T(8,128)S(1)} all-to-all(f32[16,16,128]{2,1,0:T(8,128)S(1)} %broadcast_in_dim.13), channel_id=1, replica_groups=mesh['y'=4,'x'=4,'core'=2,'z'=8] {'y','x'}, dimensions={0} | all-to-all | bytes 262144 | tf_op jit(solution)/shard_map/all_to_all | solution.py:473
  64.5 5.2 %collective-permute-start.5 = (f32[16,16,128]{2,1,0:T(8,128)S(1)}, f32[16,16,128]{2,1,0:T(8,128)S(1)}, u32[]{:S(2)}, u32[]{:S(2)}) collective-permute-start(f32[16,16,128]{2,1,0:T(8,128)S(1)} %all_to_all.46.got_mine), channel_id=1, source_target_pairs={{0,8},{8,0},{1,9},{9,1},{2,10},{10,2},{3,11},{11,3},{4,12},{12,4},... | collective-permute-start | bytes 393224 | tf_op jit(solution)/shard_map/ppermute | solution.py:491
  70.7 6.7 %expand_and_project.1 = (f32[64,2048]{1,0:T(8,128)S(1)}, f32[64,128]{1,0:T(8,128)S(1)}, f32[64,128]{1,0:T(8,128)S(1)}, f32[64,128]{1,0:T(8,128)S(1)}, f32[64,128...) custom-call(f32[16,16,128]{2,1,0:T(8,128)S(1)} %all_to_all.46.got_mine, ...), custom_call_target="tpu_custom_call" | custom-call | tf_op jit(solution)/shard_map/expand_and_project/pallas_call | solution.py:319
  77.9 1.1 collective-permute-done.6
  79.7 3.5 %all-to-all-start.3 = ((f32[16,24,128]{2,1,0:T(8,128)}), f32[16,24,128]{2,1,0:T(8,128)S(1)}, u32[]{:S(2)}, u32[]{:S(2)}) async-start(f32[16,24,128]{2,1,0:T(8,128)} %add.10), calls=%async_computation.3 | async-start | bytes 393216 | tf_op jit(solution)/shard_map/all_to_all | solution.py:473
  83.2 3.7 %collective-permute-start.7 = (f32[64,128]{1,0:T(8,128)S(1)}, f32[64,128]{1,0:T(8,128)S(1)}, u32[]{:S(2)}, u32[]{:S(2)}) collective-permute-start(f32[64,128]{1,0:T(8,128)S(1)} %get-tuple-element.69), channel_id=1, source_target_pairs={{0,8},{8,16},{16,24},{24,32},{32,40},{40,48},{48,56},{56,64},{64,7... | collective-permute-start | bytes 98312 | tf_op jit(solution)/shard_map/ppermute | solution.py:495
  86.9 1.9 collective-permute-start.8
  88.8 2.2 %collective-permute-start.9 = (f32[64,128]{1,0:T(8,128)S(1)}, f32[64,128]{1,0:T(8,128)S(1)}, u32[]{:S(2)}, u32[]{:S(2)}) collective-permute-start(f32[64,128]{1,0:T(8,128)S(1)} %get-tuple-element.71), channel_id=1, source_target_pairs={{0,1},{1,2},{2,3},{3,4},{4,5},{5,6},{6,7},{8,9},{9,10},{10,11},{11... | collective-permute-start | bytes 98312 | tf_op jit(solution)/shard_map/ppermute | solution.py:495
  91.0 1.3 collective-permute-start.10
  92.3 3.3 %collective-permute-done.10.east = f32[64,128]{1,0:T(8,128)S(1)} collective-permute-done((f32[64,128]{1,0:T(8,128)S(1)}, f32[64,128]{1,0:T(8,128)S(1)}, u32[]{:S(2)}, u32[]{:S(2)}) %collective-permute-start.10) | collective-permute-done | bytes 32800 | tf_op jit(solution)/shard_map/ppermute | solution.py:499
  95.7 11.0 %all_to_all.47 = f32[8,24,128]{2,1,0:T(8,128)S(1)} all-to-all(f32[8,24,128]{2,1,0:T(8,128)S(1)} %broadcast_in_dim.14), channel_id=1, replica_groups=mesh['y'=4,'x'=4,'core'=2,'z'=8] {'z'}, dimensions={0} | all-to-all | bytes 196608 | tf_op jit(solution)/shard_map/all_to_all | solution.py:473
  106.7 12.3 %all_to_all.48.got_mine = f32[16,24,128]{2,1,0:T(8,128)S(1)} all-to-all(f32[16,24,128]{2,1,0:T(8,128)S(1)} %broadcast_in_dim.15), channel_id=1, replica_groups=mesh['y'=4,'x'=4,'core'=2,'z'=8] {'y','x'}, dimensions={0} | all-to-all | bytes 393216 | tf_op jit(solution)/shard_map/all_to_all | solution.py:473
  119.0 5.2 %collective-permute-start.11 = (f32[16,24,128]{2,1,0:T(8,128)S(1)}, f32[16,24,128]{2,1,0:T(8,128)S(1)}, u32[]{:S(2)}, u32[]{:S(2)}) collective-permute-start(f32[16,24,128]{2,1,0:T(8,128)S(1)} %all_to_all.48.got_mine), channel_id=1, source_target_pairs={{0,8},{8,0},{1,9},{9,1},{2,10},{10,2},{3,11},{11,3},{4,12},{12,4},... | collective-permute-start | bytes 589832 | tf_op jit(solution)/shard_map/ppermute | solution.py:491
  125.4 9.7 %factor_and_expand.1 = (f32[64,2048]{1,0:T(8,128)S(1)}, f32[128,128]{1,0:T(8,128)S(1)}, f32[128,128]{1,0:T(8,128)S(1)}) custom-call(f32[16,24,128]{2,1,0:T(8,128)S(1)} %all_to_all.48.got_mine, f32[16,24,128]{2,1,0:T(8,128)S(1)} %collective-permute-done.11.got_other, bf16[4,2,256,2048]{3,2,1,0:T(8,128)(2,1)} %get-tuple-element.56.snap, ...), custom_call_target="tpu_custom_call" | custom-call | tf_op jit(solution)/shard_map/factor_and_expand/pallas_call | solution.py:357
  135.1 2.4 %collective-permute-start.12 = (f32[128,128]{1,0:T(8,128)S(1)}, f32[128,128]{1,0:T(8,128)S(1)}, u32[]{:S(2)}, u32[]{:S(2)}) collective-permute-start(f32[128,128]{1,0:T(8,128)S(1)} %get-tuple-element.80), channel_id=1, source_target_pairs={{0,8},{8,16},{16,24},{24,32},{32,40},{40,48},{48,56},{56,64},{64,7... | collective-permute-start | bytes 196616 | tf_op jit(solution)/shard_map/ppermute | solution.py:495
  137.5 2.2 %collective-permute-start.13 = (f32[128,128]{1,0:T(8,128)S(1)}, f32[128,128]{1,0:T(8,128)S(1)}, u32[]{:S(2)}, u32[]{:S(2)}) collective-permute-start(f32[128,128]{1,0:T(8,128)S(1)} %get-tuple-element.81), channel_id=1, source_target_pairs={{0,1},{1,2},{2,3},{3,4},{4,5},{5,6},{6,7},{8,9},{9,10},{10,11},{11... | collective-permute-start | bytes 196616 | tf_op jit(solution)/shard_map/ppermute | solution.py:495
  139.7 6.7 %project.1.base = f32[2,16,24,128]{3,2,1,0:T(8,128)S(1)} custom-call(bf16[4,2,256,2048]{3,2,1,0:T(8,128)(2,1)} %get-tuple-element.56.snap, f32[64,2048]{1,0:T(8,128)S(1)} %get-tuple-element.79.field), custom_call_target="tpu_custom_call" | custom-call | tf_op jit(solution)/shard_map/project/pallas_call | solution.py:382
  147.7 1.2 collective-permute-done.14
  148.9 12.4 %all_to_all.49 = f32[16,24,128]{2,1,0:T(8,128)S(1)} all-to-all(f32[16,24,128]{2,1,0:T(8,128)S(1)} %add.11), channel_id=1, replica_groups=mesh['y'=4,'x'=4,'core'=2,'z'=8] {'y','x'}, dimensions={0} | all-to-all | bytes 393216 | tf_op jit(solution)/shard_map/all_to_all | solution.py:473
  161.4 10.0 %all_to_all.50 = f32[8,24,128]{2,1,0:T(8,128)S(1)} all-to-all(f32[8,24,128]{2,1,0:T(8,128)S(1)} %broadcast_in_dim.16), channel_id=1, replica_groups=mesh['y'=4,'x'=4,'core'=2,'z'=8] {'z'}, dimensions={0} | all-to-all | bytes 196608 | tf_op jit(solution)/shard_map/all_to_all | solution.py:473
  171.4 9.9 %all_to_all.51.got_mine = f32[16,24,128]{2,1,0:T(8,128)S(1)} all-to-all(f32[16,24,128]{2,1,0:T(8,128)S(1)} %broadcast_in_dim.17), channel_id=1, replica_groups=mesh['y'=4,'x'=4,'core'=2,'z'=8] {'y','x'}, dimensions={0} | all-to-all | bytes 393216 | tf_op jit(solution)/shard_map/all_to_all | solution.py:473
  181.3 3.9 %collective-permute-start.15 = (f32[16,24,128]{2,1,0:T(8,128)S(1)}, f32[16,24,128]{2,1,0:T(8,128)S(1)}, u32[]{:S(2)}, u32[]{:S(2)}) collective-permute-start(f32[16,24,128]{2,1,0:T(8,128)S(1)} %all_to_all.51.got_mine), channel_id=1, source_target_pairs={{0,8},{8,0},{1,9},{9,1},{2,10},{10,2},{3,11},{11,3},{4,12},{12,4},... | collective-permute-start | bytes 589832 | tf_op jit(solution)/shard_map/ppermute | solution.py:491
  186.2 7.3 %factor_and_finish.1 = (f32[1024,128]{1,0:T(8,128)}, f32[64,64]{1,0:T(8,128)}) custom-call(f32[16,24,128]{2,1,0:T(8,128)S(1)} %all_to_all.51.got_mine, f32[16,24,128]{2,1,0:T(8,128)S(1)} %collective-permute-done.15.got_other, f32[64,2048]{1,0:T(8,128)S(1)} %get-tuple-element.79.field), custom_call_target="tpu_custom_call" | custom-call | tf_op jit(solution)/shard_map/factor_and_finish/pallas_call | solution.py:457
  (40 shorter events, 9.1 us)
Async XLA Ops:
  0.6 1.0 copy-start
  1.7 0.7 copy-start.1
  2.4 68.3 %copy-start.2 = (s32[16,128]{1,0:T(8,128)S(1)}, s32[16,128]{1,0:T(8,128)}, u32[]{:S(2)}) copy-start(s32[16,128]{1,0:T(8,128)} %sea.5) | copy-start | bytes 24580
  2.4 68.3 %copy-start.3 = (f32[16,128]{1,0:T(8,128)S(1)}, f32[16,128]{1,0:T(8,128)}, u32[]{:S(2)}) copy-start(f32[16,128]{1,0:T(8,128)} %pen.5) | copy-start | bytes 24580
  12.4 4.2 %collective-permute-start = (f32[16,16,128]{2,1,0:T(8,128)S(1)}, f32[16,16,128]{2,1,0:T(8,128)S(1)}, u32[]{:S(2)}, u32[]{:S(2)}) collective-permute-start(f32[16,16,128]{2,1,0:T(8,128)S(1)} %get-tuple-element.45), channel_id=1, source_target_pairs={{0,8},{8,0},{1,9},{9,1},{2,10},{10,2},{3,11},{11,3},{4,12},{12,4},... | collective-permute-start | bytes 393224 | tf_op jit(solution)/shard_map/ppermute | solution.py:482
  17.3 19.4 %all-to-all-start = ((f32[16,16,128]{2,1,0:T(8,128)}), f32[16,16,128]{2,1,0:T(8,128)S(1)}, u32[]{:S(2)}, u32[]{:S(2)}) async-start(f32[16,16,128]{2,1,0:T(8,128)} %add.9), calls=%async_computation | async-start | bytes 262144 | tf_op jit(solution)/shard_map/all_to_all | solution.py:473
  22.3 10.9 %collective-permute-start.1 = (f32[64,128]{1,0:T(8,128)S(1)}, f32[64,128]{1,0:T(8,128)S(1)}, u32[]{:S(2)}, u32[]{:S(2)}) collective-permute-start(f32[64,128]{1,0:T(8,128)S(1)} %get-tuple-element.51), channel_id=1, source_target_pairs={{0,8},{8,16},{16,24},{24,32},{32,40},{40,48},{48,56},{56,64},{64,7... | collective-permute-start | bytes 98312 | tf_op jit(solution)/shard_map/ppermute | solution.py:495
  26.4 6.8 %collective-permute-start.2 = (f32[64,128]{1,0:T(8,128)S(1)}, f32[64,128]{1,0:T(8,128)S(1)}, u32[]{:S(2)}, u32[]{:S(2)}) collective-permute-start(f32[64,128]{1,0:T(8,128)S(1)} %get-tuple-element.52), channel_id=1, source_target_pairs={{8,0},{16,8},{24,16},{32,24},{40,32},{48,40},{56,48},{64,56},{72,6... | collective-permute-start | bytes 98312 | tf_op jit(solution)/shard_map/ppermute | solution.py:499
  28.3 4.9 %collective-permute-start.3 = (f32[64,128]{1,0:T(8,128)S(1)}, f32[64,128]{1,0:T(8,128)S(1)}, u32[]{:S(2)}, u32[]{:S(2)}) collective-permute-start(f32[64,128]{1,0:T(8,128)S(1)} %get-tuple-element.53), channel_id=1, source_target_pairs={{0,1},{1,2},{2,3},{3,4},{4,5},{5,6},{6,7},{8,9},{9,10},{10,11},{11... | collective-permute-start | bytes 98312 | tf_op jit(solution)/shard_map/ppermute | solution.py:495
  31.8 4.8 %collective-permute-start.4 = (f32[64,128]{1,0:T(8,128)S(1)}, f32[64,128]{1,0:T(8,128)S(1)}, u32[]{:S(2)}, u32[]{:S(2)}) collective-permute-start(f32[64,128]{1,0:T(8,128)S(1)} %get-tuple-element.54), channel_id=1, source_target_pairs={{1,0},{2,1},{3,2},{4,3},{5,4},{6,5},{7,6},{9,8},{10,9},{11,10},{12... | collective-permute-start | bytes 98312 | tf_op jit(solution)/shard_map/ppermute | solution.py:499
  64.5 6.2 %collective-permute-start.5 = (f32[16,16,128]{2,1,0:T(8,128)S(1)}, f32[16,16,128]{2,1,0:T(8,128)S(1)}, u32[]{:S(2)}, u32[]{:S(2)}) collective-permute-start(f32[16,16,128]{2,1,0:T(8,128)S(1)} %all_to_all.46.got_mine), channel_id=1, source_target_pairs={{0,8},{8,0},{1,9},{9,1},{2,10},{10,2},{3,11},{11,3},{4,12},{12,4},... | collective-permute-start | bytes 393224 | tf_op jit(solution)/shard_map/ppermute | solution.py:491
  77.4 1.5 collective-permute-start.6
  79.7 16.0 %all-to-all-start.3 = ((f32[16,24,128]{2,1,0:T(8,128)}), f32[16,24,128]{2,1,0:T(8,128)S(1)}, u32[]{:S(2)}, u32[]{:S(2)}) async-start(f32[16,24,128]{2,1,0:T(8,128)} %add.10), calls=%async_computation.3 | async-start | bytes 393216 | tf_op jit(solution)/shard_map/all_to_all | solution.py:473
  83.2 9.1 %collective-permute-start.7 = (f32[64,128]{1,0:T(8,128)S(1)}, f32[64,128]{1,0:T(8,128)S(1)}, u32[]{:S(2)}, u32[]{:S(2)}) collective-permute-start(f32[64,128]{1,0:T(8,128)S(1)} %get-tuple-element.69), channel_id=1, source_target_pairs={{0,8},{8,16},{16,24},{24,32},{32,40},{40,48},{48,56},{56,64},{64,7... | collective-permute-start | bytes 98312 | tf_op jit(solution)/shard_map/ppermute | solution.py:495
  86.9 5.4 %collective-permute-start.8 = (f32[64,128]{1,0:T(8,128)S(1)}, f32[64,128]{1,0:T(8,128)S(1)}, u32[]{:S(2)}, u32[]{:S(2)}) collective-permute-start(f32[64,128]{1,0:T(8,128)S(1)} %get-tuple-element.70), channel_id=1, source_target_pairs={{8,0},{16,8},{24,16},{32,24},{40,32},{48,40},{56,48},{64,56},{72,6... | collective-permute-start | bytes 98312 | tf_op jit(solution)/shard_map/ppermute | solution.py:499
  88.8 3.5 %collective-permute-start.9 = (f32[64,128]{1,0:T(8,128)S(1)}, f32[64,128]{1,0:T(8,128)S(1)}, u32[]{:S(2)}, u32[]{:S(2)}) collective-permute-start(f32[64,128]{1,0:T(8,128)S(1)} %get-tuple-element.71), channel_id=1, source_target_pairs={{0,1},{1,2},{2,3},{3,4},{4,5},{5,6},{6,7},{8,9},{9,10},{10,11},{11... | collective-permute-start | bytes 98312 | tf_op jit(solution)/shard_map/ppermute | solution.py:495
  91.0 4.7 %collective-permute-start.10 = (f32[64,128]{1,0:T(8,128)S(1)}, f32[64,128]{1,0:T(8,128)S(1)}, u32[]{:S(2)}, u32[]{:S(2)}) collective-permute-start(f32[64,128]{1,0:T(8,128)S(1)} %get-tuple-element.72), channel_id=1, source_target_pairs={{1,0},{2,1},{3,2},{4,3},{5,4},{6,5},{7,6},{9,8},{10,9},{11,10},{12... | collective-permute-start | bytes 98312 | tf_op jit(solution)/shard_map/ppermute | solution.py:499
  119.0 6.3 %collective-permute-start.11 = (f32[16,24,128]{2,1,0:T(8,128)S(1)}, f32[16,24,128]{2,1,0:T(8,128)S(1)}, u32[]{:S(2)}, u32[]{:S(2)}) collective-permute-start(f32[16,24,128]{2,1,0:T(8,128)S(1)} %all_to_all.48.got_mine), channel_id=1, source_target_pairs={{0,8},{8,0},{1,9},{9,1},{2,10},{10,2},{3,11},{11,3},{4,12},{12,4},... | collective-permute-start | bytes 589832 | tf_op jit(solution)/shard_map/ppermute | solution.py:491
  135.1 11.3 %collective-permute-start.12 = (f32[128,128]{1,0:T(8,128)S(1)}, f32[128,128]{1,0:T(8,128)S(1)}, u32[]{:S(2)}, u32[]{:S(2)}) collective-permute-start(f32[128,128]{1,0:T(8,128)S(1)} %get-tuple-element.80), channel_id=1, source_target_pairs={{0,8},{8,16},{16,24},{24,32},{32,40},{40,48},{48,56},{56,64},{64,7... | collective-permute-start | bytes 196616 | tf_op jit(solution)/shard_map/ppermute | solution.py:495
  137.5 8.9 %collective-permute-start.13 = (f32[128,128]{1,0:T(8,128)S(1)}, f32[128,128]{1,0:T(8,128)S(1)}, u32[]{:S(2)}, u32[]{:S(2)}) collective-permute-start(f32[128,128]{1,0:T(8,128)S(1)} %get-tuple-element.81), channel_id=1, source_target_pairs={{0,1},{1,2},{2,3},{3,4},{4,5},{5,6},{6,7},{8,9},{9,10},{10,11},{11... | collective-permute-start | bytes 196616 | tf_op jit(solution)/shard_map/ppermute | solution.py:495
  147.3 1.5 collective-permute-start.14
  181.3 5.0 %collective-permute-start.15 = (f32[16,24,128]{2,1,0:T(8,128)S(1)}, f32[16,24,128]{2,1,0:T(8,128)S(1)}, u32[]{:S(2)}, u32[]{:S(2)}) collective-permute-start(f32[16,24,128]{2,1,0:T(8,128)S(1)} %all_to_all.51.got_mine), channel_id=1, source_target_pairs={{0,8},{8,0},{1,9},{9,1},{2,10},{10,2},{3,11},{11,3},{4,12},{12,4},... | collective-permute-start | bytes 589832 | tf_op jit(solution)/shard_map/ppermute | solution.py:491

commit v2 on v1

--- a/solution.py
+++ b/solution.py
@@ -21,6 +21,7 @@
 CHIPS = ("y", "x")
 LAT = ("y", "x", "core")
 SWAP = [(0, 1), (1, 0)]
+CROSS = [pair for i in range(1, 31, 2) for pair in ((i, i + 1), (i + 1, i))]
 VMEM_LIMIT = 50 * 1024 * 1024
 SMALL_LIMIT = 20 * 1024 * 1024
 
@@ -65,6 +66,19 @@
         first = jnp.where(lane == a, block[:, 0:1], first)
         last = jnp.where(lane == a, block[:, LANES - 1 : LANES], last)
     return first, last
+
+
+def packed_columns(strip):
+    total = strip[0:8]
+    for g in range(1, 8):
+        total = total + pltpu.roll(strip[8 * g : 8 * g + 8], 16 * g, 1)
+    return total
+
+
+def unpacked_columns(packed):
+    return jnp.concatenate(
+        [packed if g == 0 else pltpu.roll(packed, LANES - 16 * g, 1) for g in range(8)], axis=0
+    )
 
 
 def smooth(field_ref, a, north, south, west, east):
@@ -87,7 +101,33 @@
 def hand_out(pay, mine, other):
     me = lax.axis_index("core")
     mine[...] = pay[me]
-    other[...] = pay[1 - me]
+    depth = pay.shape[2]
+    for chip in range(16):
+        other[chip * depth : (chip + 1) * depth, :] = pay[1 - me, chip]
+
+
+def hand_out_edges(field, depth, other, cross, columns):
+    me = lax.axis_index("core")
+    top = field[:, cols(0)]
+    bottom = field[:, cols(ROWS - 1)]
+    other[16 * depth : 16 * depth + K, :] = jnp.where(me == 0, bottom, top)
+    cross[...] = jnp.where(me == 0, top, bottom)
+    first, last = edge_columns(field)
+    columns[0:8, :] = packed_columns(first)
+    columns[8:16, :] = packed_columns(last)
+
+
+def take_in_edges(pair, cross, columns):
+    me = lax.axis_index("core")
+    z = lax.axis_index("z")
+    depth = columns.shape[1] - 16
+    north = jnp.where(me == 0, cross[...], pair[...])
+    south = jnp.where(me == 0, pair[...], cross[...])
+    before = columns[jnp.maximum(z - 1, 0), depth + 8 : depth + 16, :]
+    after = columns[jnp.minimum(z + 1, 7), depth : depth + 8, :]
+    west = unpacked_columns(jnp.where(z > 0, before, 0.0))
+    east = unpacked_columns(jnp.where(z < 7, after, 0.0))
+    return north, south, west, east
 
 
 def take_in(mine, other, full):
@@ -123,25 +163,41 @@
 def inverse_factor(square):
     lane = lane_of((8, LANES))
     sub = lax.broadcasted_iota(jnp.int32, (8, LANES), 0)
-    blocks = []
-    for b in range(K // 8):
+    count = K // 8
+    held = []
+    for b in range(count):
         unit = jnp.where(lane - K == sub + 8 * b, 1.0, 0.0)
-        blocks.append(jnp.where(lane < K, square[8 * b : 8 * b + 8] * (1.0 / NPTS), unit))
-    for j in range(K):
-        home, inner = j // 8, j % 8
-        row = blocks[home][inner : inner + 1, :]
-        scaled = row / blocks[home][inner : inner + 1, j : j + 1]
-        for b in range(home, K // 8):
-            column = blocks[b][:, j : j + 1]
-            if b == home:
-                if inner == 7:
-                    continue
-                column = jnp.where(sub > inner, column, 0.0)
-            blocks[b] = blocks[b] - column * scaled
+        held.append(jnp.where(lane < K, square[8 * b : 8 * b + 8] * (1.0 / NPTS), unit))
+    for home in range(count):
+        columns = [
+            [
+                jnp.broadcast_to(held[b][:, 8 * home + q : 8 * home + q + 1], (8, LANES))
+                for b in range(home, count)
+            ]
+            for q in range(8)
+        ]
+        rows, scales = [], []
+        for q in range(8):
+            inverse = 1.0 / columns[q][0][q : q + 1, :]
+            row = held[home][q : q + 1, :]
+            scale = [column * inverse for column in columns[q]]
+            scale[0] = jnp.where(sub > q, scale[0], 0.0)
+            if q < 7:
+                held[home] = held[home] - scale[0] * row
+            for p in range(q + 1, 8):
+                entry = columns[p][0][q : q + 1, :]
+                columns[p] = [c - m * entry for c, m in zip(columns[p], scale)]
+            rows.append(row)
+            scales.append(scale)
+        for at, b in enumerate(range(home + 1, count), 1):
+            update = scales[0][at] * rows[0]
+            for q in range(1, 8):
+                update = update + scales[q][at] * rows[q]
+            held[b] = held[b] - update
     done = []
-    for b in range(K // 8):
-        diagonal = jnp.sum(jnp.where(lane == sub + 8 * b, blocks[b], 0.0), axis=1, keepdims=True)
-        done.append(blocks[b] * lax.rsqrt(diagonal))
+    for b in range(count):
+        diagonal = jnp.sum(jnp.where(lane == sub + 8 * b, held[b], 0.0), axis=1, keepdims=True)
+        done.append(held[b] * lax.rsqrt(diagonal))
     return pltpu.roll(jnp.concatenate(done, axis=0), K, 1)[:, 0:K]
 
 
@@ -170,71 +226,69 @@
 
 
 def begin_kernel(
-    snap, basis, sea, split_out, flat, top, bottom, first, last, mine, other, split, pay
+    snap, basis, sea, snap_out, flat, mine, other, cross, columns,
+    raw, held, split, pay, in_sems, out_sems,
 ):
-    step = pl.program_id(0)
-
-    @pl.when(step == 0)
-    def _():
-        pay[...] = jnp.zeros_like(pay)
-        for a in range(ROWS):
-            value = basis[pl.ds(a, K, stride=ROWS), :] * sea[a : a + 1, :].astype(F32)
-            flat[:, cols(a)] = value
-            store_split(split, a, value)
-        top[...] = flat[:, cols(0)]
-        bottom[...] = flat[:, cols(ROWS - 1)]
-        first[...], last[...] = edge_columns(flat)
-
-    for a in range(ROWS):
-        high, low = parts(snap[pl.ds(a, BLOCK, stride=ROWS), :])
-        split_out[0, 0, :, cols(a)] = high
-        split_out[0, 1, :, cols(a)] = low
-    both = dot_nt(split_out[0].reshape(2 * BLOCK, PTS), split[...])
-    both = both[0:BLOCK] + both[BLOCK : 2 * BLOCK]
-    summed = (both + pltpu.roll(both, K, 1)).reshape(16, 16, LANES)
-    half = step % 2
-    keep = (lane_of(summed.shape) < K) & (step >= 2)
-    pay[half, :, 0:16, :] = jnp.where(keep, pay[half, :, 0:16, :], summed)
-
-    @pl.when(step == pl.num_programs(0) - 1)
-    def _():
-        hand_out(pay, mine, other)
-
-
-def whole(shape):
-    return pl.BlockSpec(shape, lambda i: (0,) * len(shape))
+    deep = BLOCK // 2
+
+    def arrive(piece):
+        span = pl.ds(piece * deep * ROWS, deep * ROWS)
+        return pltpu.make_async_copy(snap.at[span], raw.at[span], in_sems.at[piece])
+
+    def leave(piece):
+        at = (piece // 2, slice(None), pl.ds((piece % 2) * deep, deep))
+        return pltpu.make_async_copy(held.at[at], snap_out.at[at], out_sems.at[piece])
+
+    for piece in range(2 * NBLOCK):
+        arrive(piece).start()
+    for a in range(ROWS):
+        value = basis[pl.ds(a, K, stride=ROWS), :] * sea[a : a + 1, :].astype(F32)
+        flat[:, cols(a)] = value
+        store_split(split, a, value)
+    hand_out_edges(flat, DEPTH, other, cross, columns)
+    for block in range(NBLOCK):
+        for piece in (2 * block, 2 * block + 1):
+            arrive(piece).wait()
+            span = slice((piece % 2) * deep, (piece % 2 + 1) * deep)
+            for a in range(ROWS):
+                high, low = parts(raw[pl.ds(piece * deep * ROWS + a, deep, stride=ROWS), :])
+                held[block, 0, span, cols(a)] = high
+                held[block, 1, span, cols(a)] = low
+            leave(piece).start()
+        both = dot_nt(held[block].reshape(2 * BLOCK, PTS), split[...])
+        put_coefficients(pay, block, both[0:BLOCK] + both[BLOCK : 2 * BLOCK])
+    hand_out(pay, mine, other)
+    for piece in range(2 * NBLOCK):
+        leave(piece).wait()
+
+
+VM = pl.BlockSpec(memory_space=pltpu.VMEM)
+HB = pl.BlockSpec(memory_space=pl.ANY)
+
+
+def shared_outputs(depth):
+    return [
+        jax.ShapeDtypeStruct((K, PTS), F32),
+        jax.ShapeDtypeStruct((16, depth, LANES), F32),
+        jax.ShapeDtypeStruct((16 * depth + K, LANES), F32),
+        jax.ShapeDtypeStruct((K, LANES), F32),
+        jax.ShapeDtypeStruct((16, LANES), F32),
+    ]
 
 
 def begin(snapshots, basis, sea):
-    halo = jax.ShapeDtypeStruct((K, LANES), F32)
-    share = jax.ShapeDtypeStruct((16, DEPTH, LANES), F32)
     return pl.pallas_call(
         begin_kernel,
-        grid=(NBLOCK,),
-        in_specs=[
-            pl.BlockSpec((BLOCK * ROWS, LANES), lambda i: (i, 0)),
-            whole((K * ROWS, LANES)),
-            whole((ROWS, LANES)),
-        ],
-        out_specs=[
-            pl.BlockSpec((1, 2, BLOCK, PTS), lambda i: (i, 0, 0, 0)),
-            whole((K, PTS)),
-            *[whole((K, LANES))] * 4,
-            *[whole((16, DEPTH, LANES))] * 2,
-        ],
-        out_shape=[
-            jax.ShapeDtypeStruct((NBLOCK, 2, BLOCK, PTS), BF16),
-            jax.ShapeDtypeStruct((K, PTS), F32),
-            halo,
-            halo,
-            halo,
-            halo,
-            share,
-            share,
-        ],
+        in_specs=[HB, VM, VM],
+        out_specs=[HB, *[VM] * 5],
+        out_shape=[jax.ShapeDtypeStruct((NBLOCK, 2, BLOCK, PTS), BF16), *shared_outputs(DEPTH)],
         scratch_shapes=[
+            pltpu.VMEM((NSNAP * ROWS, LANES), F32),
+            pltpu.VMEM((NBLOCK, 2, BLOCK, PTS), BF16),
             pltpu.VMEM((2 * K, PTS), BF16),
             pltpu.VMEM((2, 16, DEPTH, LANES), F32),
+            pltpu.SemaphoreType.DMA((2 * NBLOCK,)),
+            pltpu.SemaphoreType.DMA((2 * NBLOCK,)),
         ],
         compiler_params=pltpu.CompilerParams(vmem_limit_bytes=VMEM_LIMIT),
         name="split_and_project",
@@ -272,7 +326,7 @@
 
 
 def applied_field(total, prev, sides, sea, pen, out):
-    north, south, west, east = (side[...] for side in sides)
+    north, south, west, east = sides
     for a in range(ROWS):
         lap = smooth(prev, a, north, south, west, east)
         mask = sea[a : a + 1, :].astype(F32)
@@ -280,20 +334,19 @@
 
 
 def first_kernel(
-    got_mine, got_other, snap, prev, north, south, west, east, sea, pen,
-    field, top, bottom, first, last, mine, other,
+    got_mine, got_other, snap, prev, pair, near, around, sea, pen,
+    field, mine, other, cross, columns,
     full, held, spread, total, split, pay, sems,
 ):
     begin_copies(snap, held, sems)
     take_in(got_mine, got_other, full)
     coefficients_of(full, spread)
+    sides = take_in_edges(pair, near, around)
     expand(spread, snap, held, sems, total)
-    applied_field(total, prev, (north, south, west, east), sea, pen, field)
+    applied_field(total, prev, sides, sea, pen, field)
     for a in range(ROWS):
         store_split(split, a, field[:, cols(a)])
-    top[...] = field[:, cols(0)]
-    bottom[...] = field[:, cols(ROWS - 1)]
-    first[...], last[...] = edge_columns(field)
+    hand_out_edges(field, SHARD, other, cross, columns)
     pay[...] = jnp.zeros_like(pay)
     put_square(pay, 16, folded(dot_nt(split[...], split[...])))
     project(held, split, pay)
@@ -309,18 +362,12 @@
     ]
 
 
-VM = pl.BlockSpec(memory_space=pltpu.VMEM)
-HB = pl.BlockSpec(memory_space=pl.ANY)
-
-
 def first_step(got, snap, prev, sides, sea, pen):
-    halo = jax.ShapeDtypeStruct((K, LANES), F32)
-    share = jax.ShapeDtypeStruct((16, SHARD, LANES), F32)
     return pl.pallas_call(
         first_kernel,
-        in_specs=[VM, VM, HB, *[VM] * 7],
-        out_specs=[VM] * 7,
-        out_shape=[jax.ShapeDtypeStruct((K, PTS), F32), halo, halo, halo, halo, share, share],
+        in_specs=[VM, VM, HB, *[VM] * 6],
+        out_specs=[VM] * 5,
+        out_shape=shared_outputs(SHARD),
         scratch_shapes=[
             *scratch_for_expand(DEPTH),
             pltpu.VMEM((2 * K, PTS), BF16),
@@ -333,7 +380,7 @@
 
 
 def second_kernel(
-    got_mine, got_other, snap, prev, north, south, west, east, sea, pen,
+    got_mine, got_other, snap, prev, pair, near, around, sea, pen,
     field, bottom, last,
     full, held, spread, total, raw, sems,
 ):
@@ -341,8 +388,9 @@
     take_in(got_mine, got_other, full)
     coefficients_of(full, spread)
     inverse = inverse_factor(square_of(full, 16))
+    sides = take_in_edges(pair, near, around)
     expand(spread, snap, held, sems, total)
-    applied_field(total, prev, (north, south, west, east), sea, pen, raw)
+    applied_field(total, prev, sides, sea, pen, raw)
     field[...] = dot_nn(inverse, raw[...], HIGHEST)
     bottom[0:K, :] = field[:, cols(ROWS - 1)]
     bottom[K : 2 * K, :] = field[:, cols(ROWS - 1)] * pen[ROWS - 1 : ROWS, :]
@@ -356,7 +404,7 @@
     halo = jax.ShapeDtypeStruct((2 * K, LANES), F32)
     return pl.pallas_call(
         second_kernel,
-        in_specs=[VM, VM, HB, *[VM] * 7],
+        in_specs=[VM, VM, HB, *[VM] * 6],
         out_specs=[VM] * 3,
         out_shape=[jax.ShapeDtypeStruct((K, PTS), F32), halo, halo],
         scratch_shapes=[
@@ -423,12 +471,14 @@
 
 
 def rough_step(field, north, west, pen, base):
-    share = jax.ShapeDtypeStruct((16, SHARD, LANES), F32)
     return pl.pallas_call(
         rough_kernel,
         in_specs=[VM] * 5,
         out_specs=[VM] * 2,
-        out_shape=[share, share],
+        out_shape=[
+            jax.ShapeDtypeStruct((16, SHARD, LANES), F32),
+            jax.ShapeDtypeStruct((16 * SHARD, LANES), F32),
+        ],
         scratch_shapes=[
             pltpu.VMEM((2 * K, PTS + 4 * LANES), BF16),
             pltpu.VMEM((2 * K, PTS + 4 * LANES), BF16),
@@ -478,40 +528,35 @@
 
 
 def summed_everywhere(mine, other, edges=None):
-    sides = None
-    pair = mine + lax.ppermute(other, "core", SWAP)
+    depth = mine.shape[1]
+    got = lax.ppermute(other, "core", SWAP)
+    pair = mine + got[: 16 * depth].reshape(mine.shape)
     if edges is not None:
-        pair, edges = lax.optimization_barrier((pair, edges))
-        sides = sides_of(*edges)
+        cross, columns = edges
+        pair, cross = lax.optimization_barrier((pair, cross))
+        near = lax.ppermute(cross, LAT, CROSS)
     shares = exchange(pair, CHIPS)
     if edges is not None:
-        shares, sides = lax.optimization_barrier((shares, sides))
-    shares = exchange(copies(shares.sum(axis=0), 8), "z")
-    half = exchange(copies(shares.sum(axis=0), 16), CHIPS)
-    return (half, lax.ppermute(half, "core", SWAP)), sides
+        shares, near = lax.optimization_barrier((shares, near))
+    share = shares.sum(axis=0)
+    if edges is not None:
+        share = jnp.concatenate([share, columns], axis=0)
+    around = exchange(copies(share, 8), "z")
+    half = exchange(copies(around[:, :depth].sum(axis=0), 16), CHIPS)
+    both = (half, lax.ppermute(half, "core", SWAP))
+    if edges is None:
+        return both, None
+    return both, (got[16 * depth :], near, around)
 
 
 def from_below(value, axis, count):
     return lax.ppermute(value, axis, [(i, i + 1) for i in range(count - 1)])
 
 
-def from_above(value, axis, count):
-    return lax.ppermute(value, axis, [(i + 1, i) for i in range(count - 1)])
-
-
-def sides_of(top, bottom, first, last):
-    return (
-        from_below(bottom, LAT, 32),
-        from_above(top, LAT, 32),
-        from_below(last, "z", 8),
-        from_above(first, "z", 8),
-    )
-
-
 def local(snapshots, land_sea, penalty, initial_basis):
-    snap, start, *edges, mine, other = begin(snapshots, initial_basis, land_sea)
+    snap, start, mine, other, *edges = begin(snapshots, initial_basis, land_sea)
     got, sides = summed_everywhere(mine, other, edges)
-    applied, *edges, mine, other = first_step(got, snap, start, sides, land_sea, penalty)
+    applied, mine, other, *edges = first_step(got, snap, start, sides, land_sea, penalty)
     got, sides = summed_everywhere(mine, other, edges)
     applied, bottom, last = second_step(got, snap, applied, sides, land_sea, penalty)
     north = from_below(bottom, LAT, 32)

time: 194 us -> 172 us (0.89)
  starting transfers between devices: 51.4 us -> 32.4 us
  Pallas kernels: 41.2 us -> 33.6 us
  blocking collectives: 83.4 us -> 87.4 us
    ppermute x6 -> x2, starting transfers between devices: 18.1 us -> 4.64 us  [from_below(): return lax.ppermute(value, axis, [(i, i + 1) for i in range(count - 1)])]
    ppermute x10 -> x8, starting transfers between devices: 24.7 us -> 19.2 us  [the longest x2 7.74 us: summed_everywhere(): near = lax.ppermute(cross, LAT, CROSS)]
    pallas_call x3, Pallas kernels: 26.4 us -> 22.3 us  [the longest x1 9.17 us: begin(): pl.pallas_call(begin_kernel, in_specs=[HB, VM, VM], out_specs=[HB, *[VM]...]
    all_to_all x7, blocking collectives: 83.4 us -> 87.4 us  [exchange(): return lax.all_to_all(value, axis, 0, 0, tiled=True)]
    pallas_call x1, Pallas kernels: 7.25 us -> 3.73 us  [last_step(): pl.pallas_call(last_kernel, in_specs=[VM] * 3, out_specs=[VM] * 2, out_sh...]
    all_to_all x2, waiting for transfers between devices: 0.01 us -> 3.04 us  [exchange(): return lax.all_to_all(value, axis, 0, 0, tiled=True)]
    ppermute x10 -> x8, waiting for transfers between devices: 13.2 us -> 10.2 us  [the longest x2 3.76 us: summed_everywhere(): near = lax.ppermute(cross, LAT, CROSS)]
  transfers between devices with their start and end apart: 18 -> 12, of which waited for: 8 -> 10; matrix products, arithmetic and copies ran while one was open for 0% -> 0% of each run, Pallas kernels for 3% -> 4%
where the time goes in v2:
time: 172 us; the launch traced here: 171 us
  blocking collectives  87.4 us (51%)
  Pallas kernels  33.6 us (20%)
  starting transfers between devices  32.4 us (19%)
  waiting for transfers between devices  13.3 us (8%)
  local copies, waits for them, and re-layouts  1.84 us (1%)
    all_to_all x7, blocking collectives, exchange(): return lax.all_to_all(value, axis, 0, 0, tiled=True)  87.4 us
    pallas_call x1, Pallas kernels, begin(): pl.pallas_call(begin_kernel, in_specs=[HB, VM, VM], out_specs=[HB, *[VM]...  9.17 us
    all_to_all x2, starting transfers between devices, exchange(): return lax.all_to_all(value, axis, 0, 0, tiled=True)  8.54 us
    ppermute x2, starting transfers between devices, summed_everywhere(): near = lax.ppermute(cross, LAT, CROSS)  7.74 us
    ppermute x3, starting transfers between devices, summed_everywhere(): both = (half, lax.ppermute(half, 'core', SWAP))  7.23 us
    pallas_call x1, Pallas kernels, first_step(): pl.pallas_call(first_kernel, in_specs=[VM, VM, HB, *[VM] * 6], out_specs=...  6.75 us
    pallas_call x1, Pallas kernels, project_step(): pl.pallas_call(project_kernel, in_specs=[HB, VM], out_specs=VM, out_shape...  6.68 us
    pallas_call x1, Pallas kernels, second_step(): pl.pallas_call(second_kernel, in_specs=[VM, VM, HB, *[VM] * 6], out_specs...  6.38 us
  transfers between devices with their start and end apart: 12, of which 10 were waited for; matrix products, arithmetic and copies ran while one was open for 0% of the time, Pallas kernels for 4%

profile of v2, /device:TPU:1, one launch (start us, length us, event | category | flops | bytes accessed | tf_op | source)
XLA Modules:
  0.0 170.9 jit_solution(4141667792685089419)
XLA Ops:
  0.6 1.0 copy-done
  2.4 9.2 %split_and_project.1 = (bf16[4,2,256,2048]{3,2,1,0:T(8,128)(2,1)}, f32[64,2048]{1,0:T(8,128)S(1)}, f32[16,16,128]{2,1,0:T(8,128)S(1)}, f32[320,128]{1,0:T(8,128)...) custom-call(f32[16384,128]{1,0:T(8,128)} %bitcast.7, f32[1024,128]{1,0:T(8,128)S(1)} %bitcast.6, s32[16,128]{1,0:T(8,128)S(1)} %copy-done.1), custom_call_target="tpu_custom_call" | custom-call | tf_op jit(solution)/shard_map/split_and_project/pallas_call | solution.py:280
  11.6 3.3 %collective-permute-start = (f32[320,128]{1,0:T(8,128)S(1)}, f32[320,128]{1,0:T(8,128)S(1)}, u32[]{:S(2)}, u32[]{:S(2)}) collective-permute-start(f32[320,128]{1,0:T(8,128)S(1)} %get-tuple-element.29), channel_id=1, source_target_pairs={{0,8},{8,0},{1,9},{9,1},{2,10},{10,2},{3,11},{11,3},{4,12},{12,4},... | collective-permute-start | bytes 491528 | tf_op jit(solution)/shard_map/ppermute | solution.py:532
  14.9 1.0 collective-permute-done
  16.6 5.0 %all-to-all-start = ((f32[16,16,128]{2,1,0:T(8,128)}), f32[16,16,128]{2,1,0:T(8,128)S(1)}, u32[]{:S(2)}, u32[]{:S(2)}) async-start(f32[16,16,128]{2,1,0:T(8,128)} %add.9), calls=%async_computation | async-start | bytes 262144 | tf_op jit(solution)/shard_map/all_to_all | solution.py:523
  21.6 4.1 %collective-permute-start.1 = (f32[64,128]{1,0:T(8,128)S(1)}, f32[64,128]{1,0:T(8,128)S(1)}, u32[]{:S(2)}, u32[]{:S(2)}) collective-permute-start(f32[64,128]{1,0:T(8,128)S(1)} %get-tuple-element.32), channel_id=1, source_target_pairs={{8,16},{16,8},{24,32},{32,24},{40,48},{48,40},{56,64},{64,56},{72,... | collective-permute-start | bytes 98312 | tf_op jit(solution)/shard_map/ppermute | solution.py:537
  25.7 1.9 %collective-permute-done.1.near = f32[64,128]{1,0:T(8,128)S(1)} collective-permute-done((f32[64,128]{1,0:T(8,128)S(1)}, f32[64,128]{1,0:T(8,128)S(1)}, u32[]{:S(2)}, u32[]{:S(2)}) %collective-permute-start.1) | collective-permute-done | bytes 32800 | tf_op jit(solution)/shard_map/ppermute | solution.py:537
  28.5 16.0 %all_to_all.45.around = f32[8,32,128]{2,1,0:T(8,128)S(1)} all-to-all(f32[8,32,128]{2,1,0:T(8,128)S(1)} %broadcast_in_dim.12), channel_id=1, replica_groups=mesh['y'=4,'x'=4,'core'=2,'z'=8] {'z'}, dimensions={0} | all-to-all | bytes 262144 | tf_op jit(solution)/shard_map/all_to_all | solution.py:523
  44.6 14.4 %all_to_all.46.got_mine = f32[16,16,128]{2,1,0:T(8,128)S(1)} all-to-all(f32[16,16,128]{2,1,0:T(8,128)S(1)} %broadcast_in_dim.13), channel_id=1, replica_groups=mesh['y'=4,'x'=4,'core'=2,'z'=8] {'y','x'}, dimensions={0} | all-to-all | bytes 262144 | tf_op jit(solution)/shard_map/all_to_all | solution.py:523
  58.9 1.8 %collective-permute-start.2 = (f32[16,16,128]{2,1,0:T(8,128)S(1)}, f32[16,16,128]{2,1,0:T(8,128)S(1)}, u32[]{:S(2)}, u32[]{:S(2)}) collective-permute-start(f32[16,16,128]{2,1,0:T(8,128)S(1)} %all_to_all.46.got_mine), channel_id=1, source_target_pairs={{0,8},{8,0},{1,9},{9,1},{2,10},{10,2},{3,11},{11,3},{4,12},{12,4},... | collective-permute-start | bytes 393224 | tf_op jit(solution)/shard_map/ppermute | solution.py:546
  60.7 1.0 collective-permute-done.2.got_other
  61.7 6.7 %expand_and_project.1 = (f32[64,2048]{1,0:T(8,128)S(1)}, f32[16,24,128]{2,1,0:T(8,128)S(1)}, f32[448,128]{1,0:T(8,128)S(1)}, f32[64,128]{1,0:T(8,128)S(1)}, f32[16,128]{1,0:T(8,128)S(1)}) custom-call(f32[16,16,128]{2,1,0:T(8,128)S(1)} %all_to_all.46.got_mine, f32[16,16,128]{2,1,0:T(8,128)S(1)} %collective-permute-done.2.got_other, ...), custom_call_target="tpu_custom_call" | custom-call | tf_op jit(solution)/shard_map/expand_and_project/pallas_call | solution.py:366
  69.1 1.1 collective-permute-done.3
  70.9 3.5 %all-to-all-start.3 = ((f32[16,24,128]{2,1,0:T(8,128)}), f32[16,24,128]{2,1,0:T(8,128)S(1)}, u32[]{:S(2)}, u32[]{:S(2)}) async-start(f32[16,24,128]{2,1,0:T(8,128)} %add.10), calls=%async_computation.3 | async-start | bytes 393216 | tf_op jit(solution)/shard_map/all_to_all | solution.py:523
  74.5 3.7 %collective-permute-start.4 = (f32[64,128]{1,0:T(8,128)S(1)}, f32[64,128]{1,0:T(8,128)S(1)}, u32[]{:S(2)}, u32[]{:S(2)}) collective-permute-start(f32[64,128]{1,0:T(8,128)S(1)} %get-tuple-element.42), channel_id=1, source_target_pairs={{8,16},{16,8},{24,32},{32,24},{40,48},{48,40},{56,64},{64,56},{72,... | collective-permute-start | bytes 98312 | tf_op jit(solution)/shard_map/ppermute | solution.py:537
  78.1 1.9 %collective-permute-done.4.near = f32[64,128]{1,0:T(8,128)S(1)} collective-permute-done((f32[64,128]{1,0:T(8,128)S(1)}, f32[64,128]{1,0:T(8,128)S(1)}, u32[]{:S(2)}, u32[]{:S(2)}) %collective-permute-start.4) | collective-permute-done | bytes 32800 | tf_op jit(solution)/shard_map/ppermute | solution.py:537
  80.0 2.2 %all-to-all-done.3 = f32[16,24,128]{2,1,0:T(8,128)S(1)} async-done(((f32[16,24,128]{2,1,0:T(8,128)}), f32[16,24,128]{2,1,0:T(8,128)S(1)}, u32[]{:S(2)}, u32[]{:S(2)}) %all-to-all-start.3) | async-done | bytes 196640 | tf_op jit(solution)/shard_map/all_to_all | solution.py:523
  82.2 10.5 %all_to_all.47.around = f32[8,40,128]{2,1,0:T(8,128)S(1)} all-to-all(f32[8,40,128]{2,1,0:T(8,128)S(1)} %broadcast_in_dim.14), channel_id=1, replica_groups=mesh['y'=4,'x'=4,'core'=2,'z'=8] {'z'}, dimensions={0} | all-to-all | bytes 327680 | tf_op jit(solution)/shard_map/all_to_all | solution.py:523
  92.7 14.4 %all_to_all.48.got_mine = f32[16,24,128]{2,1,0:T(8,128)S(1)} all-to-all(f32[16,24,128]{2,1,0:T(8,128)S(1)} %broadcast_in_dim.15), channel_id=1, replica_groups=mesh['y'=4,'x'=4,'core'=2,'z'=8] {'y','x'}, dimensions={0} | all-to-all | bytes 393216 | tf_op jit(solution)/shard_map/all_to_all | solution.py:523
  107.1 1.2 collective-permute-start.5
  108.4 1.1 collective-permute-done.5.got_other
  109.4 6.4 %factor_and_expand.1 = (f32[64,2048]{1,0:T(8,128)S(1)}, f32[128,128]{1,0:T(8,128)S(1)}, f32[128,128]{1,0:T(8,128)S(1)}) custom-call(f32[16,24,128]{2,1,0:T(8,128)S(1)} %all_to_all.48.got_mine, f32[16,24,128]{2,1,0:T(8,128)S(1)} %collective-permute-done.5.got_other, bf16[4,2,256,2048]{3,2,1,0:T(8,128)(2,1)} %get-tuple-element.35.snap, ...), custom_call_target="tpu_custom_call" | custom-call | tf_op jit(solution)/shard_map/factor_and_expand/pallas_call | solution.py:405
  115.8 2.4 %collective-permute-start.6 = (f32[128,128]{1,0:T(8,128)S(1)}, f32[128,128]{1,0:T(8,128)S(1)}, u32[]{:S(2)}, u32[]{:S(2)}) collective-permute-start(f32[128,128]{1,0:T(8,128)S(1)} %get-tuple-element.48), channel_id=1, source_target_pairs={{0,8},{8,16},{16,24},{24,32},{32,40},{40,48},{48,56},{56,64},{64,7... | collective-permute-start | bytes 196616 | tf_op jit(solution)/shard_map/ppermute | solution.py:553
  118.3 2.2 %collective-permute-start.7 = (f32[128,128]{1,0:T(8,128)S(1)}, f32[128,128]{1,0:T(8,128)S(1)}, u32[]{:S(2)}, u32[]{:S(2)}) collective-permute-start(f32[128,128]{1,0:T(8,128)S(1)} %get-tuple-element.49), channel_id=1, source_target_pairs={{0,1},{1,2},{2,3},{3,4},{4,5},{5,6},{6,7},{8,9},{9,10},{10,11},{11... | collective-permute-start | bytes 196616 | tf_op jit(solution)/shard_map/ppermute | solution.py:553
  120.5 6.7 %project.1.base = f32[2,16,24,128]{3,2,1,0:T(8,128)S(1)} custom-call(bf16[4,2,256,2048]{3,2,1,0:T(8,128)(2,1)} %get-tuple-element.35.snap, f32[64,2048]{1,0:T(8,128)S(1)} %get-tuple-element.47.field), custom_call_target="tpu_custom_call" | custom-call | tf_op jit(solution)/shard_map/project/pallas_call | solution.py:430
  128.4 1.2 collective-permute-done.8
  129.6 12.4 %all_to_all.49 = f32[16,24,128]{2,1,0:T(8,128)S(1)} all-to-all(f32[16,24,128]{2,1,0:T(8,128)S(1)} %add.11), channel_id=1, replica_groups=mesh['y'=4,'x'=4,'core'=2,'z'=8] {'y','x'}, dimensions={0} | all-to-all | bytes 393216 | tf_op jit(solution)/shard_map/all_to_all | solution.py:523
  142.1 10.0 %all_to_all.50 = f32[8,24,128]{2,1,0:T(8,128)S(1)} all-to-all(f32[8,24,128]{2,1,0:T(8,128)S(1)} %broadcast_in_dim.16), channel_id=1, replica_groups=mesh['y'=4,'x'=4,'core'=2,'z'=8] {'z'}, dimensions={0} | all-to-all | bytes 196608 | tf_op jit(solution)/shard_map/all_to_all | solution.py:523
  152.1 9.8 %all_to_all.51.got_mine = f32[16,24,128]{2,1,0:T(8,128)S(1)} all-to-all(f32[16,24,128]{2,1,0:T(8,128)S(1)} %broadcast_in_dim.17), channel_id=1, replica_groups=mesh['y'=4,'x'=4,'core'=2,'z'=8] {'y','x'}, dimensions={0} | all-to-all | bytes 393216 | tf_op jit(solution)/shard_map/all_to_all | solution.py:523
  161.9 4.2 %collective-permute-start.9 = (f32[16,24,128]{2,1,0:T(8,128)S(1)}, f32[16,24,128]{2,1,0:T(8,128)S(1)}, u32[]{:S(2)}, u32[]{:S(2)}) collective-permute-start(f32[16,24,128]{2,1,0:T(8,128)S(1)} %all_to_all.51.got_mine), channel_id=1, source_target_pairs={{0,8},{8,0},{1,9},{9,1},{2,10},{10,2},{3,11},{11,3},{4,12},{12,4},... | collective-permute-start | bytes 589832 | tf_op jit(solution)/shard_map/ppermute | solution.py:546
  166.1 1.1 collective-permute-done.9.got_other
  167.2 3.7 %factor_and_finish.1 = (f32[1024,128]{1,0:T(8,128)}, f32[64,64]{1,0:T(8,128)}) custom-call(f32[16,24,128]{2,1,0:T(8,128)S(1)} %all_to_all.51.got_mine, f32[16,24,128]{2,1,0:T(8,128)S(1)} %collective-permute-done.9.got_other, f32[64,2048]{1,0:T(8,128)S(1)} %get-tuple-element.47.field), custom_call_target="tpu_custom_call" | custom-call | tf_op jit(solution)/shard_map/factor_and_finish/pallas_call | solution.py:507
  (34 shorter events, 5.0 us)
Async XLA Ops:
  0.6 1.0 copy-start
  1.7 0.7 copy-start.1
  2.4 59.3 %copy-start.2 = (s32[16,128]{1,0:T(8,128)S(1)}, s32[16,128]{1,0:T(8,128)}, u32[]{:S(2)}) copy-start(s32[16,128]{1,0:T(8,128)} %sea.5) | copy-start | bytes 24580
  2.4 59.3 %copy-start.3 = (f32[16,128]{1,0:T(8,128)S(1)}, f32[16,128]{1,0:T(8,128)}, u32[]{:S(2)}) copy-start(f32[16,128]{1,0:T(8,128)} %pen.5) | copy-start | bytes 24580
  11.6 4.4 %collective-permute-start = (f32[320,128]{1,0:T(8,128)S(1)}, f32[320,128]{1,0:T(8,128)S(1)}, u32[]{:S(2)}, u32[]{:S(2)}) collective-permute-start(f32[320,128]{1,0:T(8,128)S(1)} %get-tuple-element.29), channel_id=1, source_target_pairs={{0,8},{8,0},{1,9},{9,1},{2,10},{10,2},{3,11},{11,3},{4,12},{12,4},... | collective-permute-start | bytes 491528 | tf_op jit(solution)/shard_map/ppermute | solution.py:532
  16.6 11.9 %all-to-all-start = ((f32[16,16,128]{2,1,0:T(8,128)}), f32[16,16,128]{2,1,0:T(8,128)S(1)}, u32[]{:S(2)}, u32[]{:S(2)}) async-start(f32[16,16,128]{2,1,0:T(8,128)} %add.9), calls=%async_computation | async-start | bytes 262144 | tf_op jit(solution)/shard_map/all_to_all | solution.py:523
  21.6 6.0 %collective-permute-start.1 = (f32[64,128]{1,0:T(8,128)S(1)}, f32[64,128]{1,0:T(8,128)S(1)}, u32[]{:S(2)}, u32[]{:S(2)}) collective-permute-start(f32[64,128]{1,0:T(8,128)S(1)} %get-tuple-element.32), channel_id=1, source_target_pairs={{8,16},{16,8},{24,32},{32,24},{40,48},{48,40},{56,64},{64,56},{72,... | collective-permute-start | bytes 98312 | tf_op jit(solution)/shard_map/ppermute | solution.py:537
  58.9 2.8 %collective-permute-start.2 = (f32[16,16,128]{2,1,0:T(8,128)S(1)}, f32[16,16,128]{2,1,0:T(8,128)S(1)}, u32[]{:S(2)}, u32[]{:S(2)}) collective-permute-start(f32[16,16,128]{2,1,0:T(8,128)S(1)} %all_to_all.46.got_mine), channel_id=1, source_target_pairs={{0,8},{8,0},{1,9},{9,1},{2,10},{10,2},{3,11},{11,3},{4,12},{12,4},... | collective-permute-start | bytes 393224 | tf_op jit(solution)/shard_map/ppermute | solution.py:546
  68.5 1.8 %collective-permute-start.3 = (f32[448,128]{1,0:T(8,128)S(1)}, f32[448,128]{1,0:T(8,128)S(1)}, u32[]{:S(2)}, u32[]{:S(2)}) collective-permute-start(f32[448,128]{1,0:T(8,128)S(1)} %get-tuple-element.39), channel_id=1, source_target_pairs={{0,8},{8,0},{1,9},{9,1},{2,10},{10,2},{3,11},{11,3},{4,12},{12,4},... | collective-permute-start | bytes 688136 | tf_op jit(solution)/shard_map/ppermute | solution.py:532
  70.9 11.2 %all-to-all-start.3 = ((f32[16,24,128]{2,1,0:T(8,128)}), f32[16,24,128]{2,1,0:T(8,128)S(1)}, u32[]{:S(2)}, u32[]{:S(2)}) async-start(f32[16,24,128]{2,1,0:T(8,128)} %add.10), calls=%async_computation.3 | async-start | bytes 393216 | tf_op jit(solution)/shard_map/all_to_all | solution.py:523
  74.5 5.6 %collective-permute-start.4 = (f32[64,128]{1,0:T(8,128)S(1)}, f32[64,128]{1,0:T(8,128)S(1)}, u32[]{:S(2)}, u32[]{:S(2)}) collective-permute-start(f32[64,128]{1,0:T(8,128)S(1)} %get-tuple-element.42), channel_id=1, source_target_pairs={{8,16},{16,8},{24,32},{32,24},{40,48},{48,40},{56,64},{64,56},{72,... | collective-permute-start | bytes 98312 | tf_op jit(solution)/shard_map/ppermute | solution.py:537
  107.1 2.3 %collective-permute-start.5 = (f32[16,24,128]{2,1,0:T(8,128)S(1)}, f32[16,24,128]{2,1,0:T(8,128)S(1)}, u32[]{:S(2)}, u32[]{:S(2)}) collective-permute-start(f32[16,24,128]{2,1,0:T(8,128)S(1)} %all_to_all.48.got_mine), channel_id=1, source_target_pairs={{0,8},{8,0},{1,9},{9,1},{2,10},{10,2},{3,11},{11,3},{4,12},{12,4},... | collective-permute-start | bytes 589832 | tf_op jit(solution)/shard_map/ppermute | solution.py:546
  115.8 11.4 %collective-permute-start.6 = (f32[128,128]{1,0:T(8,128)S(1)}, f32[128,128]{1,0:T(8,128)S(1)}, u32[]{:S(2)}, u32[]{:S(2)}) collective-permute-start(f32[128,128]{1,0:T(8,128)S(1)} %get-tuple-element.48), channel_id=1, source_target_pairs={{0,8},{8,16},{16,24},{24,32},{32,40},{40,48},{48,56},{56,64},{64,7... | collective-permute-start | bytes 196616 | tf_op jit(solution)/shard_map/ppermute | solution.py:553
  118.3 8.9 %collective-permute-start.7 = (f32[128,128]{1,0:T(8,128)S(1)}, f32[128,128]{1,0:T(8,128)S(1)}, u32[]{:S(2)}, u32[]{:S(2)}) collective-permute-start(f32[128,128]{1,0:T(8,128)S(1)} %get-tuple-element.49), channel_id=1, source_target_pairs={{0,1},{1,2},{2,3},{3,4},{4,5},{5,6},{6,7},{8,9},{9,10},{10,11},{11... | collective-permute-start | bytes 196616 | tf_op jit(solution)/shard_map/ppermute | solution.py:553
  128.1 1.5 collective-permute-start.8
  161.9 5.3 %collective-permute-start.9 = (f32[16,24,128]{2,1,0:T(8,128)S(1)}, f32[16,24,128]{2,1,0:T(8,128)S(1)}, u32[]{:S(2)}, u32[]{:S(2)}) collective-permute-start(f32[16,24,128]{2,1,0:T(8,128)S(1)} %all_to_all.51.got_mine), channel_id=1, source_target_pairs={{0,8},{8,0},{1,9},{9,1},{2,10},{10,2},{3,11},{11,3},{4,12},{12,4},... | collective-permute-start | bytes 589832 | tf_op jit(solution)/shard_map/ppermute | solution.py:546

commit v3 on v2

--- a/solution.py
+++ b/solution.py
@@ -23,6 +23,7 @@
 SWAP = [(0, 1), (1, 0)]
 CROSS = [pair for i in range(1, 31, 2) for pair in ((i, i + 1), (i + 1, i))]
 VMEM_LIMIT = 50 * 1024 * 1024
+MIDDLE_LIMIT = 36 * 1024 * 1024
 SMALL_LIMIT = 20 * 1024 * 1024
 
 
@@ -201,28 +202,27 @@
     return pltpu.roll(jnp.concatenate(done, axis=0), K, 1)[:, 0:K]
 
 
-def put_coefficients(pay, block, both):
-    half = block % 2
-    summed = both + pltpu.roll(both, K, 1)
-    summed = summed.reshape(16, 16, LANES)
-    if block < 2:
-        pay[half, :, 0:16, :] = summed
-    else:
-        old = pay[half, :, 0:16, :]
-        pay[half, :, 0:16, :] = jnp.where(lane_of(old.shape) < K, old, summed)
-
-
-def coefficients_of(full, spread):
-    packed = full[:, :, 0:16, :].reshape(NSNAP // 2, LANES)
-    turned = packed.T
-    if spread is not None:
-        for block in range(NBLOCK):
-            top = (block // 2) * K
-            left = (block % 2) * BLOCK
-            high, low = parts(turned[top : top + K, left : left + BLOCK])
-            spread[block, 0:K, :] = high
-            spread[block, K : 2 * K, :] = low
-    return turned
+def put_coefficients(pay, block, held, split):
+    both = dot_nt(split[...], held[block].reshape(2 * BLOCK, PTS))
+    rows = both[0:K] + both[K : 2 * K]
+    turned = rows[:, 0:BLOCK] + rows[:, BLOCK : 2 * BLOCK]
+    for part in range(BLOCK // LANES):
+        at = block * (BLOCK // LANES) + part
+        chips = slice(4 * (at % 4), 4 * (at % 4) + 4)
+        pay[at // 4, chips, 0:16, :] = turned[:, cols(part)].reshape(4, 16, LANES)
+
+
+def coefficients_of(full, at):
+    chips = slice(4 * (at % 4), 4 * (at % 4) + 4)
+    return full[at // 4, chips, 0:16, :].reshape(K, LANES)
+
+
+def spread_coefficients(full, spread):
+    for block in range(NBLOCK):
+        for part in range(BLOCK // LANES):
+            high, low = parts(coefficients_of(full, block * (BLOCK // LANES) + part))
+            spread[block, 0:K, cols(part)] = high
+            spread[block, K : 2 * K, cols(part)] = low
 
 
 def begin_kernel(
@@ -255,8 +255,7 @@
                 held[block, 0, span, cols(a)] = high
                 held[block, 1, span, cols(a)] = low
             leave(piece).start()
-        both = dot_nt(held[block].reshape(2 * BLOCK, PTS), split[...])
-        put_coefficients(pay, block, both[0:BLOCK] + both[BLOCK : 2 * BLOCK])
+        put_coefficients(pay, block, held, split)
     hand_out(pay, mine, other)
     for piece in range(2 * NBLOCK):
         leave(piece).wait()
@@ -281,7 +280,10 @@
         begin_kernel,
         in_specs=[HB, VM, VM],
         out_specs=[HB, *[VM] * 5],
-        out_shape=[jax.ShapeDtypeStruct((NBLOCK, 2, BLOCK, PTS), BF16), *shared_outputs(DEPTH)],
+        out_shape=[
+            jax.ShapeDtypeStruct((2 * NBLOCK, 2, BLOCK, PTS), BF16),
+            *shared_outputs(DEPTH),
+        ],
         scratch_shapes=[
             pltpu.VMEM((NSNAP * ROWS, LANES), F32),
             pltpu.VMEM((NBLOCK, 2, BLOCK, PTS), BF16),
@@ -317,33 +319,33 @@
             total[:, at] = piece if block == 0 else total[:, at] + piece
 
 
-def project(held, split, pay, arrive=None):
+def project(held, split, pay):
     for block in range(NBLOCK):
-        if arrive is not None:
-            arrive(block)
-        both = dot_nt(held[block].reshape(2 * BLOCK, PTS), split[...])
-        put_coefficients(pay, block, both[0:BLOCK] + both[BLOCK : 2 * BLOCK])
-
-
-def applied_field(total, prev, sides, sea, pen, out):
-    north, south, west, east = sides
-    for a in range(ROWS):
-        lap = smooth(prev, a, north, south, west, east)
+        put_coefficients(pay, block, held, split)
+
+
+def rough_field(prev, sides, pen, out):
+    for a in range(ROWS):
+        out[:, cols(a)] = pen[a : a + 1, :] * smooth(prev, a, *sides)
+
+
+def applied_field(total, rough, sea, out):
+    for a in range(ROWS):
         mask = sea[a : a + 1, :].astype(F32)
-        out[:, cols(a)] = mask * (total[:, cols(a)] * (1.0 / NPTS) + pen[a : a + 1, :] * lap)
+        out[:, cols(a)] = mask * (total[:, cols(a)] * (1.0 / NPTS) + rough[:, cols(a)])
 
 
 def first_kernel(
     got_mine, got_other, snap, prev, pair, near, around, sea, pen,
     field, mine, other, cross, columns,
-    full, held, spread, total, split, pay, sems,
+    full, spread, total, rough, held, split, pay, sems,
 ):
     begin_copies(snap, held, sems)
     take_in(got_mine, got_other, full)
-    coefficients_of(full, spread)
-    sides = take_in_edges(pair, near, around)
+    spread_coefficients(full, spread)
+    rough_field(prev, take_in_edges(pair, near, around), pen, rough)
     expand(spread, snap, held, sems, total)
-    applied_field(total, prev, sides, sea, pen, field)
+    applied_field(total, rough, sea, field)
     for a in range(ROWS):
         store_split(split, a, field[:, cols(a)])
     hand_out_edges(field, SHARD, other, cross, columns)
@@ -356,8 +358,8 @@
 def scratch_for_expand(depth):
     return [
         pltpu.VMEM((2, 16, depth, LANES), F32),
-        pltpu.VMEM((NBLOCK, 2, BLOCK, PTS), BF16),
         pltpu.VMEM((NBLOCK, 2 * K, BLOCK), BF16),
+        pltpu.VMEM((K, PTS), F32),
         pltpu.VMEM((K, PTS), F32),
     ]
 
@@ -370,6 +372,7 @@
         out_shape=shared_outputs(SHARD),
         scratch_shapes=[
             *scratch_for_expand(DEPTH),
+            pltpu.VMEM((NBLOCK, 2, BLOCK, PTS), BF16),
             pltpu.VMEM((2 * K, PTS), BF16),
             pltpu.VMEM((2, 16, SHARD, LANES), F32),
             pltpu.SemaphoreType.DMA((NBLOCK,)),
@@ -381,16 +384,16 @@
 
 def second_kernel(
     got_mine, got_other, snap, prev, pair, near, around, sea, pen,
-    field, bottom, last,
-    full, held, spread, total, raw, sems,
+    field, bottom, last, held,
+    full, spread, total, rough, raw, sems,
 ):
     begin_copies(snap, held, sems)
     take_in(got_mine, got_other, full)
-    coefficients_of(full, spread)
+    spread_coefficients(full, spread)
     inverse = inverse_factor(square_of(full, 16))
-    sides = take_in_edges(pair, near, around)
+    rough_field(prev, take_in_edges(pair, near, around), pen, rough)
     expand(spread, snap, held, sems, total)
-    applied_field(total, prev, sides, sea, pen, raw)
+    applied_field(total, rough, sea, raw)
     field[...] = dot_nn(inverse, raw[...], HIGHEST)
     bottom[0:K, :] = field[:, cols(ROWS - 1)]
     bottom[K : 2 * K, :] = field[:, cols(ROWS - 1)] * pen[ROWS - 1 : ROWS, :]
@@ -405,41 +408,41 @@
     return pl.pallas_call(
         second_kernel,
         in_specs=[VM, VM, HB, *[VM] * 6],
-        out_specs=[VM] * 3,
-        out_shape=[jax.ShapeDtypeStruct((K, PTS), F32), halo, halo],
+        out_specs=[VM] * 4,
+        out_shape=[
+            jax.ShapeDtypeStruct((K, PTS), F32),
+            halo,
+            halo,
+            jax.ShapeDtypeStruct((NBLOCK, 2, BLOCK, PTS), BF16),
+        ],
         scratch_shapes=[
             *scratch_for_expand(SHARD),
             pltpu.VMEM((K, PTS), F32),
             pltpu.SemaphoreType.DMA((NBLOCK,)),
         ],
-        compiler_params=pltpu.CompilerParams(vmem_limit_bytes=VMEM_LIMIT),
+        compiler_params=pltpu.CompilerParams(vmem_limit_bytes=MIDDLE_LIMIT),
         name="factor_and_expand",
     )(*got, snap, prev, *sides, sea, pen)
 
 
-def project_kernel(snap, field, pay, held, split, sems):
-    begin_copies(snap, held, sems)
+def project_kernel(held, field, pay, split):
     for a in range(ROWS):
         store_split(split, a, field[:, cols(a)])
     pay[...] = jnp.zeros_like(pay)
     put_square(pay, 16, folded(dot_nt(split[...], split[...])))
-    project(held, split, pay, lambda block: copy_of(snap, held, sems, block).wait())
-
-
-def project_step(snap, field):
+    project(held, split, pay)
+
+
+def project_step(held, field):
     return pl.pallas_call(
         project_kernel,
-        in_specs=[HB, VM],
+        in_specs=[VM, VM],
         out_specs=VM,
         out_shape=jax.ShapeDtypeStruct((2, 16, SHARD, LANES), F32),
-        scratch_shapes=[
-            pltpu.VMEM((NBLOCK, 2, BLOCK, PTS), BF16),
-            pltpu.VMEM((2 * K, PTS), BF16),
-            pltpu.SemaphoreType.DMA((NBLOCK,)),
-        ],
-        compiler_params=pltpu.CompilerParams(vmem_limit_bytes=VMEM_LIMIT),
+        scratch_shapes=[pltpu.VMEM((2 * K, PTS), BF16)],
+        compiler_params=pltpu.CompilerParams(vmem_limit_bytes=MIDDLE_LIMIT),
         name="project",
-    )(snap, field)
+    )(held, field)
 
 
 def rough_kernel(field, north, west, pen, base, mine, other, left, right, pay):
@@ -495,10 +498,9 @@
     solved = dot_nn(inverse, field[...], HIGHEST)
     for a in range(ROWS):
         basis[pl.ds(a, K, stride=ROWS), :] = solved[:, cols(a)]
-    turned = coefficients_of(full, None)
+    turned = jnp.concatenate([coefficients_of(full, at) for at in range(NSNAP // LANES)], axis=1)
     rough = square_of(full, 17)[:, 0:K]
-    low, high = turned[0:K], turned[K : 2 * K]
-    gram = dot_nt(low, low, HIGHEST) + dot_nt(high, high, HIGHEST)
+    gram = dot_nt(turned, turned, HIGHEST)
     middle = (gram * (1.0 / NPTS) + rough) * (1.0 / NPTS)
     matrix[...] = dot_nt(dot_nn(inverse, middle, HIGHEST), inverse, HIGHEST)
 
@@ -558,10 +560,10 @@
     got, sides = summed_everywhere(mine, other, edges)
     applied, mine, other, *edges = first_step(got, snap, start, sides, land_sea, penalty)
     got, sides = summed_everywhere(mine, other, edges)
-    applied, bottom, last = second_step(got, snap, applied, sides, land_sea, penalty)
+    applied, bottom, last, held = second_step(got, snap, applied, sides, land_sea, penalty)
     north = from_below(bottom, LAT, 32)
     west = from_below(last, "z", 8)
-    base = project_step(snap, applied)
+    base = project_step(held, applied)
     mine, other = rough_step(applied, north, west, penalty, base)
     got, _ = summed_everywhere(mine, other)
     return last_step(got, applied)

time: 172 us -> 169 us (0.983)
  Pallas kernels: 33.6 us -> 30.9 us
    pallas_call x1, Pallas kernels: 6.68 us -> 2.99 us  [project_step(): pl.pallas_call(project_kernel, in_specs=[VM, VM], out_specs=VM, out_shape...]
  transfers between devices with their start and end apart: 12 -> 12, of which waited for: 10 -> 10; matrix products, arithmetic and copies ran while one was open for 0% -> 0% of each run, Pallas kernels for 4% -> 2%
where the time goes in v3:
time: 169 us; the launch traced here: 168 us
  blocking collectives  87.4 us (52%)
  starting transfers between devices  32.5 us (19%)
  Pallas kernels  30.9 us (18%)
  waiting for transfers between devices  13.3 us (8%)
  local copies, waits for them, and re-layouts  1.84 us (1%)
    all_to_all x7, blocking collectives, exchange(): return lax.all_to_all(value, axis, 0, 0, tiled=True)  87.4 us
    pallas_call x1, Pallas kernels, begin(): pl.pallas_call(begin_kernel, in_specs=[HB, VM, VM], out_specs=[HB, *[VM]...  9.3 us
    all_to_all x2, starting transfers between devices, exchange(): return lax.all_to_all(value, axis, 0, 0, tiled=True)  8.54 us
    ppermute x2, starting transfers between devices, summed_everywhere(): near = lax.ppermute(cross, LAT, CROSS)  7.74 us
    pallas_call x1, Pallas kernels, first_step(): pl.pallas_call(first_kernel, in_specs=[VM, VM, HB, *[VM] * 6], out_specs=...  7.46 us
    ppermute x3, starting transfers between devices, summed_everywhere(): both = (half, lax.ppermute(half, 'core', SWAP))  7.24 us
    pallas_call x1, Pallas kernels, second_step(): pl.pallas_call(second_kernel, in_specs=[VM, VM, HB, *[VM] * 6], out_specs...  6.56 us
    ppermute x2, starting transfers between devices, from_below(): return lax.ppermute(value, axis, [(i, i + 1) for i in range(count - 1)])  4.65 us
  transfers between devices with their start and end apart: 12, of which 10 were waited for; matrix products, arithmetic and copies ran while one was open for 0% of the time, Pallas kernels for 2%

profile of v3, /device:TPU:1, one launch (start us, length us, event | category | flops | bytes accessed | tf_op | source)
XLA Modules:
  0.0 168.2 jit_solution(12144758912658001536)
XLA Ops:
  0.6 1.0 copy-done
  2.4 9.3 %split_and_project.1 = (bf16[8,2,256,2048]{3,2,1,0:T(8,128)(2,1)}, f32[64,2048]{1,0:T(8,128)S(1)}, f32[16,16,128]{2,1,0:T(8,128)S(1)}, f32[320,128]{1,0:T(8,128)...) custom-call(f32[16384,128]{1,0:T(8,128)} %bitcast.7, f32[1024,128]{1,0:T(8,128)S(1)} %bitcast.6, s32[16,128]{1,0:T(8,128)S(1)} %copy-done.1), custom_call_target="tpu_custom_call" | custom-call | tf_op jit(solution)/shard_map/split_and_project/pallas_call | solution.py:279
  11.7 3.3 %collective-permute-start = (f32[320,128]{1,0:T(8,128)S(1)}, f32[320,128]{1,0:T(8,128)S(1)}, u32[]{:S(2)}, u32[]{:S(2)}) collective-permute-start(f32[320,128]{1,0:T(8,128)S(1)} %get-tuple-element.30), channel_id=1, source_target_pairs={{0,8},{8,0},{1,9},{9,1},{2,10},{10,2},{3,11},{11,3},{4,12},{12,4},... | collective-permute-start | bytes 491528 | tf_op jit(solution)/shard_map/ppermute | solution.py:534
  15.0 1.0 collective-permute-done
  16.7 5.0 %all-to-all-start = ((f32[16,16,128]{2,1,0:T(8,128)}), f32[16,16,128]{2,1,0:T(8,128)S(1)}, u32[]{:S(2)}, u32[]{:S(2)}) async-start(f32[16,16,128]{2,1,0:T(8,128)} %add.9), calls=%async_computation | async-start | bytes 262144 | tf_op jit(solution)/shard_map/all_to_all | solution.py:525
  21.8 4.1 %collective-permute-start.1 = (f32[64,128]{1,0:T(8,128)S(1)}, f32[64,128]{1,0:T(8,128)S(1)}, u32[]{:S(2)}, u32[]{:S(2)}) collective-permute-start(f32[64,128]{1,0:T(8,128)S(1)} %get-tuple-element.33), channel_id=1, source_target_pairs={{8,16},{16,8},{24,32},{32,24},{40,48},{48,40},{56,64},{64,56},{72,... | collective-permute-start | bytes 98312 | tf_op jit(solution)/shard_map/ppermute | solution.py:539
  25.8 1.9 %collective-permute-done.1.near = f32[64,128]{1,0:T(8,128)S(1)} collective-permute-done((f32[64,128]{1,0:T(8,128)S(1)}, f32[64,128]{1,0:T(8,128)S(1)}, u32[]{:S(2)}, u32[]{:S(2)}) %collective-permute-start.1) | collective-permute-done | bytes 32800 | tf_op jit(solution)/shard_map/ppermute | solution.py:539
  28.7 16.0 %all_to_all.45.around = f32[8,32,128]{2,1,0:T(8,128)S(1)} all-to-all(f32[8,32,128]{2,1,0:T(8,128)S(1)} %broadcast_in_dim.12), channel_id=1, replica_groups=mesh['y'=4,'x'=4,'core'=2,'z'=8] {'z'}, dimensions={0} | all-to-all | bytes 262144 | tf_op jit(solution)/shard_map/all_to_all | solution.py:525
  44.7 14.4 %all_to_all.46.got_mine = f32[16,16,128]{2,1,0:T(8,128)S(1)} all-to-all(f32[16,16,128]{2,1,0:T(8,128)S(1)} %broadcast_in_dim.13), channel_id=1, replica_groups=mesh['y'=4,'x'=4,'core'=2,'z'=8] {'y','x'}, dimensions={0} | all-to-all | bytes 262144 | tf_op jit(solution)/shard_map/all_to_all | solution.py:525
  59.1 1.8 %collective-permute-start.2 = (f32[16,16,128]{2,1,0:T(8,128)S(1)}, f32[16,16,128]{2,1,0:T(8,128)S(1)}, u32[]{:S(2)}, u32[]{:S(2)}) collective-permute-start(f32[16,16,128]{2,1,0:T(8,128)S(1)} %all_to_all.46.got_mine), channel_id=1, source_target_pairs={{0,8},{8,0},{1,9},{9,1},{2,10},{10,2},{3,11},{11,3},{4,12},{12,4},... | collective-permute-start | bytes 393224 | tf_op jit(solution)/shard_map/ppermute | solution.py:548
  60.9 1.0 collective-permute-done.2.got_other
  61.8 7.5 %expand_and_project.1 = (f32[64,2048]{1,0:T(8,128)S(1)}, f32[16,24,128]{2,1,0:T(8,128)S(1)}, f32[448,128]{1,0:T(8,128)S(1)}, f32[64,128]{1,0:T(8,128)S(1)}, f32[16,128]{1,0:T(8,128)S(1)}) custom-call(f32[16,16,128]{2,1,0:T(8,128)S(1)} %all_to_all.46.got_mine, f32[16,16,128]{2,1,0:T(8,128)S(1)} %collective-permute-done.2.got_other, ...), custom_call_target="tpu_custom_call" | custom-call | tf_op jit(solution)/shard_map/expand_and_project/pallas_call | solution.py:368
  69.9 1.1 collective-permute-done.3
  71.8 3.5 %all-to-all-start.3 = ((f32[16,24,128]{2,1,0:T(8,128)}), f32[16,24,128]{2,1,0:T(8,128)S(1)}, u32[]{:S(2)}, u32[]{:S(2)}) async-start(f32[16,24,128]{2,1,0:T(8,128)} %add.10), calls=%async_computation.3 | async-start | bytes 393216 | tf_op jit(solution)/shard_map/all_to_all | solution.py:525
  75.3 3.7 %collective-permute-start.4 = (f32[64,128]{1,0:T(8,128)S(1)}, f32[64,128]{1,0:T(8,128)S(1)}, u32[]{:S(2)}, u32[]{:S(2)}) collective-permute-start(f32[64,128]{1,0:T(8,128)S(1)} %get-tuple-element.43), channel_id=1, source_target_pairs={{8,16},{16,8},{24,32},{32,24},{40,48},{48,40},{56,64},{64,56},{72,... | collective-permute-start | bytes 98312 | tf_op jit(solution)/shard_map/ppermute | solution.py:539
  79.0 1.9 %collective-permute-done.4.near = f32[64,128]{1,0:T(8,128)S(1)} collective-permute-done((f32[64,128]{1,0:T(8,128)S(1)}, f32[64,128]{1,0:T(8,128)S(1)}, u32[]{:S(2)}, u32[]{:S(2)}) %collective-permute-start.4) | collective-permute-done | bytes 32800 | tf_op jit(solution)/shard_map/ppermute | solution.py:539
  80.9 2.1 %all-to-all-done.3 = f32[16,24,128]{2,1,0:T(8,128)S(1)} async-done(((f32[16,24,128]{2,1,0:T(8,128)}), f32[16,24,128]{2,1,0:T(8,128)S(1)}, u32[]{:S(2)}, u32[]{:S(2)}) %all-to-all-start.3) | async-done | bytes 196640 | tf_op jit(solution)/shard_map/all_to_all | solution.py:525
  83.1 10.5 %all_to_all.47.around = f32[8,40,128]{2,1,0:T(8,128)S(1)} all-to-all(f32[8,40,128]{2,1,0:T(8,128)S(1)} %broadcast_in_dim.14), channel_id=1, replica_groups=mesh['y'=4,'x'=4,'core'=2,'z'=8] {'z'}, dimensions={0} | all-to-all | bytes 327680 | tf_op jit(solution)/shard_map/all_to_all | solution.py:525
  93.6 14.4 %all_to_all.48.got_mine = f32[16,24,128]{2,1,0:T(8,128)S(1)} all-to-all(f32[16,24,128]{2,1,0:T(8,128)S(1)} %broadcast_in_dim.15), channel_id=1, replica_groups=mesh['y'=4,'x'=4,'core'=2,'z'=8] {'y','x'}, dimensions={0} | all-to-all | bytes 393216 | tf_op jit(solution)/shard_map/all_to_all | solution.py:525
  108.0 1.2 collective-permute-start.5
  109.2 1.1 collective-permute-done.5.got_other
  110.3 6.6 %factor_and_expand.1 = (f32[64,2048]{1,0:T(8,128)S(1)}, f32[128,128]{1,0:T(8,128)S(1)}, f32[128,128]{1,0:T(8,128)S(1)}, bf16[4,2,256,2048]{3,2,1,0:T(8,128)(2,1)S(1)}) custom-call(f32[16,24,128]{2,1,0:T(8,128)S(1)} %all_to_all.48.got_mine, f32[16,24,128]{2,1,0:T(8,128)S(1)} %collective-permute-done.5.got_other, ...), custom_call_target="tpu_custom_call" | custom-call | tf_op jit(solution)/shard_map/factor_and_expand/pallas_call | solution.py:408
  116.8 2.5 %collective-permute-start.6 = (f32[128,128]{1,0:T(8,128)S(1)}, f32[128,128]{1,0:T(8,128)S(1)}, u32[]{:S(2)}, u32[]{:S(2)}) collective-permute-start(f32[128,128]{1,0:T(8,128)S(1)} %get-tuple-element.49), channel_id=1, source_target_pairs={{0,8},{8,16},{16,24},{24,32},{32,40},{40,48},{48,56},{56,64},{64,7... | collective-permute-start | bytes 196616 | tf_op jit(solution)/shard_map/ppermute | solution.py:555
  119.3 2.2 %collective-permute-start.7 = (f32[128,128]{1,0:T(8,128)S(1)}, f32[128,128]{1,0:T(8,128)S(1)}, u32[]{:S(2)}, u32[]{:S(2)}) collective-permute-start(f32[128,128]{1,0:T(8,128)S(1)} %get-tuple-element.50), channel_id=1, source_target_pairs={{0,1},{1,2},{2,3},{3,4},{4,5},{5,6},{6,7},{8,9},{9,10},{10,11},{11... | collective-permute-start | bytes 196616 | tf_op jit(solution)/shard_map/ppermute | solution.py:555
  121.5 3.0 %project.1.base = f32[2,16,24,128]{3,2,1,0:T(8,128)S(1)} custom-call(bf16[4,2,256,2048]{3,2,1,0:T(8,128)(2,1)S(1)} %get-tuple-element.51.held, f32[64,2048]{1,0:T(8,128)S(1)} %get-tuple-element.48.field), custom_call_target="tpu_custom_call" | custom-call | tf_op jit(solution)/shard_map/project/pallas_call | solution.py:437
  125.7 1.2 collective-permute-done.8
  127.0 12.4 %all_to_all.49 = f32[16,24,128]{2,1,0:T(8,128)S(1)} all-to-all(f32[16,24,128]{2,1,0:T(8,128)S(1)} %add.11), channel_id=1, replica_groups=mesh['y'=4,'x'=4,'core'=2,'z'=8] {'y','x'}, dimensions={0} | all-to-all | bytes 393216 | tf_op jit(solution)/shard_map/all_to_all | solution.py:525
  139.4 10.0 %all_to_all.50 = f32[8,24,128]{2,1,0:T(8,128)S(1)} all-to-all(f32[8,24,128]{2,1,0:T(8,128)S(1)} %broadcast_in_dim.16), channel_id=1, replica_groups=mesh['y'=4,'x'=4,'core'=2,'z'=8] {'z'}, dimensions={0} | all-to-all | bytes 196608 | tf_op jit(solution)/shard_map/all_to_all | solution.py:525
  149.4 9.8 %all_to_all.51.got_mine = f32[16,24,128]{2,1,0:T(8,128)S(1)} all-to-all(f32[16,24,128]{2,1,0:T(8,128)S(1)} %broadcast_in_dim.17), channel_id=1, replica_groups=mesh['y'=4,'x'=4,'core'=2,'z'=8] {'y','x'}, dimensions={0} | all-to-all | bytes 393216 | tf_op jit(solution)/shard_map/all_to_all | solution.py:525
  159.2 4.2 %collective-permute-start.9 = (f32[16,24,128]{2,1,0:T(8,128)S(1)}, f32[16,24,128]{2,1,0:T(8,128)S(1)}, u32[]{:S(2)}, u32[]{:S(2)}) collective-permute-start(f32[16,24,128]{2,1,0:T(8,128)S(1)} %all_to_all.51.got_mine), channel_id=1, source_target_pairs={{0,8},{8,0},{1,9},{9,1},{2,10},{10,2},{3,11},{11,3},{4,12},{12,4},... | collective-permute-start | bytes 589832 | tf_op jit(solution)/shard_map/ppermute | solution.py:548
  163.4 1.1 collective-permute-done.9.got_other
  164.5 3.7 %factor_and_finish.1 = (f32[1024,128]{1,0:T(8,128)}, f32[64,64]{1,0:T(8,128)}) custom-call(f32[16,24,128]{2,1,0:T(8,128)S(1)} %all_to_all.51.got_mine, f32[16,24,128]{2,1,0:T(8,128)S(1)} %collective-permute-done.9.got_other, f32[64,2048]{1,0:T(8,128)S(1)} %get-tuple-element.48.field), custom_call_target="tpu_custom_call" | custom-call | tf_op jit(solution)/shard_map/factor_and_finish/pallas_call | solution.py:509
  (34 shorter events, 5.0 us)
Async XLA Ops:
  0.6 1.0 copy-start
  1.7 0.7 copy-start.1
  2.4 59.5 %copy-start.2 = (s32[16,128]{1,0:T(8,128)S(1)}, s32[16,128]{1,0:T(8,128)}, u32[]{:S(2)}) copy-start(s32[16,128]{1,0:T(8,128)} %sea.5) | copy-start | bytes 24580
  2.4 59.5 %copy-start.3 = (f32[16,128]{1,0:T(8,128)S(1)}, f32[16,128]{1,0:T(8,128)}, u32[]{:S(2)}) copy-start(f32[16,128]{1,0:T(8,128)} %pen.5) | copy-start | bytes 24580
  11.7 4.4 %collective-permute-start = (f32[320,128]{1,0:T(8,128)S(1)}, f32[320,128]{1,0:T(8,128)S(1)}, u32[]{:S(2)}, u32[]{:S(2)}) collective-permute-start(f32[320,128]{1,0:T(8,128)S(1)} %get-tuple-element.30), channel_id=1, source_target_pairs={{0,8},{8,0},{1,9},{9,1},{2,10},{10,2},{3,11},{11,3},{4,12},{12,4},... | collective-permute-start | bytes 491528 | tf_op jit(solution)/shard_map/ppermute | solution.py:534
  16.7 11.9 %all-to-all-start = ((f32[16,16,128]{2,1,0:T(8,128)}), f32[16,16,128]{2,1,0:T(8,128)S(1)}, u32[]{:S(2)}, u32[]{:S(2)}) async-start(f32[16,16,128]{2,1,0:T(8,128)} %add.9), calls=%async_computation | async-start | bytes 262144 | tf_op jit(solution)/shard_map/all_to_all | solution.py:525
  21.8 6.0 %collective-permute-start.1 = (f32[64,128]{1,0:T(8,128)S(1)}, f32[64,128]{1,0:T(8,128)S(1)}, u32[]{:S(2)}, u32[]{:S(2)}) collective-permute-start(f32[64,128]{1,0:T(8,128)S(1)} %get-tuple-element.33), channel_id=1, source_target_pairs={{8,16},{16,8},{24,32},{32,24},{40,48},{48,40},{56,64},{64,56},{72,... | collective-permute-start | bytes 98312 | tf_op jit(solution)/shard_map/ppermute | solution.py:539
  59.1 2.8 %collective-permute-start.2 = (f32[16,16,128]{2,1,0:T(8,128)S(1)}, f32[16,16,128]{2,1,0:T(8,128)S(1)}, u32[]{:S(2)}, u32[]{:S(2)}) collective-permute-start(f32[16,16,128]{2,1,0:T(8,128)S(1)} %all_to_all.46.got_mine), channel_id=1, source_target_pairs={{0,8},{8,0},{1,9},{9,1},{2,10},{10,2},{3,11},{11,3},{4,12},{12,4},... | collective-permute-start | bytes 393224 | tf_op jit(solution)/shard_map/ppermute | solution.py:548
  69.3 1.8 %collective-permute-start.3 = (f32[448,128]{1,0:T(8,128)S(1)}, f32[448,128]{1,0:T(8,128)S(1)}, u32[]{:S(2)}, u32[]{:S(2)}) collective-permute-start(f32[448,128]{1,0:T(8,128)S(1)} %get-tuple-element.40), channel_id=1, source_target_pairs={{0,8},{8,0},{1,9},{9,1},{2,10},{10,2},{3,11},{11,3},{4,12},{12,4},... | collective-permute-start | bytes 688136 | tf_op jit(solution)/shard_map/ppermute | solution.py:534
  71.8 11.2 %all-to-all-start.3 = ((f32[16,24,128]{2,1,0:T(8,128)}), f32[16,24,128]{2,1,0:T(8,128)S(1)}, u32[]{:S(2)}, u32[]{:S(2)}) async-start(f32[16,24,128]{2,1,0:T(8,128)} %add.10), calls=%async_computation.3 | async-start | bytes 393216 | tf_op jit(solution)/shard_map/all_to_all | solution.py:525
  75.3 5.6 %collective-permute-start.4 = (f32[64,128]{1,0:T(8,128)S(1)}, f32[64,128]{1,0:T(8,128)S(1)}, u32[]{:S(2)}, u32[]{:S(2)}) collective-permute-start(f32[64,128]{1,0:T(8,128)S(1)} %get-tuple-element.43), channel_id=1, source_target_pairs={{8,16},{16,8},{24,32},{32,24},{40,48},{48,40},{56,64},{64,56},{72,... | collective-permute-start | bytes 98312 | tf_op jit(solution)/shard_map/ppermute | solution.py:539
  108.0 2.3 %collective-permute-start.5 = (f32[16,24,128]{2,1,0:T(8,128)S(1)}, f32[16,24,128]{2,1,0:T(8,128)S(1)}, u32[]{:S(2)}, u32[]{:S(2)}) collective-permute-start(f32[16,24,128]{2,1,0:T(8,128)S(1)} %all_to_all.48.got_mine), channel_id=1, source_target_pairs={{0,8},{8,0},{1,9},{9,1},{2,10},{10,2},{3,11},{11,3},{4,12},{12,4},... | collective-permute-start | bytes 589832 | tf_op jit(solution)/shard_map/ppermute | solution.py:548
  116.8 7.7 %collective-permute-start.6 = (f32[128,128]{1,0:T(8,128)S(1)}, f32[128,128]{1,0:T(8,128)S(1)}, u32[]{:S(2)}, u32[]{:S(2)}) collective-permute-start(f32[128,128]{1,0:T(8,128)S(1)} %get-tuple-element.49), channel_id=1, source_target_pairs={{0,8},{8,16},{16,24},{24,32},{32,40},{40,48},{48,56},{56,64},{64,7... | collective-permute-start | bytes 196616 | tf_op jit(solution)/shard_map/ppermute | solution.py:555
  119.3 5.2 %collective-permute-start.7 = (f32[128,128]{1,0:T(8,128)S(1)}, f32[128,128]{1,0:T(8,128)S(1)}, u32[]{:S(2)}, u32[]{:S(2)}) collective-permute-start(f32[128,128]{1,0:T(8,128)S(1)} %get-tuple-element.50), channel_id=1, source_target_pairs={{0,1},{1,2},{2,3},{3,4},{4,5},{5,6},{6,7},{8,9},{9,10},{10,11},{11... | collective-permute-start | bytes 196616 | tf_op jit(solution)/shard_map/ppermute | solution.py:555
  125.4 1.5 collective-permute-start.8
  159.2 5.3 %collective-permute-start.9 = (f32[16,24,128]{2,1,0:T(8,128)S(1)}, f32[16,24,128]{2,1,0:T(8,128)S(1)}, u32[]{:S(2)}, u32[]{:S(2)}) collective-permute-start(f32[16,24,128]{2,1,0:T(8,128)S(1)} %all_to_all.51.got_mine), channel_id=1, source_target_pairs={{0,8},{8,0},{1,9},{9,1},{2,10},{10,2},{3,11},{11,3},{4,12},{12,4},... | collective-permute-start | bytes 589832 | tf_op jit(solution)/shard_map/ppermute | solution.py:548

commit v4 on v3

--- a/solution.py
+++ b/solution.py
@@ -23,6 +23,7 @@
 SWAP = [(0, 1), (1, 0)]
 CROSS = [pair for i in range(1, 31, 2) for pair in ((i, i + 1), (i + 1, i))]
 VMEM_LIMIT = 50 * 1024 * 1024
+FIRST_LIMIT = 53 * 1024 * 1024
 MIDDLE_LIMIT = 36 * 1024 * 1024
 SMALL_LIMIT = 20 * 1024 * 1024
 
@@ -203,9 +204,9 @@
 
 
 def put_coefficients(pay, block, held, split):
-    both = dot_nt(split[...], held[block].reshape(2 * BLOCK, PTS))
-    rows = both[0:K] + both[K : 2 * K]
-    turned = rows[:, 0:BLOCK] + rows[:, BLOCK : 2 * BLOCK]
+    both = dot_nt(held[block].reshape(2 * BLOCK, PTS), split[...])
+    turned = (both[0:BLOCK] + both[BLOCK : 2 * BLOCK]).T
+    turned = turned[0:K] + turned[K : 2 * K]
     for part in range(BLOCK // LANES):
         at = block * (BLOCK // LANES) + part
         chips = slice(4 * (at % 4), 4 * (at % 4) + 4)
@@ -226,9 +227,15 @@
 
 
 def begin_kernel(
-    snap, basis, sea, snap_out, flat, mine, other, cross, columns,
-    raw, held, split, pay, in_sems, out_sems,
+    snap, basis_in, sea_in, snap_out, flat, mine, other, cross, columns,
+    raw, held, split, pay, basis, sea, in_sems, out_sems, own_sems,
 ):
+    own = [
+        pltpu.make_async_copy(basis_in, basis, own_sems.at[0]),
+        pltpu.make_async_copy(sea_in, sea, own_sems.at[1]),
+    ]
+    for copy in own:
+        copy.start()
     deep = BLOCK // 2
 
     def arrive(piece):
@@ -241,6 +248,8 @@
 
     for piece in range(2 * NBLOCK):
         arrive(piece).start()
+    for copy in own:
+        copy.wait()
     for a in range(ROWS):
         value = basis[pl.ds(a, K, stride=ROWS), :] * sea[a : a + 1, :].astype(F32)
         flat[:, cols(a)] = value
@@ -255,7 +264,7 @@
                 held[block, 0, span, cols(a)] = high
                 held[block, 1, span, cols(a)] = low
             leave(piece).start()
-        put_coefficients(pay, block, held, split)
+    project(held, split, pay)
     hand_out(pay, mine, other)
     for piece in range(2 * NBLOCK):
         leave(piece).wait()
@@ -263,6 +272,7 @@
 
 VM = pl.BlockSpec(memory_space=pltpu.VMEM)
 HB = pl.BlockSpec(memory_space=pl.ANY)
+HBM = pl.BlockSpec(memory_space=pltpu.HBM)
 
 
 def shared_outputs(depth):
@@ -278,7 +288,7 @@
 def begin(snapshots, basis, sea):
     return pl.pallas_call(
         begin_kernel,
-        in_specs=[HB, VM, VM],
+        in_specs=[HBM, HBM, HBM],
         out_specs=[HB, *[VM] * 5],
         out_shape=[
             jax.ShapeDtypeStruct((2 * NBLOCK, 2, BLOCK, PTS), BF16),
@@ -289,10 +299,13 @@
             pltpu.VMEM((NBLOCK, 2, BLOCK, PTS), BF16),
             pltpu.VMEM((2 * K, PTS), BF16),
             pltpu.VMEM((2, 16, DEPTH, LANES), F32),
+            pltpu.VMEM((K * ROWS, LANES), F32),
+            pltpu.VMEM((ROWS, LANES), jnp.int32),
             pltpu.SemaphoreType.DMA((2 * NBLOCK,)),
             pltpu.SemaphoreType.DMA((2 * NBLOCK,)),
-        ],
-        compiler_params=pltpu.CompilerParams(vmem_limit_bytes=VMEM_LIMIT),
+            pltpu.SemaphoreType.DMA((2,)),
+        ],
+        compiler_params=pltpu.CompilerParams(vmem_limit_bytes=FIRST_LIMIT),
         name="split_and_project",
     )(snapshots.reshape(NSNAP * ROWS, LANES), basis.reshape(K * ROWS, LANES), sea)
 

time: 169 us -> 166 us (0.982)
  Pallas kernels: 30.9 us -> 29.1 us
where the time goes in v4:
time: 166 us
  blocking collectives  87.8 us (53%)
  starting transfers between devices  32.5 us (20%)
  Pallas kernels  29.1 us (18%)
  waiting for transfers between devices  13.3 us (8%)
    all_to_all x7, blocking collectives, exchange(): return lax.all_to_all(value, axis, 0, 0, tiled=True)  87.8 us
    all_to_all x2, starting transfers between devices, exchange(): return lax.all_to_all(value, axis, 0, 0, tiled=True)  8.73 us
    pallas_call x1, Pallas kernels, begin(): pl.pallas_call(begin_kernel, in_specs=[HBM, HBM, HBM], out_specs=[HB, *[V...  8.39 us
    ppermute x2, starting transfers between devices, summed_everywhere(): near = lax.ppermute(cross, LAT, CROSS)  7.74 us
    ppermute x3, starting transfers between devices, summed_everywhere(): both = (half, lax.ppermute(half, 'core', SWAP))  7.27 us
    pallas_call x1, Pallas kernels, first_step(): pl.pallas_call(first_kernel, in_specs=[VM, VM, HB, *[VM] * 6], out_specs=...  7.01 us
    pallas_call x1, Pallas kernels, second_step(): pl.pallas_call(second_kernel, in_specs=[VM, VM, HB, *[VM] * 6], out_specs...  6.56 us
    ppermute x2, starting transfers between devices, from_below(): return lax.ppermute(value, axis, [(i, i + 1) for i in range(count - 1)])  4.65 us
  transfers between devices with their start and end apart: 12, of which 10 were waited for; matrix products, arithmetic and copies ran while one was open for 0% of the time, Pallas kernels for 2%

profile of v4, /device:TPU:1, one launch (start us, length us, event | category | flops | bytes accessed | tf_op | source)
XLA Modules:
  0.0 165.8 jit_solution(3309027680399804552)
XLA Ops:
  1.3 8.4 %split_and_project.1 = (bf16[8,2,256,2048]{3,2,1,0:T(8,128)(2,1)}, f32[64,2048]{1,0:T(8,128)S(1)}, f32[16,16,128]{2,1,0:T(8,128)S(1)}, f32[320,128]{1,0:T(8,128)...) custom-call(f32[16384,128]{1,0:T(8,128)} %bitcast.6, f32[1024,128]{1,0:T(8,128)} %bitcast.8, s32[16,128]{1,0:T(8,128)S(1)} %copy-done), custom_call_target="tpu_custom_call" | custom-call | tf_op jit(solution)/shard_map/split_and_project/pallas_call | solution.py:289
  9.7 3.3 %collective-permute-start = (f32[320,128]{1,0:T(8,128)S(1)}, f32[320,128]{1,0:T(8,128)S(1)}, u32[]{:S(2)}, u32[]{:S(2)}) collective-permute-start(f32[320,128]{1,0:T(8,128)S(1)} %get-tuple-element.30), channel_id=1, source_target_pairs={{0,8},{8,0},{1,9},{9,1},{2,10},{10,2},{3,11},{11,3},{4,12},{12,4},... | collective-permute-start | bytes 491528 | tf_op jit(solution)/shard_map/ppermute | solution.py:547
  13.1 1.0 collective-permute-done
  14.8 5.0 %all-to-all-start = ((f32[16,16,128]{2,1,0:T(8,128)}), f32[16,16,128]{2,1,0:T(8,128)S(1)}, u32[]{:S(2)}, u32[]{:S(2)}) async-start(f32[16,16,128]{2,1,0:T(8,128)} %add.9), calls=%async_computation | async-start | bytes 262144 | tf_op jit(solution)/shard_map/all_to_all | solution.py:538
  19.8 4.1 %collective-permute-start.1 = (f32[64,128]{1,0:T(8,128)S(1)}, f32[64,128]{1,0:T(8,128)S(1)}, u32[]{:S(2)}, u32[]{:S(2)}) collective-permute-start(f32[64,128]{1,0:T(8,128)S(1)} %get-tuple-element.33), channel_id=1, source_target_pairs={{8,16},{16,8},{24,32},{32,24},{40,48},{48,40},{56,64},{64,56},{72,... | collective-permute-start | bytes 98312 | tf_op jit(solution)/shard_map/ppermute | solution.py:552
  23.9 1.9 %collective-permute-done.1.near = f32[64,128]{1,0:T(8,128)S(1)} collective-permute-done((f32[64,128]{1,0:T(8,128)S(1)}, f32[64,128]{1,0:T(8,128)S(1)}, u32[]{:S(2)}, u32[]{:S(2)}) %collective-permute-start.1) | collective-permute-done | bytes 32800 | tf_op jit(solution)/shard_map/ppermute | solution.py:552
  26.7 16.0 %all_to_all.45.around = f32[8,32,128]{2,1,0:T(8,128)S(1)} all-to-all(f32[8,32,128]{2,1,0:T(8,128)S(1)} %broadcast_in_dim.12), channel_id=1, replica_groups=mesh['y'=4,'x'=4,'core'=2,'z'=8] {'z'}, dimensions={0} | all-to-all | bytes 262144 | tf_op jit(solution)/shard_map/all_to_all | solution.py:538
  42.7 14.4 %all_to_all.46.got_mine = f32[16,16,128]{2,1,0:T(8,128)S(1)} all-to-all(f32[16,16,128]{2,1,0:T(8,128)S(1)} %broadcast_in_dim.13), channel_id=1, replica_groups=mesh['y'=4,'x'=4,'core'=2,'z'=8] {'y','x'}, dimensions={0} | all-to-all | bytes 262144 | tf_op jit(solution)/shard_map/all_to_all | solution.py:538
  57.1 1.8 %collective-permute-start.2 = (f32[16,16,128]{2,1,0:T(8,128)S(1)}, f32[16,16,128]{2,1,0:T(8,128)S(1)}, u32[]{:S(2)}, u32[]{:S(2)}) collective-permute-start(f32[16,16,128]{2,1,0:T(8,128)S(1)} %all_to_all.46.got_mine), channel_id=1, source_target_pairs={{0,8},{8,0},{1,9},{9,1},{2,10},{10,2},{3,11},{11,3},{4,12},{12,4},... | collective-permute-start | bytes 393224 | tf_op jit(solution)/shard_map/ppermute | solution.py:561
  58.9 1.0 collective-permute-done.2.got_other
  59.9 7.0 %expand_and_project.1 = (f32[64,2048]{1,0:T(8,128)S(1)}, f32[16,24,128]{2,1,0:T(8,128)S(1)}, f32[448,128]{1,0:T(8,128)S(1)}, f32[64,128]{1,0:T(8,128)S(1)}, f32[16,128]{1,0:T(8,128)S(1)}) custom-call(f32[16,16,128]{2,1,0:T(8,128)S(1)} %all_to_all.46.got_mine, f32[16,16,128]{2,1,0:T(8,128)S(1)} %collective-permute-done.2.got_other, ...), custom_call_target="tpu_custom_call" | custom-call | tf_op jit(solution)/shard_map/expand_and_project/pallas_call | solution.py:381
  67.4 1.1 collective-permute-done.3
  69.2 3.7 %all-to-all-start.3 = ((f32[16,24,128]{2,1,0:T(8,128)}), f32[16,24,128]{2,1,0:T(8,128)S(1)}, u32[]{:S(2)}, u32[]{:S(2)}) async-start(f32[16,24,128]{2,1,0:T(8,128)} %add.10), calls=%async_computation.3 | async-start | bytes 393216 | tf_op jit(solution)/shard_map/all_to_all | solution.py:538
  72.9 3.7 %collective-permute-start.4 = (f32[64,128]{1,0:T(8,128)S(1)}, f32[64,128]{1,0:T(8,128)S(1)}, u32[]{:S(2)}, u32[]{:S(2)}) collective-permute-start(f32[64,128]{1,0:T(8,128)S(1)} %get-tuple-element.43), channel_id=1, source_target_pairs={{8,16},{16,8},{24,32},{32,24},{40,48},{48,40},{56,64},{64,56},{72,... | collective-permute-start | bytes 98312 | tf_op jit(solution)/shard_map/ppermute | solution.py:552
  76.6 1.9 %collective-permute-done.4.near = f32[64,128]{1,0:T(8,128)S(1)} collective-permute-done((f32[64,128]{1,0:T(8,128)S(1)}, f32[64,128]{1,0:T(8,128)S(1)}, u32[]{:S(2)}, u32[]{:S(2)}) %collective-permute-start.4) | collective-permute-done | bytes 32800 | tf_op jit(solution)/shard_map/ppermute | solution.py:552
  78.5 2.2 %all-to-all-done.3 = f32[16,24,128]{2,1,0:T(8,128)S(1)} async-done(((f32[16,24,128]{2,1,0:T(8,128)}), f32[16,24,128]{2,1,0:T(8,128)S(1)}, u32[]{:S(2)}, u32[]{:S(2)}) %all-to-all-start.3) | async-done | bytes 196640 | tf_op jit(solution)/shard_map/all_to_all | solution.py:538
  80.7 10.5 %all_to_all.47.around = f32[8,40,128]{2,1,0:T(8,128)S(1)} all-to-all(f32[8,40,128]{2,1,0:T(8,128)S(1)} %broadcast_in_dim.14), channel_id=1, replica_groups=mesh['y'=4,'x'=4,'core'=2,'z'=8] {'z'}, dimensions={0} | all-to-all | bytes 327680 | tf_op jit(solution)/shard_map/all_to_all | solution.py:538
  91.2 14.4 %all_to_all.48.got_mine = f32[16,24,128]{2,1,0:T(8,128)S(1)} all-to-all(f32[16,24,128]{2,1,0:T(8,128)S(1)} %broadcast_in_dim.15), channel_id=1, replica_groups=mesh['y'=4,'x'=4,'core'=2,'z'=8] {'y','x'}, dimensions={0} | all-to-all | bytes 393216 | tf_op jit(solution)/shard_map/all_to_all | solution.py:538
  105.6 1.2 collective-permute-start.5
  106.8 1.1 collective-permute-done.5.got_other
  107.9 6.6 %factor_and_expand.1 = (f32[64,2048]{1,0:T(8,128)S(1)}, f32[128,128]{1,0:T(8,128)S(1)}, f32[128,128]{1,0:T(8,128)S(1)}, bf16[4,2,256,2048]{3,2,1,0:T(8,128)(2,1)S(1)}) custom-call(f32[16,24,128]{2,1,0:T(8,128)S(1)} %all_to_all.48.got_mine, f32[16,24,128]{2,1,0:T(8,128)S(1)} %collective-permute-done.5.got_other, ...), custom_call_target="tpu_custom_call" | custom-call | tf_op jit(solution)/shard_map/factor_and_expand/pallas_call | solution.py:421
  114.4 2.5 %collective-permute-start.6 = (f32[128,128]{1,0:T(8,128)S(1)}, f32[128,128]{1,0:T(8,128)S(1)}, u32[]{:S(2)}, u32[]{:S(2)}) collective-permute-start(f32[128,128]{1,0:T(8,128)S(1)} %get-tuple-element.49), channel_id=1, source_target_pairs={{0,8},{8,16},{16,24},{24,32},{32,40},{40,48},{48,56},{56,64},{64,7... | collective-permute-start | bytes 196616 | tf_op jit(solution)/shard_map/ppermute | solution.py:568
  116.9 2.2 %collective-permute-start.7 = (f32[128,128]{1,0:T(8,128)S(1)}, f32[128,128]{1,0:T(8,128)S(1)}, u32[]{:S(2)}, u32[]{:S(2)}) collective-permute-start(f32[128,128]{1,0:T(8,128)S(1)} %get-tuple-element.50), channel_id=1, source_target_pairs={{0,1},{1,2},{2,3},{3,4},{4,5},{5,6},{6,7},{8,9},{9,10},{10,11},{11... | collective-permute-start | bytes 196616 | tf_op jit(solution)/shard_map/ppermute | solution.py:568
  119.1 2.6 %project.1.base = f32[2,16,24,128]{3,2,1,0:T(8,128)S(1)} custom-call(bf16[4,2,256,2048]{3,2,1,0:T(8,128)(2,1)S(1)} %get-tuple-element.51.held, f32[64,2048]{1,0:T(8,128)S(1)} %get-tuple-element.48.field), custom_call_target="tpu_custom_call" | custom-call | tf_op jit(solution)/shard_map/project/pallas_call | solution.py:450
  121.7 0.9 roughness_products.1
  122.9 1.2 collective-permute-done.8
  124.2 12.4 %all_to_all.49 = f32[16,24,128]{2,1,0:T(8,128)S(1)} all-to-all(f32[16,24,128]{2,1,0:T(8,128)S(1)} %add.11), channel_id=1, replica_groups=mesh['y'=4,'x'=4,'core'=2,'z'=8] {'y','x'}, dimensions={0} | all-to-all | bytes 393216 | tf_op jit(solution)/shard_map/all_to_all | solution.py:538
  136.6 10.3 %all_to_all.50 = f32[8,24,128]{2,1,0:T(8,128)S(1)} all-to-all(f32[8,24,128]{2,1,0:T(8,128)S(1)} %broadcast_in_dim.16), channel_id=1, replica_groups=mesh['y'=4,'x'=4,'core'=2,'z'=8] {'z'}, dimensions={0} | all-to-all | bytes 196608 | tf_op jit(solution)/shard_map/all_to_all | solution.py:538
  147.0 9.8 %all_to_all.51.got_mine = f32[16,24,128]{2,1,0:T(8,128)S(1)} all-to-all(f32[16,24,128]{2,1,0:T(8,128)S(1)} %broadcast_in_dim.17), channel_id=1, replica_groups=mesh['y'=4,'x'=4,'core'=2,'z'=8] {'y','x'}, dimensions={0} | all-to-all | bytes 393216 | tf_op jit(solution)/shard_map/all_to_all | solution.py:538
  156.8 4.2 %collective-permute-start.9 = (f32[16,24,128]{2,1,0:T(8,128)S(1)}, f32[16,24,128]{2,1,0:T(8,128)S(1)}, u32[]{:S(2)}, u32[]{:S(2)}) collective-permute-start(f32[16,24,128]{2,1,0:T(8,128)S(1)} %all_to_all.51.got_mine), channel_id=1, source_target_pairs={{0,8},{8,0},{1,9},{9,1},{2,10},{10,2},{3,11},{11,3},{4,12},{12,4},... | collective-permute-start | bytes 589832 | tf_op jit(solution)/shard_map/ppermute | solution.py:561
  161.0 1.1 collective-permute-done.9.got_other
  162.1 3.7 %factor_and_finish.1 = (f32[1024,128]{1,0:T(8,128)}, f32[64,64]{1,0:T(8,128)}) custom-call(f32[16,24,128]{2,1,0:T(8,128)S(1)} %all_to_all.51.got_mine, f32[16,24,128]{2,1,0:T(8,128)S(1)} %collective-permute-done.9.got_other, f32[64,2048]{1,0:T(8,128)S(1)} %get-tuple-element.48.field), custom_call_target="tpu_custom_call" | custom-call | tf_op jit(solution)/shard_map/factor_and_finish/pallas_call | solution.py:522
  (32 shorter events, 4.0 us)
Async XLA Ops:
  0.6 0.7 copy-start
  1.3 58.6 %copy-start.1 = (s32[16,128]{1,0:T(8,128)S(1)}, s32[16,128]{1,0:T(8,128)}, u32[]{:S(2)}) copy-start(s32[16,128]{1,0:T(8,128)} %sea.3) | copy-start | bytes 24580
  1.3 58.6 %copy-start.2 = (f32[16,128]{1,0:T(8,128)S(1)}, f32[16,128]{1,0:T(8,128)}, u32[]{:S(2)}) copy-start(f32[16,128]{1,0:T(8,128)} %pen.5) | copy-start | bytes 24580
  9.7 4.3 %collective-permute-start = (f32[320,128]{1,0:T(8,128)S(1)}, f32[320,128]{1,0:T(8,128)S(1)}, u32[]{:S(2)}, u32[]{:S(2)}) collective-permute-start(f32[320,128]{1,0:T(8,128)S(1)} %get-tuple-element.30), channel_id=1, source_target_pairs={{0,8},{8,0},{1,9},{9,1},{2,10},{10,2},{3,11},{11,3},{4,12},{12,4},... | collective-permute-start | bytes 491528 | tf_op jit(solution)/shard_map/ppermute | solution.py:547
  14.8 11.9 %all-to-all-start = ((f32[16,16,128]{2,1,0:T(8,128)}), f32[16,16,128]{2,1,0:T(8,128)S(1)}, u32[]{:S(2)}, u32[]{:S(2)}) async-start(f32[16,16,128]{2,1,0:T(8,128)} %add.9), calls=%async_computation | async-start | bytes 262144 | tf_op jit(solution)/shard_map/all_to_all | solution.py:538
  19.8 6.0 %collective-permute-start.1 = (f32[64,128]{1,0:T(8,128)S(1)}, f32[64,128]{1,0:T(8,128)S(1)}, u32[]{:S(2)}, u32[]{:S(2)}) collective-permute-start(f32[64,128]{1,0:T(8,128)S(1)} %get-tuple-element.33), channel_id=1, source_target_pairs={{8,16},{16,8},{24,32},{32,24},{40,48},{48,40},{56,64},{64,56},{72,... | collective-permute-start | bytes 98312 | tf_op jit(solution)/shard_map/ppermute | solution.py:552
  57.1 2.8 %collective-permute-start.2 = (f32[16,16,128]{2,1,0:T(8,128)S(1)}, f32[16,16,128]{2,1,0:T(8,128)S(1)}, u32[]{:S(2)}, u32[]{:S(2)}) collective-permute-start(f32[16,16,128]{2,1,0:T(8,128)S(1)} %all_to_all.46.got_mine), channel_id=1, source_target_pairs={{0,8},{8,0},{1,9},{9,1},{2,10},{10,2},{3,11},{11,3},{4,12},{12,4},... | collective-permute-start | bytes 393224 | tf_op jit(solution)/shard_map/ppermute | solution.py:561
  66.9 1.6 collective-permute-start.3
  69.2 11.4 %all-to-all-start.3 = ((f32[16,24,128]{2,1,0:T(8,128)}), f32[16,24,128]{2,1,0:T(8,128)S(1)}, u32[]{:S(2)}, u32[]{:S(2)}) async-start(f32[16,24,128]{2,1,0:T(8,128)} %add.10), calls=%async_computation.3 | async-start | bytes 393216 | tf_op jit(solution)/shard_map/all_to_all | solution.py:538
  72.9 5.6 %collective-permute-start.4 = (f32[64,128]{1,0:T(8,128)S(1)}, f32[64,128]{1,0:T(8,128)S(1)}, u32[]{:S(2)}, u32[]{:S(2)}) collective-permute-start(f32[64,128]{1,0:T(8,128)S(1)} %get-tuple-element.43), channel_id=1, source_target_pairs={{8,16},{16,8},{24,32},{32,24},{40,48},{48,40},{56,64},{64,56},{72,... | collective-permute-start | bytes 98312 | tf_op jit(solution)/shard_map/ppermute | solution.py:552
  105.6 2.3 %collective-permute-start.5 = (f32[16,24,128]{2,1,0:T(8,128)S(1)}, f32[16,24,128]{2,1,0:T(8,128)S(1)}, u32[]{:S(2)}, u32[]{:S(2)}) collective-permute-start(f32[16,24,128]{2,1,0:T(8,128)S(1)} %all_to_all.48.got_mine), channel_id=1, source_target_pairs={{0,8},{8,0},{1,9},{9,1},{2,10},{10,2},{3,11},{11,3},{4,12},{12,4},... | collective-permute-start | bytes 589832 | tf_op jit(solution)/shard_map/ppermute | solution.py:561
  114.4 7.2 %collective-permute-start.6 = (f32[128,128]{1,0:T(8,128)S(1)}, f32[128,128]{1,0:T(8,128)S(1)}, u32[]{:S(2)}, u32[]{:S(2)}) collective-permute-start(f32[128,128]{1,0:T(8,128)S(1)} %get-tuple-element.49), channel_id=1, source_target_pairs={{0,8},{8,16},{16,24},{24,32},{32,40},{40,48},{48,56},{56,64},{64,7... | collective-permute-start | bytes 196616 | tf_op jit(solution)/shard_map/ppermute | solution.py:568
  116.9 4.8 %collective-permute-start.7 = (f32[128,128]{1,0:T(8,128)S(1)}, f32[128,128]{1,0:T(8,128)S(1)}, u32[]{:S(2)}, u32[]{:S(2)}) collective-permute-start(f32[128,128]{1,0:T(8,128)S(1)} %get-tuple-element.50), channel_id=1, source_target_pairs={{0,1},{1,2},{2,3},{3,4},{4,5},{5,6},{6,7},{8,9},{9,10},{10,11},{11... | collective-permute-start | bytes 196616 | tf_op jit(solution)/shard_map/ppermute | solution.py:568
  122.6 1.5 collective-permute-start.8
  156.8 5.3 %collective-permute-start.9 = (f32[16,24,128]{2,1,0:T(8,128)S(1)}, f32[16,24,128]{2,1,0:T(8,128)S(1)}, u32[]{:S(2)}, u32[]{:S(2)}) collective-permute-start(f32[16,24,128]{2,1,0:T(8,128)S(1)} %all_to_all.51.got_mine), channel_id=1, source_target_pairs={{0,8},{8,0},{1,9},{9,1},{2,10},{10,2},{3,11},{11,3},{4,12},{12,4},... | collective-permute-start | bytes 589832 | tf_op jit(solution)/shard_map/ppermute | solution.py:561

commit v5 on v4

--- a/solution.py
+++ b/solution.py
@@ -132,15 +132,9 @@
     return north, south, west, east
 
 
-def take_in(mine, other, full):
-    me = lax.axis_index("core")
-    full[me] = mine[...]
-    full[1 - me] = other[...]
-
-
 def row_of_shards(full, row):
     return jnp.concatenate(
-        [full[half, chip, row : row + 1, :] for half in range(2) for chip in range(16)], axis=0
+        [full[2 * chip + half, row : row + 1, :] for half in range(2) for chip in range(16)], axis=0
     )
 
 
@@ -214,8 +208,8 @@
 
 
 def coefficients_of(full, at):
-    chips = slice(4 * (at % 4), 4 * (at % 4) + 4)
-    return full[at // 4, chips, 0:16, :].reshape(K, LANES)
+    chips = range(4 * (at % 4), 4 * (at % 4) + 4)
+    return jnp.concatenate([full[2 * chip + at // 4, 0:16, :] for chip in chips], axis=0)
 
 
 def spread_coefficients(full, spread):
@@ -349,12 +343,11 @@
 
 
 def first_kernel(
-    got_mine, got_other, snap, prev, pair, near, around, sea, pen,
+    full, snap, prev, pair, near, around, sea, pen,
     field, mine, other, cross, columns,
-    full, spread, total, rough, held, split, pay, sems,
+    spread, total, rough, held, split, pay, sems,
 ):
     begin_copies(snap, held, sems)
-    take_in(got_mine, got_other, full)
     spread_coefficients(full, spread)
     rough_field(prev, take_in_edges(pair, near, around), pen, rough)
     expand(spread, snap, held, sems, total)
@@ -368,9 +361,8 @@
     hand_out(pay, mine, other)
 
 
-def scratch_for_expand(depth):
+def scratch_for_expand():
     return [
-        pltpu.VMEM((2, 16, depth, LANES), F32),
         pltpu.VMEM((NBLOCK, 2 * K, BLOCK), BF16),
         pltpu.VMEM((K, PTS), F32),
         pltpu.VMEM((K, PTS), F32),
@@ -380,11 +372,11 @@
 def first_step(got, snap, prev, sides, sea, pen):
     return pl.pallas_call(
         first_kernel,
-        in_specs=[VM, VM, HB, *[VM] * 6],
+        in_specs=[VM, HB, *[VM] * 6],
         out_specs=[VM] * 5,
         out_shape=shared_outputs(SHARD),
         scratch_shapes=[
-            *scratch_for_expand(DEPTH),
+            *scratch_for_expand(),
             pltpu.VMEM((NBLOCK, 2, BLOCK, PTS), BF16),
             pltpu.VMEM((2 * K, PTS), BF16),
             pltpu.VMEM((2, 16, SHARD, LANES), F32),
@@ -392,16 +384,15 @@
         ],
         compiler_params=pltpu.CompilerParams(vmem_limit_bytes=VMEM_LIMIT),
         name="expand_and_project",
-    )(*got, snap, prev, *sides, sea, pen)
+    )(got, snap, prev, *sides, sea, pen)
 
 
 def second_kernel(
-    got_mine, got_other, snap, prev, pair, near, around, sea, pen,
+    full, snap, prev, pair, near, around, sea, pen,
     field, bottom, last, held,
-    full, spread, total, rough, raw, sems,
+    spread, total, rough, raw, sems,
 ):
     begin_copies(snap, held, sems)
-    take_in(got_mine, got_other, full)
     spread_coefficients(full, spread)
     inverse = inverse_factor(square_of(full, 16))
     rough_field(prev, take_in_edges(pair, near, around), pen, rough)
@@ -420,7 +411,7 @@
     halo = jax.ShapeDtypeStruct((2 * K, LANES), F32)
     return pl.pallas_call(
         second_kernel,
-        in_specs=[VM, VM, HB, *[VM] * 6],
+        in_specs=[VM, HB, *[VM] * 6],
         out_specs=[VM] * 4,
         out_shape=[
             jax.ShapeDtypeStruct((K, PTS), F32),
@@ -429,13 +420,13 @@
             jax.ShapeDtypeStruct((NBLOCK, 2, BLOCK, PTS), BF16),
         ],
         scratch_shapes=[
-            *scratch_for_expand(SHARD),
+            *scratch_for_expand(),
             pltpu.VMEM((K, PTS), F32),
             pltpu.SemaphoreType.DMA((NBLOCK,)),
         ],
         compiler_params=pltpu.CompilerParams(vmem_limit_bytes=MIDDLE_LIMIT),
         name="factor_and_expand",
-    )(*got, snap, prev, *sides, sea, pen)
+    )(got, snap, prev, *sides, sea, pen)
 
 
 def project_kernel(held, field, pay, split):
@@ -505,8 +496,7 @@
     )(field, north, west, pen, base)
 
 
-def last_kernel(got_mine, got_other, field, basis, matrix, full):
-    take_in(got_mine, got_other, full)
+def last_kernel(full, field, basis, matrix):
     inverse = inverse_factor(square_of(full, 16))
     solved = dot_nn(inverse, field[...], HIGHEST)
     for a in range(ROWS):
@@ -521,16 +511,15 @@
 def last_step(got, field):
     basis, matrix = pl.pallas_call(
         last_kernel,
-        in_specs=[VM] * 3,
+        in_specs=[VM] * 2,
         out_specs=[VM] * 2,
         out_shape=[
             jax.ShapeDtypeStruct((K * ROWS, LANES), F32),
             jax.ShapeDtypeStruct((K, K), F32),
         ],
-        scratch_shapes=[pltpu.VMEM((2, 16, SHARD, LANES), F32)],
         compiler_params=pltpu.CompilerParams(vmem_limit_bytes=SMALL_LIMIT),
         name="factor_and_finish",
-    )(*got, field)
+    )(got, field)
     return basis.reshape(K, ROWS, LANES), matrix
 
 
@@ -557,11 +546,10 @@
     if edges is not None:
         share = jnp.concatenate([share, columns], axis=0)
     around = exchange(copies(share, 8), "z")
-    half = exchange(copies(around[:, :depth].sum(axis=0), 16), CHIPS)
-    both = (half, lax.ppermute(half, "core", SWAP))
+    full = exchange(copies(around[:, :depth].sum(axis=0), 32), LAT)
     if edges is None:
-        return both, None
-    return both, (got[16 * depth :], near, around)
+        return full, None
+    return full, (got[16 * depth :], near, around)
 
 
 def from_below(value, axis, count):

time: 166 us -> 170 us (1.024)
  blocking collectives: 87.8 us -> 65.3 us
  waiting for transfers between devices: 13.3 us -> 29.5 us
  starting transfers between devices: 32.5 us -> 40.4 us
    all_to_all x7 -> x5, blocking collectives: 87.8 us -> 65.3 us  [exchange(): return lax.all_to_all(value, axis, 0, 0, tiled=True)]
    all_to_all x2 -> x4, waiting for transfers between devices: 3.03 us -> 22.2 us  [exchange(): return lax.all_to_all(value, axis, 0, 0, tiled=True)]
    all_to_all x2 -> x4, starting transfers between devices: 8.73 us -> 24.1 us  [exchange(): return lax.all_to_all(value, axis, 0, 0, tiled=True)]
    ppermute x3 -> x0, starting transfers between devices: 7.27 us -> none  [summed_everywhere(): both = (half, lax.ppermute(half, 'core', SWAP))]
    ppermute x3 -> x0, waiting for transfers between devices: 3.12 us -> none  [summed_everywhere(): both = (half, lax.ppermute(half, 'core', SWAP))]
  transfers between devices with their start and end apart: 12 -> 11, of which waited for: 10 -> 9; matrix products, arithmetic and copies ran while one was open for 0% -> 0% of each run, Pallas kernels for 2% -> 2%
where the time goes in v5:
time: 170 us; the launch traced here: 169 us
  blocking collectives  65.3 us (38%)
  starting transfers between devices  40.4 us (24%)
  waiting for transfers between devices  29.5 us (17%)
  Pallas kernels  29 us (17%)
  local copies, waits for them, and re-layouts  2.28 us (1%)
    all_to_all x5, blocking collectives, exchange(): return lax.all_to_all(value, axis, 0, 0, tiled=True)  65.3 us
    all_to_all x4, starting transfers between devices, exchange(): return lax.all_to_all(value, axis, 0, 0, tiled=True)  24.1 us
    all_to_all x4, waiting for transfers between devices, exchange(): return lax.all_to_all(value, axis, 0, 0, tiled=True)  22.2 us
    pallas_call x1, Pallas kernels, begin(): pl.pallas_call(begin_kernel, in_specs=[HBM, HBM, HBM], out_specs=[HB, *[V...  8.4 us
    ppermute x2, starting transfers between devices, summed_everywhere(): near = lax.ppermute(cross, LAT, CROSS)  7.68 us
    pallas_call x1, Pallas kernels, first_step(): pl.pallas_call(first_kernel, in_specs=[VM, HB, *[VM] * 6], out_specs=[VM]...  6.95 us
    pallas_call x1, Pallas kernels, second_step(): pl.pallas_call(second_kernel, in_specs=[VM, HB, *[VM] * 6], out_specs=[VM...  6.56 us
    ppermute x2, starting transfers between devices, from_below(): return lax.ppermute(value, axis, [(i, i + 1) for i in range(count - 1)])  4.64 us
  transfers between devices with their start and end apart: 11, of which 9 were waited for; matrix products, arithmetic and copies ran while one was open for 0% of the time, Pallas kernels for 2%

profile of v5, /device:TPU:1, one launch (start us, length us, event | category | flops | bytes accessed | tf_op | source)
XLA Modules:
  0.0 168.8 jit_solution(13564968370024042241)
XLA Ops:
  1.3 8.4 %split_and_project.1 = (bf16[8,2,256,2048]{3,2,1,0:T(8,128)(2,1)}, f32[64,2048]{1,0:T(8,128)S(1)}, f32[16,16,128]{2,1,0:T(8,128)S(1)}, f32[320,128]{1,0:T(8,128)...) custom-call(f32[16384,128]{1,0:T(8,128)} %bitcast.6, f32[1024,128]{1,0:T(8,128)} %bitcast.8, s32[16,128]{1,0:T(8,128)S(1)} %copy-done), custom_call_target="tpu_custom_call" | custom-call | tf_op jit(solution)/shard_map/split_and_project/pallas_call | solution.py:283
  9.7 3.3 %collective-permute-start = (f32[320,128]{1,0:T(8,128)S(1)}, f32[320,128]{1,0:T(8,128)S(1)}, u32[]{:S(2)}, u32[]{:S(2)}) collective-permute-start(f32[320,128]{1,0:T(8,128)S(1)} %get-tuple-element.30), channel_id=1, source_target_pairs={{0,8},{8,0},{1,9},{9,1},{2,10},{10,2},{3,11},{11,3},{4,12},{12,4},... | collective-permute-start | bytes 491528 | tf_op jit(solution)/shard_map/ppermute | solution.py:536
  13.1 1.0 collective-permute-done
  14.8 5.0 %all-to-all-start = ((f32[16,16,128]{2,1,0:T(8,128)}), f32[16,16,128]{2,1,0:T(8,128)S(1)}, u32[]{:S(2)}, u32[]{:S(2)}) async-start(f32[16,16,128]{2,1,0:T(8,128)} %add.9), calls=%async_computation | async-start | bytes 262144 | tf_op jit(solution)/shard_map/all_to_all | solution.py:527
  19.8 4.1 %collective-permute-start.1 = (f32[64,128]{1,0:T(8,128)S(1)}, f32[64,128]{1,0:T(8,128)S(1)}, u32[]{:S(2)}, u32[]{:S(2)}) collective-permute-start(f32[64,128]{1,0:T(8,128)S(1)} %get-tuple-element.33), channel_id=1, source_target_pairs={{8,16},{16,8},{24,32},{32,24},{40,48},{48,40},{56,64},{64,56},{72,... | collective-permute-start | bytes 98312 | tf_op jit(solution)/shard_map/ppermute | solution.py:541
  23.9 1.9 %collective-permute-done.1.near = f32[64,128]{1,0:T(8,128)S(1)} collective-permute-done((f32[64,128]{1,0:T(8,128)S(1)}, f32[64,128]{1,0:T(8,128)S(1)}, u32[]{:S(2)}, u32[]{:S(2)}) %collective-permute-start.1) | collective-permute-done | bytes 32800 | tf_op jit(solution)/shard_map/ppermute | solution.py:541
  25.8 0.9 all-to-all-done
  26.7 16.0 %all_to_all.45.around = f32[8,32,128]{2,1,0:T(8,128)S(1)} all-to-all(f32[8,32,128]{2,1,0:T(8,128)S(1)} %broadcast_in_dim.12), channel_id=1, replica_groups=mesh['y'=4,'x'=4,'core'=2,'z'=8] {'z'}, dimensions={0} | all-to-all | bytes 262144 | tf_op jit(solution)/shard_map/all_to_all | solution.py:527
  42.7 0.7 broadcast_in_dim.13
  43.5 8.4 %all-to-all-start.2 = ((f32[32,16,128]{2,1,0:T(8,128)}), f32[32,16,128]{2,1,0:T(8,128)S(1)}, u32[]{:S(2)}, u32[]{:S(2)}) async-start(f32[32,16,128]{2,1,0:T(8,128)} %broadcast_in_dim.13), calls=%async_computation.2 | async-start | bytes 524288 | tf_op jit(solution)/shard_map/all_to_all | solution.py:527
  51.9 8.9 %all-to-all-done.2.full = f32[32,16,128]{2,1,0:T(8,128)S(1)} async-done(((f32[32,16,128]{2,1,0:T(8,128)}), f32[32,16,128]{2,1,0:T(8,128)S(1)}, u32[]{:S(2)}, u32[]{:S(2)}) %all-to-all-start.2) | async-done | bytes 262176 | tf_op jit(solution)/shard_map/all_to_all | solution.py:527
  60.8 7.0 %expand_and_project.1 = (f32[64,2048]{1,0:T(8,128)S(1)}, f32[16,24,128]{2,1,0:T(8,128)S(1)}, f32[448,128]{1,0:T(8,128)S(1)}, f32[64,128]{1,0:T(8,128)S(1)}, f32[16,128]{1,0:T(8,128)S(1)}) custom-call(f32[32,16,128]{2,1,0:T(8,128)S(1)} %all-to-all-done.2.full, bf16[8,2,256,2048]{3,2,1,0:T(8,128)(2,1)} %get-tuple-element.36.snap, ...), custom_call_target="tpu_custom_call" | custom-call | tf_op jit(solution)/shard_map/expand_and_project/pallas_call | solution.py:373
  68.1 1.3 collective-permute-done.2
  69.3 0.7 add.10
  70.0 3.5 %all-to-all-start.3 = ((f32[16,24,128]{2,1,0:T(8,128)}), f32[16,24,128]{2,1,0:T(8,128)S(1)}, u32[]{:S(2)}, u32[]{:S(2)}) async-start(f32[16,24,128]{2,1,0:T(8,128)} %add.10), calls=%async_computation.3 | async-start | bytes 393216 | tf_op jit(solution)/shard_map/all_to_all | solution.py:527
  73.6 3.6 %collective-permute-start.3 = (f32[64,128]{1,0:T(8,128)S(1)}, f32[64,128]{1,0:T(8,128)S(1)}, u32[]{:S(2)}, u32[]{:S(2)}) collective-permute-start(f32[64,128]{1,0:T(8,128)S(1)} %get-tuple-element.43), channel_id=1, source_target_pairs={{8,16},{16,8},{24,32},{32,24},{40,48},{48,40},{56,64},{64,56},{72,... | collective-permute-start | bytes 98312 | tf_op jit(solution)/shard_map/ppermute | solution.py:541
  77.2 1.9 %collective-permute-done.3.near = f32[64,128]{1,0:T(8,128)S(1)} collective-permute-done((f32[64,128]{1,0:T(8,128)S(1)}, f32[64,128]{1,0:T(8,128)S(1)}, u32[]{:S(2)}, u32[]{:S(2)}) %collective-permute-start.3) | collective-permute-done | bytes 32800 | tf_op jit(solution)/shard_map/ppermute | solution.py:541
  79.1 2.3 %all-to-all-done.3 = f32[16,24,128]{2,1,0:T(8,128)S(1)} async-done(((f32[16,24,128]{2,1,0:T(8,128)}), f32[16,24,128]{2,1,0:T(8,128)S(1)}, u32[]{:S(2)}, u32[]{:S(2)}) %all-to-all-start.3) | async-done | bytes 196640 | tf_op jit(solution)/shard_map/all_to_all | solution.py:527
  81.4 10.6 %all_to_all.46.around = f32[8,40,128]{2,1,0:T(8,128)S(1)} all-to-all(f32[8,40,128]{2,1,0:T(8,128)S(1)} %broadcast_in_dim.14), channel_id=1, replica_groups=mesh['y'=4,'x'=4,'core'=2,'z'=8] {'z'}, dimensions={0} | all-to-all | bytes 327680 | tf_op jit(solution)/shard_map/all_to_all | solution.py:527
  92.1 0.8 broadcast_in_dim.15
  92.9 7.1 %all-to-all-start.5 = ((f32[32,24,128]{2,1,0:T(8,128)}), f32[32,24,128]{2,1,0:T(8,128)S(1)}, u32[]{:S(2)}, u32[]{:S(2)}) async-start(f32[32,24,128]{2,1,0:T(8,128)} %broadcast_in_dim.15), calls=%async_computation.5 | async-start | bytes 786432 | tf_op jit(solution)/shard_map/all_to_all | solution.py:527
  100.0 10.2 %all-to-all-done.5.full = f32[32,24,128]{2,1,0:T(8,128)S(1)} async-done(((f32[32,24,128]{2,1,0:T(8,128)}), f32[32,24,128]{2,1,0:T(8,128)S(1)}, u32[]{:S(2)}, u32[]{:S(2)}) %all-to-all-start.5) | async-done | bytes 393248 | tf_op jit(solution)/shard_map/all_to_all | solution.py:527
  110.2 6.6 %factor_and_expand.1 = (f32[64,2048]{1,0:T(8,128)S(1)}, f32[128,128]{1,0:T(8,128)S(1)}, f32[128,128]{1,0:T(8,128)S(1)}, bf16[4,2,256,2048]{3,2,1,0:T(8,128)(2,1)S(1)}) custom-call(f32[32,24,128]{2,1,0:T(8,128)S(1)} %all-to-all-done.5.full, bf16[8,2,256,2048]{3,2,1,0:T(8,128)(2,1)} %get-tuple-element.36.snap, f32[64,2048]{1,0:T(8,128)S(1)} %get-tuple-element.46.prev, ...), custom_call_target="tpu_custom_call" | custom-call | tf_op jit(solution)/shard_map/factor_and_expand/pallas_call | solution.py:412
  116.7 2.5 %collective-permute-start.4 = (f32[128,128]{1,0:T(8,128)S(1)}, f32[128,128]{1,0:T(8,128)S(1)}, u32[]{:S(2)}, u32[]{:S(2)}) collective-permute-start(f32[128,128]{1,0:T(8,128)S(1)} %get-tuple-element.49), channel_id=1, source_target_pairs={{0,8},{8,16},{16,24},{24,32},{32,40},{40,48},{48,56},{56,64},{64,7... | collective-permute-start | bytes 196616 | tf_op jit(solution)/shard_map/ppermute | solution.py:556
  119.2 2.2 %collective-permute-start.5 = (f32[128,128]{1,0:T(8,128)S(1)}, f32[128,128]{1,0:T(8,128)S(1)}, u32[]{:S(2)}, u32[]{:S(2)}) collective-permute-start(f32[128,128]{1,0:T(8,128)S(1)} %get-tuple-element.50), channel_id=1, source_target_pairs={{0,1},{1,2},{2,3},{3,4},{4,5},{5,6},{6,7},{8,9},{9,10},{10,11},{11... | collective-permute-start | bytes 196616 | tf_op jit(solution)/shard_map/ppermute | solution.py:556
  121.4 2.6 %project.1.base = f32[2,16,24,128]{3,2,1,0:T(8,128)S(1)} custom-call(bf16[4,2,256,2048]{3,2,1,0:T(8,128)(2,1)S(1)} %get-tuple-element.51.held, f32[64,2048]{1,0:T(8,128)S(1)} %get-tuple-element.48.field), custom_call_target="tpu_custom_call" | custom-call | tf_op jit(solution)/shard_map/project/pallas_call | solution.py:441
  124.0 0.9 roughness_products.1
  125.2 1.2 collective-permute-done.6
  126.4 12.4 %all_to_all.47 = f32[16,24,128]{2,1,0:T(8,128)S(1)} all-to-all(f32[16,24,128]{2,1,0:T(8,128)S(1)} %add.11), channel_id=1, replica_groups=mesh['y'=4,'x'=4,'core'=2,'z'=8] {'y','x'}, dimensions={0} | all-to-all | bytes 393216 | tf_op jit(solution)/shard_map/all_to_all | solution.py:527
  138.8 10.3 %all_to_all.48 = f32[8,24,128]{2,1,0:T(8,128)S(1)} all-to-all(f32[8,24,128]{2,1,0:T(8,128)S(1)} %broadcast_in_dim.16), channel_id=1, replica_groups=mesh['y'=4,'x'=4,'core'=2,'z'=8] {'z'}, dimensions={0} | all-to-all | bytes 196608 | tf_op jit(solution)/shard_map/all_to_all | solution.py:527
  149.2 15.9 %all_to_all.49.full = f32[32,24,128]{2,1,0:T(8,128)S(1)} all-to-all(f32[32,24,128]{2,1,0:T(8,128)S(1)} %broadcast_in_dim.17), channel_id=1, replica_groups=mesh['y'=4,'x'=4,'core'=2,'z'=8] {'y','x','core'}, dimensions={0} | all-to-all | bytes 786432 | tf_op jit(solution)/shard_map/all_to_all | solution.py:527
  165.2 3.7 %factor_and_finish.1 = (f32[1024,128]{1,0:T(8,128)}, f32[64,64]{1,0:T(8,128)}) custom-call(f32[32,24,128]{2,1,0:T(8,128)S(1)} %all_to_all.49.full, f32[64,2048]{1,0:T(8,128)S(1)} %get-tuple-element.48.field), custom_call_target="tpu_custom_call" | custom-call | tf_op jit(solution)/shard_map/factor_and_finish/pallas_call | solution.py:512
  (28 shorter events, 2.2 us)
Async XLA Ops:
  0.6 0.7 copy-start
  1.3 59.5 %copy-start.1 = (s32[16,128]{1,0:T(8,128)S(1)}, s32[16,128]{1,0:T(8,128)}, u32[]{:S(2)}) copy-start(s32[16,128]{1,0:T(8,128)} %sea.3) | copy-start | bytes 24580
  1.3 59.5 %copy-start.2 = (f32[16,128]{1,0:T(8,128)S(1)}, f32[16,128]{1,0:T(8,128)}, u32[]{:S(2)}) copy-start(f32[16,128]{1,0:T(8,128)} %pen.5) | copy-start | bytes 24580
  9.7 4.3 %collective-permute-start = (f32[320,128]{1,0:T(8,128)S(1)}, f32[320,128]{1,0:T(8,128)S(1)}, u32[]{:S(2)}, u32[]{:S(2)}) collective-permute-start(f32[320,128]{1,0:T(8,128)S(1)} %get-tuple-element.30), channel_id=1, source_target_pairs={{0,8},{8,0},{1,9},{9,1},{2,10},{10,2},{3,11},{11,3},{4,12},{12,4},... | collective-permute-start | bytes 491528 | tf_op jit(solution)/shard_map/ppermute | solution.py:536
  14.8 11.9 %all-to-all-start = ((f32[16,16,128]{2,1,0:T(8,128)}), f32[16,16,128]{2,1,0:T(8,128)S(1)}, u32[]{:S(2)}, u32[]{:S(2)}) async-start(f32[16,16,128]{2,1,0:T(8,128)} %add.9), calls=%async_computation | async-start | bytes 262144 | tf_op jit(solution)/shard_map/all_to_all | solution.py:527
  19.8 6.0 %collective-permute-start.1 = (f32[64,128]{1,0:T(8,128)S(1)}, f32[64,128]{1,0:T(8,128)S(1)}, u32[]{:S(2)}, u32[]{:S(2)}) collective-permute-start(f32[64,128]{1,0:T(8,128)S(1)} %get-tuple-element.33), channel_id=1, source_target_pairs={{8,16},{16,8},{24,32},{32,24},{40,48},{48,40},{56,64},{64,56},{72,... | collective-permute-start | bytes 98312 | tf_op jit(solution)/shard_map/ppermute | solution.py:541
  43.5 17.3 %all-to-all-start.2 = ((f32[32,16,128]{2,1,0:T(8,128)}), f32[32,16,128]{2,1,0:T(8,128)S(1)}, u32[]{:S(2)}, u32[]{:S(2)}) async-start(f32[32,16,128]{2,1,0:T(8,128)} %broadcast_in_dim.13), calls=%async_computation.2 | async-start | bytes 524288 | tf_op jit(solution)/shard_map/all_to_all | solution.py:527
  67.7 1.6 collective-permute-start.2
  70.0 11.3 %all-to-all-start.3 = ((f32[16,24,128]{2,1,0:T(8,128)}), f32[16,24,128]{2,1,0:T(8,128)S(1)}, u32[]{:S(2)}, u32[]{:S(2)}) async-start(f32[16,24,128]{2,1,0:T(8,128)} %add.10), calls=%async_computation.3 | async-start | bytes 393216 | tf_op jit(solution)/shard_map/all_to_all | solution.py:527
  73.6 5.5 %collective-permute-start.3 = (f32[64,128]{1,0:T(8,128)S(1)}, f32[64,128]{1,0:T(8,128)S(1)}, u32[]{:S(2)}, u32[]{:S(2)}) collective-permute-start(f32[64,128]{1,0:T(8,128)S(1)} %get-tuple-element.43), channel_id=1, source_target_pairs={{8,16},{16,8},{24,32},{32,24},{40,48},{48,40},{56,64},{64,56},{72,... | collective-permute-start | bytes 98312 | tf_op jit(solution)/shard_map/ppermute | solution.py:541
  92.9 17.3 %all-to-all-start.5 = ((f32[32,24,128]{2,1,0:T(8,128)}), f32[32,24,128]{2,1,0:T(8,128)S(1)}, u32[]{:S(2)}, u32[]{:S(2)}) async-start(f32[32,24,128]{2,1,0:T(8,128)} %broadcast_in_dim.15), calls=%async_computation.5 | async-start | bytes 786432 | tf_op jit(solution)/shard_map/all_to_all | solution.py:527
  116.7 7.2 %collective-permute-start.4 = (f32[128,128]{1,0:T(8,128)S(1)}, f32[128,128]{1,0:T(8,128)S(1)}, u32[]{:S(2)}, u32[]{:S(2)}) collective-permute-start(f32[128,128]{1,0:T(8,128)S(1)} %get-tuple-element.49), channel_id=1, source_target_pairs={{0,8},{8,16},{16,24},{24,32},{32,40},{40,48},{48,56},{56,64},{64,7... | collective-permute-start | bytes 196616 | tf_op jit(solution)/shard_map/ppermute | solution.py:556
  119.2 4.8 %collective-permute-start.5 = (f32[128,128]{1,0:T(8,128)S(1)}, f32[128,128]{1,0:T(8,128)S(1)}, u32[]{:S(2)}, u32[]{:S(2)}) collective-permute-start(f32[128,128]{1,0:T(8,128)S(1)} %get-tuple-element.50), channel_id=1, source_target_pairs={{0,1},{1,2},{2,3},{3,4},{4,5},{5,6},{6,7},{8,9},{9,10},{10,11},{11... | collective-permute-start | bytes 196616 | tf_op jit(solution)/shard_map/ppermute | solution.py:556
  124.9 1.5 collective-permute-start.6

commit v6 on v4

--- a/solution.py
+++ b/solution.py
@@ -13,6 +13,7 @@
 PTS = ROWS * LANES
 BLOCK = 256
 NBLOCK = NSNAP // BLOCK
+HALF = BLOCK // 2
 SHARD = 24
 DEPTH = 16
 F32 = jnp.float32
@@ -25,6 +26,7 @@
 VMEM_LIMIT = 50 * 1024 * 1024
 FIRST_LIMIT = 53 * 1024 * 1024
 MIDDLE_LIMIT = 36 * 1024 * 1024
+LATE = 2
 SMALL_LIMIT = 20 * 1024 * 1024
 
 
@@ -226,6 +228,19 @@
             spread[block, K : 2 * K, cols(part)] = low
 
 
+def arrival(snap, raw, sems, piece):
+    span = pl.ds(piece * HALF * ROWS, HALF * ROWS)
+    return pltpu.make_async_copy(snap.at[span], raw.at[span], sems.at[piece])
+
+
+def split_piece(raw, held, piece):
+    span = slice((piece % 2) * HALF, (piece % 2 + 1) * HALF)
+    for a in range(ROWS):
+        high, low = parts(raw[pl.ds(piece * HALF * ROWS + a, HALF, stride=ROWS), :])
+        held[piece // 2, 0, span, cols(a)] = high
+        held[piece // 2, 1, span, cols(a)] = low
+
+
 def begin_kernel(
     snap, basis_in, sea_in, snap_out, flat, mine, other, cross, columns,
     raw, held, split, pay, basis, sea, in_sems, out_sems, own_sems,
@@ -236,18 +251,12 @@
     ]
     for copy in own:
         copy.start()
-    deep = BLOCK // 2
-
-    def arrive(piece):
-        span = pl.ds(piece * deep * ROWS, deep * ROWS)
-        return pltpu.make_async_copy(snap.at[span], raw.at[span], in_sems.at[piece])
-
     def leave(piece):
-        at = (piece // 2, slice(None), pl.ds((piece % 2) * deep, deep))
+        at = (piece // 2, slice(None), pl.ds((piece % 2) * HALF, HALF))
         return pltpu.make_async_copy(held.at[at], snap_out.at[at], out_sems.at[piece])
 
     for piece in range(2 * NBLOCK):
-        arrive(piece).start()
+        arrival(snap, raw, in_sems, piece).start(priority=piece % 2)
     for copy in own:
         copy.wait()
     for a in range(ROWS):
@@ -257,16 +266,13 @@
     hand_out_edges(flat, DEPTH, other, cross, columns)
     for block in range(NBLOCK):
         for piece in (2 * block, 2 * block + 1):
-            arrive(piece).wait()
-            span = slice((piece % 2) * deep, (piece % 2 + 1) * deep)
-            for a in range(ROWS):
-                high, low = parts(raw[pl.ds(piece * deep * ROWS + a, deep, stride=ROWS), :])
-                held[block, 0, span, cols(a)] = high
-                held[block, 1, span, cols(a)] = low
-            leave(piece).start()
+            arrival(snap, raw, in_sems, piece).wait()
+            split_piece(raw, held, piece)
+            if block >= LATE:
+                leave(piece).start(priority=piece % 2)
     project(held, split, pay)
     hand_out(pay, mine, other)
-    for piece in range(2 * NBLOCK):
+    for piece in range(2 * LATE, 2 * NBLOCK):
         leave(piece).wait()
 
 
@@ -314,15 +320,10 @@
     return pltpu.make_async_copy(snap.at[block], held.at[block], sems.at[block])
 
 
-def begin_copies(snap, held, sems):
-    for block in range(NBLOCK):
-        copy_of(snap, held, sems, block).start()
-
-
-def expand(spread, snap, held, sems, total):
+def expand(spread, held, total, arrive):
     width = 512
     for block in range(NBLOCK):
-        copy_of(snap, held, sems, block).wait()
+        arrive(block)
         for left in range(0, PTS, width):
             at = slice(left, left + width)
             both = dot_nn(spread[block], held[block, 0, :, at]) + dot_nn(
@@ -349,15 +350,31 @@
 
 
 def first_kernel(
-    got_mine, got_other, snap, prev, pair, near, around, sea, pen,
-    field, mine, other, cross, columns,
-    full, spread, total, rough, held, split, pay, sems,
+    got_mine, got_other, fresh, snap, prev, pair, near, around, sea, pen,
+    snap_out, field, mine, other, cross, columns,
+    full, spread, total, rough, held, split, pay, raw, sems, fresh_sems, out_sems,
 ):
-    begin_copies(snap, held, sems)
+    for piece in range(2 * LATE):
+        arrival(fresh, raw, fresh_sems, piece).start(priority=piece % 2)
+    for block in range(LATE, NBLOCK):
+        copy_of(snap, held, sems, block).start(priority=block % 2)
     take_in(got_mine, got_other, full)
     spread_coefficients(full, spread)
     rough_field(prev, take_in_edges(pair, near, around), pen, rough)
-    expand(spread, snap, held, sems, total)
+
+    def leave(block):
+        return pltpu.make_async_copy(held.at[block], snap_out.at[block], out_sems.at[block])
+
+    def arrive(block):
+        if block >= LATE:
+            copy_of(snap, held, sems, block).wait()
+            return
+        for piece in (2 * block, 2 * block + 1):
+            arrival(fresh, raw, fresh_sems, piece).wait()
+            split_piece(raw, held, piece)
+        leave(block).start(priority=block % 2)
+
+    expand(spread, held, total, arrive)
     applied_field(total, rough, sea, field)
     for a in range(ROWS):
         store_split(split, a, field[:, cols(a)])
@@ -366,6 +383,8 @@
     put_square(pay, 16, folded(dot_nt(split[...], split[...])))
     project(held, split, pay)
     hand_out(pay, mine, other)
+    for block in range(LATE):
+        leave(block).wait()
 
 
 def scratch_for_expand(depth):
@@ -377,37 +396,56 @@
     ]
 
 
-def first_step(got, snap, prev, sides, sea, pen):
+def first_step(got, fresh, snap, prev, sides, sea, pen):
     return pl.pallas_call(
         first_kernel,
-        in_specs=[VM, VM, HB, *[VM] * 6],
-        out_specs=[VM] * 5,
-        out_shape=shared_outputs(SHARD),
+        in_specs=[VM, VM, HB, HB, *[VM] * 6],
+        out_specs=[HB, *[VM] * 5],
+        out_shape=[
+            jax.ShapeDtypeStruct((2 * NBLOCK, 2, BLOCK, PTS), BF16),
+            *shared_outputs(SHARD),
+        ],
         scratch_shapes=[
             *scratch_for_expand(DEPTH),
             pltpu.VMEM((NBLOCK, 2, BLOCK, PTS), BF16),
             pltpu.VMEM((2 * K, PTS), BF16),
             pltpu.VMEM((2, 16, SHARD, LANES), F32),
+            pltpu.VMEM((LATE * BLOCK * ROWS, LANES), F32),
             pltpu.SemaphoreType.DMA((NBLOCK,)),
+            pltpu.SemaphoreType.DMA((2 * LATE,)),
+            pltpu.SemaphoreType.DMA((LATE,)),
         ],
         compiler_params=pltpu.CompilerParams(vmem_limit_bytes=VMEM_LIMIT),
         name="expand_and_project",
-    )(*got, snap, prev, *sides, sea, pen)
+    )(*got, fresh.reshape(NSNAP * ROWS, LANES), snap, prev, *sides, sea, pen)
+
+
+def solved(inverse, field, split):
+    for a in range(ROWS):
+        store_split(split, a, field[:, cols(a)])
+    high, low = parts(inverse)
+    left = [jnp.concatenate([part, part], axis=1) for part in (high, low)]
+    both = dot_nn(jnp.concatenate(left, axis=0), split[...])
+    return both[0:K] + both[K : 2 * K]
 
 
 def second_kernel(
-    got_mine, got_other, snap, prev, pair, near, around, sea, pen,
+    got_mine, got_other, early, snap, prev, pair, near, around, sea, pen,
     field, bottom, last, held,
-    full, spread, total, rough, raw, sems,
+    full, spread, total, rough, raw, split, sems,
 ):
-    begin_copies(snap, held, sems)
+    def copy(block):
+        return copy_of(early if block < LATE else snap, held, sems, block)
+
+    for block in range(NBLOCK):
+        copy(block).start(priority=block % 2)
     take_in(got_mine, got_other, full)
     spread_coefficients(full, spread)
     inverse = inverse_factor(square_of(full, 16))
     rough_field(prev, take_in_edges(pair, near, around), pen, rough)
-    expand(spread, snap, held, sems, total)
+    expand(spread, held, total, lambda block: copy(block).wait())
     applied_field(total, rough, sea, raw)
-    field[...] = dot_nn(inverse, raw[...], HIGHEST)
+    field[...] = solved(inverse, raw, split)
     bottom[0:K, :] = field[:, cols(ROWS - 1)]
     bottom[K : 2 * K, :] = field[:, cols(ROWS - 1)] * pen[ROWS - 1 : ROWS, :]
     _, last[0:K, :] = edge_columns(field)
@@ -416,11 +454,11 @@
     _, last[K : 2 * K, :] = edge_columns(raw)
 
 
-def second_step(got, snap, prev, sides, sea, pen):
+def second_step(got, early, snap, prev, sides, sea, pen):
     halo = jax.ShapeDtypeStruct((2 * K, LANES), F32)
     return pl.pallas_call(
         second_kernel,
-        in_specs=[VM, VM, HB, *[VM] * 6],
+        in_specs=[VM, VM, HB, HB, *[VM] * 6],
         out_specs=[VM] * 4,
         out_shape=[
             jax.ShapeDtypeStruct((K, PTS), F32),
@@ -431,11 +469,12 @@
         scratch_shapes=[
             *scratch_for_expand(SHARD),
             pltpu.VMEM((K, PTS), F32),
+            pltpu.VMEM((2 * K, PTS), BF16),
             pltpu.SemaphoreType.DMA((NBLOCK,)),
         ],
         compiler_params=pltpu.CompilerParams(vmem_limit_bytes=MIDDLE_LIMIT),
         name="factor_and_expand",
-    )(*got, snap, prev, *sides, sea, pen)
+    )(*got, early, snap, prev, *sides, sea, pen)
 
 
 def project_kernel(held, field, pay, split):
@@ -505,12 +544,12 @@
     )(field, north, west, pen, base)
 
 
-def last_kernel(got_mine, got_other, field, basis, matrix, full):
+def last_kernel(got_mine, got_other, field, basis, matrix, full, split):
     take_in(got_mine, got_other, full)
     inverse = inverse_factor(square_of(full, 16))
-    solved = dot_nn(inverse, field[...], HIGHEST)
-    for a in range(ROWS):
-        basis[pl.ds(a, K, stride=ROWS), :] = solved[:, cols(a)]
+    final = solved(inverse, field, split)
+    for a in range(ROWS):
+        basis[pl.ds(a, K, stride=ROWS), :] = final[:, cols(a)]
     turned = jnp.concatenate([coefficients_of(full, at) for at in range(NSNAP // LANES)], axis=1)
     rough = square_of(full, 17)[:, 0:K]
     gram = dot_nt(turned, turned, HIGHEST)
@@ -527,7 +566,10 @@
             jax.ShapeDtypeStruct((K * ROWS, LANES), F32),
             jax.ShapeDtypeStruct((K, K), F32),
         ],
-        scratch_shapes=[pltpu.VMEM((2, 16, SHARD, LANES), F32)],
+        scratch_shapes=[
+            pltpu.VMEM((2, 16, SHARD, LANES), F32),
+            pltpu.VMEM((2 * K, PTS), BF16),
+        ],
         compiler_params=pltpu.CompilerParams(vmem_limit_bytes=SMALL_LIMIT),
         name="factor_and_finish",
     )(*got, field)
@@ -571,9 +613,11 @@
 def local(snapshots, land_sea, penalty, initial_basis):
     snap, start, mine, other, *edges = begin(snapshots, initial_basis, land_sea)
     got, sides = summed_everywhere(mine, other, edges)
-    applied, mine, other, *edges = first_step(got, snap, start, sides, land_sea, penalty)
+    early, applied, mine, other, *edges = first_step(
+        got, snapshots, snap, start, sides, land_sea, penalty
+    )
     got, sides = summed_everywhere(mine, other, edges)
-    applied, bottom, last, held = second_step(got, snap, applied, sides, land_sea, penalty)
+    applied, bottom, last, held = second_step(got, early, snap, applied, sides, land_sea, penalty)
     north = from_below(bottom, LAT, 32)
     west = from_below(last, "z", 8)
     base = project_step(held, applied)

time: 166 us -> 169 us (1.018)
  no operation moved by 1% of the time
where the time goes in v6:
time: 169 us; the launch traced here: 168 us
  blocking collectives  87.6 us (52%)
  starting transfers between devices  32.5 us (19%)
  Pallas kernels  30 us (18%)
  waiting for transfers between devices  13.3 us (8%)
  local copies, waits for them, and re-layouts  2.2 us (1%)
    all_to_all x7, blocking collectives, exchange(): return lax.all_to_all(value, axis, 0, 0, tiled=True)  87.6 us
    pallas_call x1, Pallas kernels, begin(): pl.pallas_call(begin_kernel, in_specs=[HBM, HBM, HBM], out_specs=[HB, *[V...  8.62 us
    all_to_all x2, starting transfers between devices, exchange(): return lax.all_to_all(value, axis, 0, 0, tiled=True)  8.54 us
    pallas_call x1, Pallas kernels, first_step(): pl.pallas_call(first_kernel, in_specs=[VM, VM, HB, HB, *[VM] * 6], out_sp...  8.3 us
    ppermute x2, starting transfers between devices, summed_everywhere(): near = lax.ppermute(cross, LAT, CROSS)  7.74 us
    ppermute x3, starting transfers between devices, summed_everywhere(): both = (half, lax.ppermute(half, 'core', SWAP))  7.27 us
    pallas_call x1, Pallas kernels, second_step(): pl.pallas_call(second_kernel, in_specs=[VM, VM, HB, HB, *[VM] * 6], out_s...  6.44 us
    ppermute x2, starting transfers between devices, from_below(): return lax.ppermute(value, axis, [(i, i + 1) for i in range(count - 1)])  4.86 us
  transfers between devices with their start and end apart: 12, of which 10 were waited for; matrix products, arithmetic and copies ran while one was open for 0% of the time, Pallas kernels for 2%

profile of v6, /device:TPU:1, one launch (start us, length us, event | category | flops | bytes accessed | tf_op | source)
XLA Modules:
  0.0 167.9 jit_solution(3417715062729234666)
XLA Ops:
  1.3 8.6 %split_and_project.1 = (bf16[8,2,256,2048]{3,2,1,0:T(8,128)(2,1)}, f32[64,2048]{1,0:T(8,128)S(1)}, f32[16,16,128]{2,1,0:T(8,128)S(1)}, f32[320,128]{1,0:T(8,128)...) custom-call(f32[16384,128]{1,0:T(8,128)} %bitcast.6, f32[1024,128]{1,0:T(8,128)} %bitcast.9, s32[16,128]{1,0:T(8,128)S(1)} %copy-done), custom_call_target="tpu_custom_call" | custom-call | tf_op jit(solution)/shard_map/split_and_project/pallas_call | solution.py:295
  10.0 3.3 %collective-permute-start = (f32[320,128]{1,0:T(8,128)S(1)}, f32[320,128]{1,0:T(8,128)S(1)}, u32[]{:S(2)}, u32[]{:S(2)}) collective-permute-start(f32[320,128]{1,0:T(8,128)S(1)} %get-tuple-element.31), channel_id=1, source_target_pairs={{0,8},{8,0},{1,9},{9,1},{2,10},{10,2},{3,11},{11,3},{4,12},{12,4},... | collective-permute-start | bytes 491528 | tf_op jit(solution)/shard_map/ppermute | solution.py:589
  13.3 1.0 collective-permute-done
  15.0 5.0 %all-to-all-start = ((f32[16,16,128]{2,1,0:T(8,128)}), f32[16,16,128]{2,1,0:T(8,128)S(1)}, u32[]{:S(2)}, u32[]{:S(2)}) async-start(f32[16,16,128]{2,1,0:T(8,128)} %add.9), calls=%async_computation | async-start | bytes 262144 | tf_op jit(solution)/shard_map/all_to_all | solution.py:580
  20.0 4.1 %collective-permute-start.1 = (f32[64,128]{1,0:T(8,128)S(1)}, f32[64,128]{1,0:T(8,128)S(1)}, u32[]{:S(2)}, u32[]{:S(2)}) collective-permute-start(f32[64,128]{1,0:T(8,128)S(1)} %get-tuple-element.34), channel_id=1, source_target_pairs={{8,16},{16,8},{24,32},{32,24},{40,48},{48,40},{56,64},{64,56},{72,... | collective-permute-start | bytes 98312 | tf_op jit(solution)/shard_map/ppermute | solution.py:594
  24.1 1.9 %collective-permute-done.1.near = f32[64,128]{1,0:T(8,128)S(1)} collective-permute-done((f32[64,128]{1,0:T(8,128)S(1)}, f32[64,128]{1,0:T(8,128)S(1)}, u32[]{:S(2)}, u32[]{:S(2)}) %collective-permute-start.1) | collective-permute-done | bytes 32800 | tf_op jit(solution)/shard_map/ppermute | solution.py:594
  26.9 16.0 %all_to_all.45.around = f32[8,32,128]{2,1,0:T(8,128)S(1)} all-to-all(f32[8,32,128]{2,1,0:T(8,128)S(1)} %broadcast_in_dim.12), channel_id=1, replica_groups=mesh['y'=4,'x'=4,'core'=2,'z'=8] {'z'}, dimensions={0} | all-to-all | bytes 262144 | tf_op jit(solution)/shard_map/all_to_all | solution.py:580
  43.0 14.4 %all_to_all.46.got_mine = f32[16,16,128]{2,1,0:T(8,128)S(1)} all-to-all(f32[16,16,128]{2,1,0:T(8,128)S(1)} %broadcast_in_dim.13), channel_id=1, replica_groups=mesh['y'=4,'x'=4,'core'=2,'z'=8] {'y','x'}, dimensions={0} | all-to-all | bytes 262144 | tf_op jit(solution)/shard_map/all_to_all | solution.py:580
  57.4 1.8 %collective-permute-start.2 = (f32[16,16,128]{2,1,0:T(8,128)S(1)}, f32[16,16,128]{2,1,0:T(8,128)S(1)}, u32[]{:S(2)}, u32[]{:S(2)}) collective-permute-start(f32[16,16,128]{2,1,0:T(8,128)S(1)} %all_to_all.46.got_mine), channel_id=1, source_target_pairs={{0,8},{8,0},{1,9},{9,1},{2,10},{10,2},{3,11},{11,3},{4,12},{12,4},... | collective-permute-start | bytes 393224 | tf_op jit(solution)/shard_map/ppermute | solution.py:603
  59.2 1.0 collective-permute-done.2.got_other
  61.5 8.3 %expand_and_project.1 = (bf16[8,2,256,2048]{3,2,1,0:T(8,128)(2,1)}, f32[64,2048]{1,0:T(8,128)S(1)}, f32[16,24,128]{2,1,0:T(8,128)S(1)}, f32[448,128]{1,0:T(8,128...) custom-call(f32[16,16,128]{2,1,0:T(8,128)S(1)} %all_to_all.46.got_mine, ...), custom_call_target="tpu_custom_call" | custom-call | tf_op jit(solution)/shard_map/expand_and_project/pallas_call | solution.py:400
  70.3 1.1 collective-permute-done.3
  72.1 3.5 %all-to-all-start.3 = ((f32[16,24,128]{2,1,0:T(8,128)}), f32[16,24,128]{2,1,0:T(8,128)S(1)}, u32[]{:S(2)}, u32[]{:S(2)}) async-start(f32[16,24,128]{2,1,0:T(8,128)} %add.10), calls=%async_computation.3 | async-start | bytes 393216 | tf_op jit(solution)/shard_map/all_to_all | solution.py:580
  75.7 3.7 %collective-permute-start.4 = (f32[64,128]{1,0:T(8,128)S(1)}, f32[64,128]{1,0:T(8,128)S(1)}, u32[]{:S(2)}, u32[]{:S(2)}) collective-permute-start(f32[64,128]{1,0:T(8,128)S(1)} %get-tuple-element.44), channel_id=1, source_target_pairs={{8,16},{16,8},{24,32},{32,24},{40,48},{48,40},{56,64},{64,56},{72,... | collective-permute-start | bytes 98312 | tf_op jit(solution)/shard_map/ppermute | solution.py:594
  79.3 1.9 %collective-permute-done.4.near = f32[64,128]{1,0:T(8,128)S(1)} collective-permute-done((f32[64,128]{1,0:T(8,128)S(1)}, f32[64,128]{1,0:T(8,128)S(1)}, u32[]{:S(2)}, u32[]{:S(2)}) %collective-permute-start.4) | collective-permute-done | bytes 32800 | tf_op jit(solution)/shard_map/ppermute | solution.py:594
  81.2 2.2 %all-to-all-done.3 = f32[16,24,128]{2,1,0:T(8,128)S(1)} async-done(((f32[16,24,128]{2,1,0:T(8,128)}), f32[16,24,128]{2,1,0:T(8,128)S(1)}, u32[]{:S(2)}, u32[]{:S(2)}) %all-to-all-start.3) | async-done | bytes 196640 | tf_op jit(solution)/shard_map/all_to_all | solution.py:580
  83.4 10.5 %all_to_all.47.around = f32[8,40,128]{2,1,0:T(8,128)S(1)} all-to-all(f32[8,40,128]{2,1,0:T(8,128)S(1)} %broadcast_in_dim.14), channel_id=1, replica_groups=mesh['y'=4,'x'=4,'core'=2,'z'=8] {'z'}, dimensions={0} | all-to-all | bytes 327680 | tf_op jit(solution)/shard_map/all_to_all | solution.py:580
  93.9 14.4 %all_to_all.48.got_mine = f32[16,24,128]{2,1,0:T(8,128)S(1)} all-to-all(f32[16,24,128]{2,1,0:T(8,128)S(1)} %broadcast_in_dim.15), channel_id=1, replica_groups=mesh['y'=4,'x'=4,'core'=2,'z'=8] {'y','x'}, dimensions={0} | all-to-all | bytes 393216 | tf_op jit(solution)/shard_map/all_to_all | solution.py:580
  108.3 1.2 collective-permute-start.5
  109.6 1.1 collective-permute-done.5.got_other
  110.6 6.4 %factor_and_expand.1 = (f32[64,2048]{1,0:T(8,128)S(1)}, f32[128,128]{1,0:T(8,128)S(1)}, f32[128,128]{1,0:T(8,128)S(1)}, bf16[4,2,256,2048]{3,2,1,0:T(8,128)(2,1)S(1)}) custom-call(f32[16,24,128]{2,1,0:T(8,128)S(1)} %all_to_all.48.got_mine, f32[16,24,128]{2,1,0:T(8,128)S(1)} %collective-permute-done.5.got_other, ...), custom_call_target="tpu_custom_call" | custom-call | tf_op jit(solution)/shard_map/factor_and_expand/pallas_call | solution.py:459
  117.1 2.4 %collective-permute-start.6 = (f32[128,128]{1,0:T(8,128)S(1)}, f32[128,128]{1,0:T(8,128)S(1)}, u32[]{:S(2)}, u32[]{:S(2)}) collective-permute-start(f32[128,128]{1,0:T(8,128)S(1)} %get-tuple-element.51), channel_id=1, source_target_pairs={{0,8},{8,16},{16,24},{24,32},{32,40},{40,48},{48,56},{56,64},{64,7... | collective-permute-start | bytes 196616 | tf_op jit(solution)/shard_map/ppermute | solution.py:610
  119.5 2.4 %collective-permute-start.7 = (f32[128,128]{1,0:T(8,128)S(1)}, f32[128,128]{1,0:T(8,128)S(1)}, u32[]{:S(2)}, u32[]{:S(2)}) collective-permute-start(f32[128,128]{1,0:T(8,128)S(1)} %get-tuple-element.52), channel_id=1, source_target_pairs={{0,1},{1,2},{2,3},{3,4},{4,5},{5,6},{6,7},{8,9},{9,10},{10,11},{11... | collective-permute-start | bytes 196616 | tf_op jit(solution)/shard_map/ppermute | solution.py:610
  122.0 2.6 %project.1.base = f32[2,16,24,128]{3,2,1,0:T(8,128)S(1)} custom-call(bf16[4,2,256,2048]{3,2,1,0:T(8,128)(2,1)S(1)} %get-tuple-element.53.held, f32[64,2048]{1,0:T(8,128)S(1)} %get-tuple-element.50.field), custom_call_target="tpu_custom_call" | custom-call | tf_op jit(solution)/shard_map/project/pallas_call | solution.py:489
  124.6 0.9 roughness_products.1
  125.8 1.2 collective-permute-done.8
  127.0 12.4 %all_to_all.49 = f32[16,24,128]{2,1,0:T(8,128)S(1)} all-to-all(f32[16,24,128]{2,1,0:T(8,128)S(1)} %add.11), channel_id=1, replica_groups=mesh['y'=4,'x'=4,'core'=2,'z'=8] {'y','x'}, dimensions={0} | all-to-all | bytes 393216 | tf_op jit(solution)/shard_map/all_to_all | solution.py:580
  139.5 10.1 %all_to_all.50 = f32[8,24,128]{2,1,0:T(8,128)S(1)} all-to-all(f32[8,24,128]{2,1,0:T(8,128)S(1)} %broadcast_in_dim.16), channel_id=1, replica_groups=mesh['y'=4,'x'=4,'core'=2,'z'=8] {'z'}, dimensions={0} | all-to-all | bytes 196608 | tf_op jit(solution)/shard_map/all_to_all | solution.py:580
  149.7 9.8 %all_to_all.51.got_mine = f32[16,24,128]{2,1,0:T(8,128)S(1)} all-to-all(f32[16,24,128]{2,1,0:T(8,128)S(1)} %broadcast_in_dim.17), channel_id=1, replica_groups=mesh['y'=4,'x'=4,'core'=2,'z'=8] {'y','x'}, dimensions={0} | all-to-all | bytes 393216 | tf_op jit(solution)/shard_map/all_to_all | solution.py:580
  159.4 4.2 %collective-permute-start.9 = (f32[16,24,128]{2,1,0:T(8,128)S(1)}, f32[16,24,128]{2,1,0:T(8,128)S(1)}, u32[]{:S(2)}, u32[]{:S(2)}) collective-permute-start(f32[16,24,128]{2,1,0:T(8,128)S(1)} %all_to_all.51.got_mine), channel_id=1, source_target_pairs={{0,8},{8,0},{1,9},{9,1},{2,10},{10,2},{3,11},{11,3},{4,12},{12,4},... | collective-permute-start | bytes 589832 | tf_op jit(solution)/shard_map/ppermute | solution.py:603
  163.7 1.1 collective-permute-done.9.got_other
  164.8 3.2 %factor_and_finish.1 = (f32[1024,128]{1,0:T(8,128)}, f32[64,64]{1,0:T(8,128)}) custom-call(f32[16,24,128]{2,1,0:T(8,128)S(1)} %all_to_all.51.got_mine, f32[16,24,128]{2,1,0:T(8,128)S(1)} %collective-permute-done.9.got_other, f32[64,2048]{1,0:T(8,128)S(1)} %get-tuple-element.50.field), custom_call_target="tpu_custom_call" | custom-call | tf_op jit(solution)/shard_map/factor_and_finish/pallas_call | solution.py:561
  (36 shorter events, 5.4 us)
Async XLA Ops:
  0.6 0.7 copy-start
  10.0 100.7 %copy-start.2 = (s32[16,128]{1,0:T(8,128)S(1)}, s32[16,128]{1,0:T(8,128)}, u32[]{:S(2)}) copy-start(s32[16,128]{1,0:T(8,128)} %sea.3) | copy-start | bytes 24580
  10.0 100.7 %copy-start.4 = (f32[16,128]{1,0:T(8,128)S(1)}, f32[16,128]{1,0:T(8,128)}, u32[]{:S(2)}) copy-start(f32[16,128]{1,0:T(8,128)} %pen.5) | copy-start | bytes 24580
  10.0 4.4 %collective-permute-start = (f32[320,128]{1,0:T(8,128)S(1)}, f32[320,128]{1,0:T(8,128)S(1)}, u32[]{:S(2)}, u32[]{:S(2)}) collective-permute-start(f32[320,128]{1,0:T(8,128)S(1)} %get-tuple-element.31), channel_id=1, source_target_pairs={{0,8},{8,0},{1,9},{9,1},{2,10},{10,2},{3,11},{11,3},{4,12},{12,4},... | collective-permute-start | bytes 491528 | tf_op jit(solution)/shard_map/ppermute | solution.py:589
  15.0 11.9 %all-to-all-start = ((f32[16,16,128]{2,1,0:T(8,128)}), f32[16,16,128]{2,1,0:T(8,128)S(1)}, u32[]{:S(2)}, u32[]{:S(2)}) async-start(f32[16,16,128]{2,1,0:T(8,128)} %add.9), calls=%async_computation | async-start | bytes 262144 | tf_op jit(solution)/shard_map/all_to_all | solution.py:580
  20.0 6.0 %collective-permute-start.1 = (f32[64,128]{1,0:T(8,128)S(1)}, f32[64,128]{1,0:T(8,128)S(1)}, u32[]{:S(2)}, u32[]{:S(2)}) collective-permute-start(f32[64,128]{1,0:T(8,128)S(1)} %get-tuple-element.34), channel_id=1, source_target_pairs={{8,16},{16,8},{24,32},{32,24},{40,48},{48,40},{56,64},{64,56},{72,... | collective-permute-start | bytes 98312 | tf_op jit(solution)/shard_map/ppermute | solution.py:594
  57.4 2.8 %collective-permute-start.2 = (f32[16,16,128]{2,1,0:T(8,128)S(1)}, f32[16,16,128]{2,1,0:T(8,128)S(1)}, u32[]{:S(2)}, u32[]{:S(2)}) collective-permute-start(f32[16,16,128]{2,1,0:T(8,128)S(1)} %all_to_all.46.got_mine), channel_id=1, source_target_pairs={{0,8},{8,0},{1,9},{9,1},{2,10},{10,2},{3,11},{11,3},{4,12},{12,4},... | collective-permute-start | bytes 393224 | tf_op jit(solution)/shard_map/ppermute | solution.py:603
  60.1 0.7 copy-start.1
  60.8 0.7 copy-start.3
  69.8 1.6 collective-permute-start.3
  72.1 11.2 %all-to-all-start.3 = ((f32[16,24,128]{2,1,0:T(8,128)}), f32[16,24,128]{2,1,0:T(8,128)S(1)}, u32[]{:S(2)}, u32[]{:S(2)}) async-start(f32[16,24,128]{2,1,0:T(8,128)} %add.10), calls=%async_computation.3 | async-start | bytes 393216 | tf_op jit(solution)/shard_map/all_to_all | solution.py:580
  75.7 5.6 %collective-permute-start.4 = (f32[64,128]{1,0:T(8,128)S(1)}, f32[64,128]{1,0:T(8,128)S(1)}, u32[]{:S(2)}, u32[]{:S(2)}) collective-permute-start(f32[64,128]{1,0:T(8,128)S(1)} %get-tuple-element.44), channel_id=1, source_target_pairs={{8,16},{16,8},{24,32},{32,24},{40,48},{48,40},{56,64},{64,56},{72,... | collective-permute-start | bytes 98312 | tf_op jit(solution)/shard_map/ppermute | solution.py:594
  108.3 2.3 %collective-permute-start.5 = (f32[16,24,128]{2,1,0:T(8,128)S(1)}, f32[16,24,128]{2,1,0:T(8,128)S(1)}, u32[]{:S(2)}, u32[]{:S(2)}) collective-permute-start(f32[16,24,128]{2,1,0:T(8,128)S(1)} %all_to_all.48.got_mine), channel_id=1, source_target_pairs={{0,8},{8,0},{1,9},{9,1},{2,10},{10,2},{3,11},{11,3},{4,12},{12,4},... | collective-permute-start | bytes 589832 | tf_op jit(solution)/shard_map/ppermute | solution.py:603
  117.1 7.5 %collective-permute-start.6 = (f32[128,128]{1,0:T(8,128)S(1)}, f32[128,128]{1,0:T(8,128)S(1)}, u32[]{:S(2)}, u32[]{:S(2)}) collective-permute-start(f32[128,128]{1,0:T(8,128)S(1)} %get-tuple-element.51), channel_id=1, source_target_pairs={{0,8},{8,16},{16,24},{24,32},{32,40},{40,48},{48,56},{56,64},{64,7... | collective-permute-start | bytes 196616 | tf_op jit(solution)/shard_map/ppermute | solution.py:610
  119.5 5.0 %collective-permute-start.7 = (f32[128,128]{1,0:T(8,128)S(1)}, f32[128,128]{1,0:T(8,128)S(1)}, u32[]{:S(2)}, u32[]{:S(2)}) collective-permute-start(f32[128,128]{1,0:T(8,128)S(1)} %get-tuple-element.52), channel_id=1, source_target_pairs={{0,1},{1,2},{2,3},{3,4},{4,5},{5,6},{6,7},{8,9},{9,10},{10,11},{11... | collective-permute-start | bytes 196616 | tf_op jit(solution)/shard_map/ppermute | solution.py:610
  125.5 1.5 collective-permute-start.8
  159.4 5.3 %collective-permute-start.9 = (f32[16,24,128]{2,1,0:T(8,128)S(1)}, f32[16,24,128]{2,1,0:T(8,128)S(1)}, u32[]{:S(2)}, u32[]{:S(2)}) collective-permute-start(f32[16,24,128]{2,1,0:T(8,128)S(1)} %all_to_all.51.got_mine), channel_id=1, source_target_pairs={{0,8},{8,0},{1,9},{9,1},{2,10},{10,2},{3,11},{11,3},{4,12},{12,4},... | collective-permute-start | bytes 589832 | tf_op jit(solution)/shard_map/ppermute | solution.py:603

commit v7 on v4

--- a/solution.py
+++ b/solution.py
@@ -395,10 +395,19 @@
     )(*got, snap, prev, *sides, sea, pen)
 
 
+def solved(inverse, field, split):
+    for a in range(ROWS):
+        store_split(split, a, field[:, cols(a)])
+    high, low = parts(inverse)
+    left = [jnp.concatenate([part, part], axis=1) for part in (high, low)]
+    both = dot_nn(jnp.concatenate(left, axis=0), split[...])
+    return both[0:K] + both[K : 2 * K]
+
+
 def second_kernel(
     got_mine, got_other, snap, prev, pair, near, around, sea, pen,
     field, bottom, last, held,
-    full, spread, total, rough, raw, sems,
+    full, spread, total, rough, raw, split, sems,
 ):
     begin_copies(snap, held, sems)
     take_in(got_mine, got_other, full)
@@ -407,7 +416,7 @@
     rough_field(prev, take_in_edges(pair, near, around), pen, rough)
     expand(spread, snap, held, sems, total)
     applied_field(total, rough, sea, raw)
-    field[...] = dot_nn(inverse, raw[...], HIGHEST)
+    field[...] = solved(inverse, raw, split)
     bottom[0:K, :] = field[:, cols(ROWS - 1)]
     bottom[K : 2 * K, :] = field[:, cols(ROWS - 1)] * pen[ROWS - 1 : ROWS, :]
     _, last[0:K, :] = edge_columns(field)
@@ -431,6 +440,7 @@
         scratch_shapes=[
             *scratch_for_expand(SHARD),
             pltpu.VMEM((K, PTS), F32),
+            pltpu.VMEM((2 * K, PTS), BF16),
             pltpu.SemaphoreType.DMA((NBLOCK,)),
         ],
         compiler_params=pltpu.CompilerParams(vmem_limit_bytes=MIDDLE_LIMIT),
@@ -505,15 +515,16 @@
     )(field, north, west, pen, base)
 
 
-def last_kernel(got_mine, got_other, field, basis, matrix, full):
+def last_kernel(got_mine, got_other, field, basis, matrix, full, split, wide):
     take_in(got_mine, got_other, full)
     inverse = inverse_factor(square_of(full, 16))
-    solved = dot_nn(inverse, field[...], HIGHEST)
-    for a in range(ROWS):
-        basis[pl.ds(a, K, stride=ROWS), :] = solved[:, cols(a)]
-    turned = jnp.concatenate([coefficients_of(full, at) for at in range(NSNAP // LANES)], axis=1)
+    final = solved(inverse, field, split)
+    for a in range(ROWS):
+        basis[pl.ds(a, K, stride=ROWS), :] = final[:, cols(a)]
+    for at in range(NSNAP // LANES):
+        store_split(wide, at, coefficients_of(full, at))
     rough = square_of(full, 17)[:, 0:K]
-    gram = dot_nt(turned, turned, HIGHEST)
+    gram = folded(dot_nt(wide[...], wide[...]))[:, 0:K]
     middle = (gram * (1.0 / NPTS) + rough) * (1.0 / NPTS)
     matrix[...] = dot_nt(dot_nn(inverse, middle, HIGHEST), inverse, HIGHEST)
 
@@ -527,7 +538,11 @@
             jax.ShapeDtypeStruct((K * ROWS, LANES), F32),
             jax.ShapeDtypeStruct((K, K), F32),
         ],
-        scratch_shapes=[pltpu.VMEM((2, 16, SHARD, LANES), F32)],
+        scratch_shapes=[
+            pltpu.VMEM((2, 16, SHARD, LANES), F32),
+            pltpu.VMEM((2 * K, PTS), BF16),
+            pltpu.VMEM((2 * K, NSNAP), BF16),
+        ],
         compiler_params=pltpu.CompilerParams(vmem_limit_bytes=SMALL_LIMIT),
         name="factor_and_finish",
     )(*got, field)

time: 166 us -> 166 us (level)
  no operation moved by 1% of the time
where the time goes in v7:
time: 166 us; the launch traced here: 165 us
  blocking collectives  87.8 us (53%)
  starting transfers between devices  32.5 us (20%)
  Pallas kernels  28.6 us (17%)
  waiting for transfers between devices  13.3 us (8%)
    all_to_all x7, blocking collectives, exchange(): return lax.all_to_all(value, axis, 0, 0, tiled=True)  87.8 us
    all_to_all x2, starting transfers between devices, exchange(): return lax.all_to_all(value, axis, 0, 0, tiled=True)  8.73 us
    pallas_call x1, Pallas kernels, begin(): pl.pallas_call(begin_kernel, in_specs=[HBM, HBM, HBM], out_specs=[HB, *[V...  8.39 us
    ppermute x2, starting transfers between devices, summed_everywhere(): near = lax.ppermute(cross, LAT, CROSS)  7.74 us
    ppermute x3, starting transfers between devices, summed_everywhere(): both = (half, lax.ppermute(half, 'core', SWAP))  7.27 us
    pallas_call x1, Pallas kernels, first_step(): pl.pallas_call(first_kernel, in_specs=[VM, VM, HB, *[VM] * 6], out_specs=...  7.01 us
    pallas_call x1, Pallas kernels, second_step(): pl.pallas_call(second_kernel, in_specs=[VM, VM, HB, *[VM] * 6], out_specs...  6.32 us
    ppermute x2, starting transfers between devices, from_below(): return lax.ppermute(value, axis, [(i, i + 1) for i in range(count - 1)])  4.64 us
  transfers between devices with their start and end apart: 12, of which 10 were waited for; matrix products, arithmetic and copies ran while one was open for 0% of the time, Pallas kernels for 2%

profile of v7, /device:TPU:1, one launch (start us, length us, event | category | flops | bytes accessed | tf_op | source)
XLA Modules:
  0.0 165.3 jit_solution(4972546916760656994)
XLA Ops:
  1.3 8.4 %split_and_project.1 = (bf16[8,2,256,2048]{3,2,1,0:T(8,128)(2,1)}, f32[64,2048]{1,0:T(8,128)S(1)}, f32[16,16,128]{2,1,0:T(8,128)S(1)}, f32[320,128]{1,0:T(8,128)...) custom-call(f32[16384,128]{1,0:T(8,128)} %bitcast.6, f32[1024,128]{1,0:T(8,128)} %bitcast.8, s32[16,128]{1,0:T(8,128)S(1)} %copy-done), custom_call_target="tpu_custom_call" | custom-call | tf_op jit(solution)/shard_map/split_and_project/pallas_call | solution.py:289
  9.7 3.3 %collective-permute-start = (f32[320,128]{1,0:T(8,128)S(1)}, f32[320,128]{1,0:T(8,128)S(1)}, u32[]{:S(2)}, u32[]{:S(2)}) collective-permute-start(f32[320,128]{1,0:T(8,128)S(1)} %get-tuple-element.30), channel_id=1, source_target_pairs={{0,8},{8,0},{1,9},{9,1},{2,10},{10,2},{3,11},{11,3},{4,12},{12,4},... | collective-permute-start | bytes 491528 | tf_op jit(solution)/shard_map/ppermute | solution.py:562
  13.1 1.0 collective-permute-done
  14.8 5.0 %all-to-all-start = ((f32[16,16,128]{2,1,0:T(8,128)}), f32[16,16,128]{2,1,0:T(8,128)S(1)}, u32[]{:S(2)}, u32[]{:S(2)}) async-start(f32[16,16,128]{2,1,0:T(8,128)} %add.9), calls=%async_computation | async-start | bytes 262144 | tf_op jit(solution)/shard_map/all_to_all | solution.py:553
  19.8 4.1 %collective-permute-start.1 = (f32[64,128]{1,0:T(8,128)S(1)}, f32[64,128]{1,0:T(8,128)S(1)}, u32[]{:S(2)}, u32[]{:S(2)}) collective-permute-start(f32[64,128]{1,0:T(8,128)S(1)} %get-tuple-element.33), channel_id=1, source_target_pairs={{8,16},{16,8},{24,32},{32,24},{40,48},{48,40},{56,64},{64,56},{72,... | collective-permute-start | bytes 98312 | tf_op jit(solution)/shard_map/ppermute | solution.py:567
  23.9 1.9 %collective-permute-done.1.near = f32[64,128]{1,0:T(8,128)S(1)} collective-permute-done((f32[64,128]{1,0:T(8,128)S(1)}, f32[64,128]{1,0:T(8,128)S(1)}, u32[]{:S(2)}, u32[]{:S(2)}) %collective-permute-start.1) | collective-permute-done | bytes 32800 | tf_op jit(solution)/shard_map/ppermute | solution.py:567
  26.7 16.0 %all_to_all.45.around = f32[8,32,128]{2,1,0:T(8,128)S(1)} all-to-all(f32[8,32,128]{2,1,0:T(8,128)S(1)} %broadcast_in_dim.12), channel_id=1, replica_groups=mesh['y'=4,'x'=4,'core'=2,'z'=8] {'z'}, dimensions={0} | all-to-all | bytes 262144 | tf_op jit(solution)/shard_map/all_to_all | solution.py:553
  42.7 14.4 %all_to_all.46.got_mine = f32[16,16,128]{2,1,0:T(8,128)S(1)} all-to-all(f32[16,16,128]{2,1,0:T(8,128)S(1)} %broadcast_in_dim.13), channel_id=1, replica_groups=mesh['y'=4,'x'=4,'core'=2,'z'=8] {'y','x'}, dimensions={0} | all-to-all | bytes 262144 | tf_op jit(solution)/shard_map/all_to_all | solution.py:553
  57.1 1.8 %collective-permute-start.2 = (f32[16,16,128]{2,1,0:T(8,128)S(1)}, f32[16,16,128]{2,1,0:T(8,128)S(1)}, u32[]{:S(2)}, u32[]{:S(2)}) collective-permute-start(f32[16,16,128]{2,1,0:T(8,128)S(1)} %all_to_all.46.got_mine), channel_id=1, source_target_pairs={{0,8},{8,0},{1,9},{9,1},{2,10},{10,2},{3,11},{11,3},{4,12},{12,4},... | collective-permute-start | bytes 393224 | tf_op jit(solution)/shard_map/ppermute | solution.py:576
  58.9 1.0 collective-permute-done.2.got_other
  59.9 7.0 %expand_and_project.1 = (f32[64,2048]{1,0:T(8,128)S(1)}, f32[16,24,128]{2,1,0:T(8,128)S(1)}, f32[448,128]{1,0:T(8,128)S(1)}, f32[64,128]{1,0:T(8,128)S(1)}, f32[16,128]{1,0:T(8,128)S(1)}) custom-call(f32[16,16,128]{2,1,0:T(8,128)S(1)} %all_to_all.46.got_mine, f32[16,16,128]{2,1,0:T(8,128)S(1)} %collective-permute-done.2.got_other, ...), custom_call_target="tpu_custom_call" | custom-call | tf_op jit(solution)/shard_map/expand_and_project/pallas_call | solution.py:381
  67.4 1.1 collective-permute-done.3
  69.2 3.7 %all-to-all-start.3 = ((f32[16,24,128]{2,1,0:T(8,128)}), f32[16,24,128]{2,1,0:T(8,128)S(1)}, u32[]{:S(2)}, u32[]{:S(2)}) async-start(f32[16,24,128]{2,1,0:T(8,128)} %add.10), calls=%async_computation.3 | async-start | bytes 393216 | tf_op jit(solution)/shard_map/all_to_all | solution.py:553
  72.9 3.7 %collective-permute-start.4 = (f32[64,128]{1,0:T(8,128)S(1)}, f32[64,128]{1,0:T(8,128)S(1)}, u32[]{:S(2)}, u32[]{:S(2)}) collective-permute-start(f32[64,128]{1,0:T(8,128)S(1)} %get-tuple-element.43), channel_id=1, source_target_pairs={{8,16},{16,8},{24,32},{32,24},{40,48},{48,40},{56,64},{64,56},{72,... | collective-permute-start | bytes 98312 | tf_op jit(solution)/shard_map/ppermute | solution.py:567
  76.6 1.9 %collective-permute-done.4.near = f32[64,128]{1,0:T(8,128)S(1)} collective-permute-done((f32[64,128]{1,0:T(8,128)S(1)}, f32[64,128]{1,0:T(8,128)S(1)}, u32[]{:S(2)}, u32[]{:S(2)}) %collective-permute-start.4) | collective-permute-done | bytes 32800 | tf_op jit(solution)/shard_map/ppermute | solution.py:567
  78.5 2.2 %all-to-all-done.3 = f32[16,24,128]{2,1,0:T(8,128)S(1)} async-done(((f32[16,24,128]{2,1,0:T(8,128)}), f32[16,24,128]{2,1,0:T(8,128)S(1)}, u32[]{:S(2)}, u32[]{:S(2)}) %all-to-all-start.3) | async-done | bytes 196640 | tf_op jit(solution)/shard_map/all_to_all | solution.py:553
  80.7 10.5 %all_to_all.47.around = f32[8,40,128]{2,1,0:T(8,128)S(1)} all-to-all(f32[8,40,128]{2,1,0:T(8,128)S(1)} %broadcast_in_dim.14), channel_id=1, replica_groups=mesh['y'=4,'x'=4,'core'=2,'z'=8] {'z'}, dimensions={0} | all-to-all | bytes 327680 | tf_op jit(solution)/shard_map/all_to_all | solution.py:553
  91.2 14.4 %all_to_all.48.got_mine = f32[16,24,128]{2,1,0:T(8,128)S(1)} all-to-all(f32[16,24,128]{2,1,0:T(8,128)S(1)} %broadcast_in_dim.15), channel_id=1, replica_groups=mesh['y'=4,'x'=4,'core'=2,'z'=8] {'y','x'}, dimensions={0} | all-to-all | bytes 393216 | tf_op jit(solution)/shard_map/all_to_all | solution.py:553
  105.6 1.2 collective-permute-start.5
  106.8 1.1 collective-permute-done.5.got_other
  107.9 6.3 %factor_and_expand.1 = (f32[64,2048]{1,0:T(8,128)S(1)}, f32[128,128]{1,0:T(8,128)S(1)}, f32[128,128]{1,0:T(8,128)S(1)}, bf16[4,2,256,2048]{3,2,1,0:T(8,128)(2,1)S(1)}) custom-call(f32[16,24,128]{2,1,0:T(8,128)S(1)} %all_to_all.48.got_mine, f32[16,24,128]{2,1,0:T(8,128)S(1)} %collective-permute-done.5.got_other, ...), custom_call_target="tpu_custom_call" | custom-call | tf_op jit(solution)/shard_map/factor_and_expand/pallas_call | solution.py:430
  114.2 2.5 %collective-permute-start.6 = (f32[128,128]{1,0:T(8,128)S(1)}, f32[128,128]{1,0:T(8,128)S(1)}, u32[]{:S(2)}, u32[]{:S(2)}) collective-permute-start(f32[128,128]{1,0:T(8,128)S(1)} %get-tuple-element.49), channel_id=1, source_target_pairs={{0,8},{8,16},{16,24},{24,32},{32,40},{40,48},{48,56},{56,64},{64,7... | collective-permute-start | bytes 196616 | tf_op jit(solution)/shard_map/ppermute | solution.py:583
  116.7 2.2 %collective-permute-start.7 = (f32[128,128]{1,0:T(8,128)S(1)}, f32[128,128]{1,0:T(8,128)S(1)}, u32[]{:S(2)}, u32[]{:S(2)}) collective-permute-start(f32[128,128]{1,0:T(8,128)S(1)} %get-tuple-element.50), channel_id=1, source_target_pairs={{0,1},{1,2},{2,3},{3,4},{4,5},{5,6},{6,7},{8,9},{9,10},{10,11},{11... | collective-permute-start | bytes 196616 | tf_op jit(solution)/shard_map/ppermute | solution.py:583
  118.9 2.6 %project.1.base = f32[2,16,24,128]{3,2,1,0:T(8,128)S(1)} custom-call(bf16[4,2,256,2048]{3,2,1,0:T(8,128)(2,1)S(1)} %get-tuple-element.51.held, f32[64,2048]{1,0:T(8,128)S(1)} %get-tuple-element.48.field), custom_call_target="tpu_custom_call" | custom-call | tf_op jit(solution)/shard_map/project/pallas_call | solution.py:460
  121.5 0.9 roughness_products.1
  122.7 1.2 collective-permute-done.8
  123.9 12.4 %all_to_all.49 = f32[16,24,128]{2,1,0:T(8,128)S(1)} all-to-all(f32[16,24,128]{2,1,0:T(8,128)S(1)} %add.11), channel_id=1, replica_groups=mesh['y'=4,'x'=4,'core'=2,'z'=8] {'y','x'}, dimensions={0} | all-to-all | bytes 393216 | tf_op jit(solution)/shard_map/all_to_all | solution.py:553
  136.4 10.3 %all_to_all.50 = f32[8,24,128]{2,1,0:T(8,128)S(1)} all-to-all(f32[8,24,128]{2,1,0:T(8,128)S(1)} %broadcast_in_dim.16), channel_id=1, replica_groups=mesh['y'=4,'x'=4,'core'=2,'z'=8] {'z'}, dimensions={0} | all-to-all | bytes 196608 | tf_op jit(solution)/shard_map/all_to_all | solution.py:553
  146.8 9.8 %all_to_all.51.got_mine = f32[16,24,128]{2,1,0:T(8,128)S(1)} all-to-all(f32[16,24,128]{2,1,0:T(8,128)S(1)} %broadcast_in_dim.17), channel_id=1, replica_groups=mesh['y'=4,'x'=4,'core'=2,'z'=8] {'y','x'}, dimensions={0} | all-to-all | bytes 393216 | tf_op jit(solution)/shard_map/all_to_all | solution.py:553
  156.6 4.2 %collective-permute-start.9 = (f32[16,24,128]{2,1,0:T(8,128)S(1)}, f32[16,24,128]{2,1,0:T(8,128)S(1)}, u32[]{:S(2)}, u32[]{:S(2)}) collective-permute-start(f32[16,24,128]{2,1,0:T(8,128)S(1)} %all_to_all.51.got_mine), channel_id=1, source_target_pairs={{0,8},{8,0},{1,9},{9,1},{2,10},{10,2},{3,11},{11,3},{4,12},{12,4},... | collective-permute-start | bytes 589832 | tf_op jit(solution)/shard_map/ppermute | solution.py:576
  160.8 1.1 collective-permute-done.9.got_other
  161.9 3.4 %factor_and_finish.1 = (f32[1024,128]{1,0:T(8,128)}, f32[64,64]{1,0:T(8,128)}) custom-call(f32[16,24,128]{2,1,0:T(8,128)S(1)} %all_to_all.51.got_mine, f32[16,24,128]{2,1,0:T(8,128)S(1)} %collective-permute-done.9.got_other, f32[64,2048]{1,0:T(8,128)S(1)} %get-tuple-element.48.field), custom_call_target="tpu_custom_call" | custom-call | tf_op jit(solution)/shard_map/factor_and_finish/pallas_call | solution.py:533
  (32 shorter events, 4.0 us)
Async XLA Ops:
  0.6 0.7 copy-start
  1.3 58.6 %copy-start.1 = (s32[16,128]{1,0:T(8,128)S(1)}, s32[16,128]{1,0:T(8,128)}, u32[]{:S(2)}) copy-start(s32[16,128]{1,0:T(8,128)} %sea.3) | copy-start | bytes 24580
  1.3 58.6 %copy-start.2 = (f32[16,128]{1,0:T(8,128)S(1)}, f32[16,128]{1,0:T(8,128)}, u32[]{:S(2)}) copy-start(f32[16,128]{1,0:T(8,128)} %pen.5) | copy-start | bytes 24580
  9.7 4.3 %collective-permute-start = (f32[320,128]{1,0:T(8,128)S(1)}, f32[320,128]{1,0:T(8,128)S(1)}, u32[]{:S(2)}, u32[]{:S(2)}) collective-permute-start(f32[320,128]{1,0:T(8,128)S(1)} %get-tuple-element.30), channel_id=1, source_target_pairs={{0,8},{8,0},{1,9},{9,1},{2,10},{10,2},{3,11},{11,3},{4,12},{12,4},... | collective-permute-start | bytes 491528 | tf_op jit(solution)/shard_map/ppermute | solution.py:562
  14.8 11.9 %all-to-all-start = ((f32[16,16,128]{2,1,0:T(8,128)}), f32[16,16,128]{2,1,0:T(8,128)S(1)}, u32[]{:S(2)}, u32[]{:S(2)}) async-start(f32[16,16,128]{2,1,0:T(8,128)} %add.9), calls=%async_computation | async-start | bytes 262144 | tf_op jit(solution)/shard_map/all_to_all | solution.py:553
  19.8 6.0 %collective-permute-start.1 = (f32[64,128]{1,0:T(8,128)S(1)}, f32[64,128]{1,0:T(8,128)S(1)}, u32[]{:S(2)}, u32[]{:S(2)}) collective-permute-start(f32[64,128]{1,0:T(8,128)S(1)} %get-tuple-element.33), channel_id=1, source_target_pairs={{8,16},{16,8},{24,32},{32,24},{40,48},{48,40},{56,64},{64,56},{72,... | collective-permute-start | bytes 98312 | tf_op jit(solution)/shard_map/ppermute | solution.py:567
  57.1 2.8 %collective-permute-start.2 = (f32[16,16,128]{2,1,0:T(8,128)S(1)}, f32[16,16,128]{2,1,0:T(8,128)S(1)}, u32[]{:S(2)}, u32[]{:S(2)}) collective-permute-start(f32[16,16,128]{2,1,0:T(8,128)S(1)} %all_to_all.46.got_mine), channel_id=1, source_target_pairs={{0,8},{8,0},{1,9},{9,1},{2,10},{10,2},{3,11},{11,3},{4,12},{12,4},... | collective-permute-start | bytes 393224 | tf_op jit(solution)/shard_map/ppermute | solution.py:576
  66.9 1.6 collective-permute-start.3
  69.2 11.4 %all-to-all-start.3 = ((f32[16,24,128]{2,1,0:T(8,128)}), f32[16,24,128]{2,1,0:T(8,128)S(1)}, u32[]{:S(2)}, u32[]{:S(2)}) async-start(f32[16,24,128]{2,1,0:T(8,128)} %add.10), calls=%async_computation.3 | async-start | bytes 393216 | tf_op jit(solution)/shard_map/all_to_all | solution.py:553
  72.9 5.6 %collective-permute-start.4 = (f32[64,128]{1,0:T(8,128)S(1)}, f32[64,128]{1,0:T(8,128)S(1)}, u32[]{:S(2)}, u32[]{:S(2)}) collective-permute-start(f32[64,128]{1,0:T(8,128)S(1)} %get-tuple-element.43), channel_id=1, source_target_pairs={{8,16},{16,8},{24,32},{32,24},{40,48},{48,40},{56,64},{64,56},{72,... | collective-permute-start | bytes 98312 | tf_op jit(solution)/shard_map/ppermute | solution.py:567
  105.6 2.3 %collective-permute-start.5 = (f32[16,24,128]{2,1,0:T(8,128)S(1)}, f32[16,24,128]{2,1,0:T(8,128)S(1)}, u32[]{:S(2)}, u32[]{:S(2)}) collective-permute-start(f32[16,24,128]{2,1,0:T(8,128)S(1)} %all_to_all.48.got_mine), channel_id=1, source_target_pairs={{0,8},{8,0},{1,9},{9,1},{2,10},{10,2},{3,11},{11,3},{4,12},{12,4},... | collective-permute-start | bytes 589832 | tf_op jit(solution)/shard_map/ppermute | solution.py:576
  114.2 7.2 %collective-permute-start.6 = (f32[128,128]{1,0:T(8,128)S(1)}, f32[128,128]{1,0:T(8,128)S(1)}, u32[]{:S(2)}, u32[]{:S(2)}) collective-permute-start(f32[128,128]{1,0:T(8,128)S(1)} %get-tuple-element.49), channel_id=1, source_target_pairs={{0,8},{8,16},{16,24},{24,32},{32,40},{40,48},{48,56},{56,64},{64,7... | collective-permute-start | bytes 196616 | tf_op jit(solution)/shard_map/ppermute | solution.py:583
  116.7 4.8 %collective-permute-start.7 = (f32[128,128]{1,0:T(8,128)S(1)}, f32[128,128]{1,0:T(8,128)S(1)}, u32[]{:S(2)}, u32[]{:S(2)}) collective-permute-start(f32[128,128]{1,0:T(8,128)S(1)} %get-tuple-element.50), channel_id=1, source_target_pairs={{0,1},{1,2},{2,3},{3,4},{4,5},{5,6},{6,7},{8,9},{9,10},{10,11},{11... | collective-permute-start | bytes 196616 | tf_op jit(solution)/shard_map/ppermute | solution.py:583
  122.4 1.5 collective-permute-start.8
  156.6 5.3 %collective-permute-start.9 = (f32[16,24,128]{2,1,0:T(8,128)S(1)}, f32[16,24,128]{2,1,0:T(8,128)S(1)}, u32[]{:S(2)}, u32[]{:S(2)}) collective-permute-start(f32[16,24,128]{2,1,0:T(8,128)S(1)} %all_to_all.51.got_mine), channel_id=1, source_target_pairs={{0,8},{8,0},{1,9},{9,1},{2,10},{10,2},{3,11},{11,3},{4,12},{12,4},... | collective-permute-start | bytes 589832 | tf_op jit(solution)/shard_map/ppermute | solution.py:576

commit v8 on v7

--- a/solution.py
+++ b/solution.py
@@ -122,10 +122,10 @@
 def take_in_edges(pair, cross, columns):
     me = lax.axis_index("core")
     z = lax.axis_index("z")
-    depth = columns.shape[1] - 16
+    depth = columns.shape[1] - 8
     north = jnp.where(me == 0, cross[...], pair[...])
     south = jnp.where(me == 0, pair[...], cross[...])
-    before = columns[jnp.maximum(z - 1, 0), depth + 8 : depth + 16, :]
+    before = columns[jnp.maximum(z - 1, 0), depth : depth + 8, :]
     after = columns[jnp.minimum(z + 1, 7), depth : depth + 8, :]
     west = unpacked_columns(jnp.where(z > 0, before, 0.0))
     east = unpacked_columns(jnp.where(z < 7, after, 0.0))
@@ -515,16 +515,15 @@
     )(field, north, west, pen, base)
 
 
-def last_kernel(got_mine, got_other, field, basis, matrix, full, split, wide):
+def last_kernel(got_mine, got_other, field, basis, matrix, full, split):
     take_in(got_mine, got_other, full)
     inverse = inverse_factor(square_of(full, 16))
     final = solved(inverse, field, split)
     for a in range(ROWS):
         basis[pl.ds(a, K, stride=ROWS), :] = final[:, cols(a)]
-    for at in range(NSNAP // LANES):
-        store_split(wide, at, coefficients_of(full, at))
+    turned = jnp.concatenate([coefficients_of(full, at) for at in range(NSNAP // LANES)], axis=1)
     rough = square_of(full, 17)[:, 0:K]
-    gram = folded(dot_nt(wide[...], wide[...]))[:, 0:K]
+    gram = dot_nt(turned, turned, HIGHEST)
     middle = (gram * (1.0 / NPTS) + rough) * (1.0 / NPTS)
     matrix[...] = dot_nt(dot_nn(inverse, middle, HIGHEST), inverse, HIGHEST)
 
@@ -541,7 +540,6 @@
         scratch_shapes=[
             pltpu.VMEM((2, 16, SHARD, LANES), F32),
             pltpu.VMEM((2 * K, PTS), BF16),
-            pltpu.VMEM((2 * K, NSNAP), BF16),
         ],
         compiler_params=pltpu.CompilerParams(vmem_limit_bytes=SMALL_LIMIT),
         name="factor_and_finish",
@@ -568,10 +566,11 @@
     shares = exchange(pair, CHIPS)
     if edges is not None:
         shares, near = lax.optimization_barrier((shares, near))
-    share = shares.sum(axis=0)
+    sent = copies(shares.sum(axis=0), 8)
     if edges is not None:
-        share = jnp.concatenate([share, columns], axis=0)
-    around = exchange(copies(share, 8), "z")
+        below = lax.broadcasted_iota(jnp.int32, (8, 1, 1), 0) < lax.axis_index("z")
+        sent = jnp.concatenate([sent, jnp.where(below, columns[0:8], columns[8:16])], axis=1)
+    around = exchange(sent, "z")
     half = exchange(copies(around[:, :depth].sum(axis=0), 16), CHIPS)
     both = (half, lax.ppermute(half, "core", SWAP))
     if edges is None:

time: 166 us -> 165 us (level)
  no operation moved by 1% of the time
where the time goes in v8:
time: 165 us; the launch traced here: 164 us
  blocking collectives  86.5 us (52%)
  starting transfers between devices  32.5 us (20%)
  Pallas kernels  28.4 us (17%)
  waiting for transfers between devices  13.1 us (8%)
  other arithmetic  1.67 us (1%)
    all_to_all x7, blocking collectives, exchange(): return lax.all_to_all(value, axis, 0, 0, tiled=True)  86.5 us
    all_to_all x2, starting transfers between devices, exchange(): return lax.all_to_all(value, axis, 0, 0, tiled=True)  8.73 us
    pallas_call x1, Pallas kernels, begin(): pl.pallas_call(begin_kernel, in_specs=[HBM, HBM, HBM], out_specs=[HB, *[V...  8.4 us
    ppermute x2, starting transfers between devices, summed_everywhere(): near = lax.ppermute(cross, LAT, CROSS)  7.74 us
    ppermute x3, starting transfers between devices, summed_everywhere(): both = (half, lax.ppermute(half, 'core', SWAP))  7.3 us
    pallas_call x1, Pallas kernels, first_step(): pl.pallas_call(first_kernel, in_specs=[VM, VM, HB, *[VM] * 6], out_specs=...  7.02 us
    pallas_call x1, Pallas kernels, second_step(): pl.pallas_call(second_kernel, in_specs=[VM, VM, HB, *[VM] * 6], out_specs...  6.32 us
    ppermute x2, starting transfers between devices, from_below(): return lax.ppermute(value, axis, [(i, i + 1) for i in range(count - 1)])  4.65 us
  transfers between devices with their start and end apart: 12, of which 10 were waited for; matrix products, arithmetic and copies ran while one was open for 0% of the time, Pallas kernels for 2%

profile of v8, /device:TPU:1, one launch (start us, length us, event | category | flops | bytes accessed | tf_op | source)
XLA Modules:
  0.0 163.8 jit_solution(15388130583734179572)
XLA Ops:
  1.3 8.4 %split_and_project.1 = (bf16[8,2,256,2048]{3,2,1,0:T(8,128)(2,1)}, f32[64,2048]{1,0:T(8,128)S(1)}, f32[16,16,128]{2,1,0:T(8,128)S(1)}, f32[320,128]{1,0:T(8,128)...) custom-call(f32[16384,128]{1,0:T(8,128)} %bitcast.6, f32[1024,128]{1,0:T(8,128)} %bitcast.8, s32[16,128]{1,0:T(8,128)S(1)} %copy-done), custom_call_target="tpu_custom_call" | custom-call | tf_op jit(solution)/shard_map/split_and_project/pallas_call | solution.py:289
  9.7 3.3 %collective-permute-start = (f32[320,128]{1,0:T(8,128)S(1)}, f32[320,128]{1,0:T(8,128)S(1)}, u32[]{:S(2)}, u32[]{:S(2)}) collective-permute-start(f32[320,128]{1,0:T(8,128)S(1)} %get-tuple-element.30), channel_id=1, source_target_pairs={{0,8},{8,0},{1,9},{9,1},{2,10},{10,2},{3,11},{11,3},{4,12},{12,4},... | collective-permute-start | bytes 491528 | tf_op jit(solution)/shard_map/ppermute | solution.py:560
  13.1 1.0 collective-permute-done
  14.8 5.0 %all-to-all-start = ((f32[16,16,128]{2,1,0:T(8,128)}), f32[16,16,128]{2,1,0:T(8,128)S(1)}, u32[]{:S(2)}, u32[]{:S(2)}) async-start(f32[16,16,128]{2,1,0:T(8,128)} %add.9), calls=%async_computation | async-start | bytes 262144 | tf_op jit(solution)/shard_map/all_to_all | solution.py:551
  19.8 4.1 %collective-permute-start.1 = (f32[64,128]{1,0:T(8,128)S(1)}, f32[64,128]{1,0:T(8,128)S(1)}, u32[]{:S(2)}, u32[]{:S(2)}) collective-permute-start(f32[64,128]{1,0:T(8,128)S(1)} %get-tuple-element.33), channel_id=1, source_target_pairs={{8,16},{16,8},{24,32},{32,24},{40,48},{48,40},{56,64},{64,56},{72,... | collective-permute-start | bytes 98312 | tf_op jit(solution)/shard_map/ppermute | solution.py:565
  24.0 1.8 %collective-permute-done.1.near = f32[64,128]{1,0:T(8,128)S(1)} collective-permute-done((f32[64,128]{1,0:T(8,128)S(1)}, f32[64,128]{1,0:T(8,128)S(1)}, u32[]{:S(2)}, u32[]{:S(2)}) %collective-permute-start.1) | collective-permute-done | bytes 32800 | tf_op jit(solution)/shard_map/ppermute | solution.py:565
  26.7 15.7 %all_to_all.45.around = f32[8,24,128]{2,1,0:T(8,128)S(1)} all-to-all(f32[8,24,128]{2,1,0:T(8,128)S(1)} %pad_maximum_fusion.1), channel_id=1, replica_groups=mesh['y'=4,'x'=4,'core'=2,'z'=8] {'z'}, dimensions={0} | all-to-all | bytes 196608 | tf_op jit(solution)/shard_map/all_to_all | solution.py:551
  42.4 14.1 %all_to_all.46.got_mine = f32[16,16,128]{2,1,0:T(8,128)S(1)} all-to-all(f32[16,16,128]{2,1,0:T(8,128)S(1)} %broadcast_in_dim.65), channel_id=1, replica_groups=mesh['y'=4,'x'=4,'core'=2,'z'=8] {'y','x'}, dimensions={0} | all-to-all | bytes 262144 | tf_op jit(solution)/shard_map/all_to_all | solution.py:551
  56.5 1.8 %collective-permute-start.2 = (f32[16,16,128]{2,1,0:T(8,128)S(1)}, f32[16,16,128]{2,1,0:T(8,128)S(1)}, u32[]{:S(2)}, u32[]{:S(2)}) collective-permute-start(f32[16,16,128]{2,1,0:T(8,128)S(1)} %all_to_all.46.got_mine), channel_id=1, source_target_pairs={{0,8},{8,0},{1,9},{9,1},{2,10},{10,2},{3,11},{11,3},{4,12},{12,4},... | collective-permute-start | bytes 393224 | tf_op jit(solution)/shard_map/ppermute | solution.py:575
  58.4 1.0 collective-permute-done.2.got_other
  59.4 7.0 %expand_and_project.1 = (f32[64,2048]{1,0:T(8,128)S(1)}, f32[16,24,128]{2,1,0:T(8,128)S(1)}, f32[448,128]{1,0:T(8,128)S(1)}, f32[64,128]{1,0:T(8,128)S(1)}, f32[16,128]{1,0:T(8,128)S(1)}) custom-call(f32[16,16,128]{2,1,0:T(8,128)S(1)} %all_to_all.46.got_mine, f32[16,16,128]{2,1,0:T(8,128)S(1)} %collective-permute-done.2.got_other, ...), custom_call_target="tpu_custom_call" | custom-call | tf_op jit(solution)/shard_map/expand_and_project/pallas_call | solution.py:381
  66.8 1.1 collective-permute-done.3
  68.7 3.7 %all-to-all-start.3 = ((f32[16,24,128]{2,1,0:T(8,128)}), f32[16,24,128]{2,1,0:T(8,128)S(1)}, u32[]{:S(2)}, u32[]{:S(2)}) async-start(f32[16,24,128]{2,1,0:T(8,128)} %add.10), calls=%async_computation.3 | async-start | bytes 393216 | tf_op jit(solution)/shard_map/all_to_all | solution.py:551
  72.4 3.7 %collective-permute-start.4 = (f32[64,128]{1,0:T(8,128)S(1)}, f32[64,128]{1,0:T(8,128)S(1)}, u32[]{:S(2)}, u32[]{:S(2)}) collective-permute-start(f32[64,128]{1,0:T(8,128)S(1)} %get-tuple-element.43), channel_id=1, source_target_pairs={{8,16},{16,8},{24,32},{32,24},{40,48},{48,40},{56,64},{64,56},{72,... | collective-permute-start | bytes 98312 | tf_op jit(solution)/shard_map/ppermute | solution.py:565
  76.1 1.8 %collective-permute-done.4.near = f32[64,128]{1,0:T(8,128)S(1)} collective-permute-done((f32[64,128]{1,0:T(8,128)S(1)}, f32[64,128]{1,0:T(8,128)S(1)}, u32[]{:S(2)}, u32[]{:S(2)}) %collective-permute-start.4) | collective-permute-done | bytes 32800 | tf_op jit(solution)/shard_map/ppermute | solution.py:565
  77.9 2.2 %all-to-all-done.3 = f32[16,24,128]{2,1,0:T(8,128)S(1)} async-done(((f32[16,24,128]{2,1,0:T(8,128)}), f32[16,24,128]{2,1,0:T(8,128)S(1)}, u32[]{:S(2)}, u32[]{:S(2)}) %all-to-all-start.3) | async-done | bytes 196640 | tf_op jit(solution)/shard_map/all_to_all | solution.py:551
  80.2 10.3 %all_to_all.47.around = f32[8,32,128]{2,1,0:T(8,128)S(1)} all-to-all(f32[8,32,128]{2,1,0:T(8,128)S(1)} %pad_maximum_fusion), channel_id=1, replica_groups=mesh['y'=4,'x'=4,'core'=2,'z'=8] {'z'}, dimensions={0} | all-to-all | bytes 262144 | tf_op jit(solution)/shard_map/all_to_all | solution.py:551
  90.5 13.8 %all_to_all.48.got_mine = f32[16,24,128]{2,1,0:T(8,128)S(1)} all-to-all(f32[16,24,128]{2,1,0:T(8,128)S(1)} %broadcast_in_dim.69), channel_id=1, replica_groups=mesh['y'=4,'x'=4,'core'=2,'z'=8] {'y','x'}, dimensions={0} | all-to-all | bytes 393216 | tf_op jit(solution)/shard_map/all_to_all | solution.py:551
  104.3 1.2 collective-permute-start.5
  105.6 1.1 collective-permute-done.5.got_other
  106.6 6.3 %factor_and_expand.1 = (f32[64,2048]{1,0:T(8,128)S(1)}, f32[128,128]{1,0:T(8,128)S(1)}, f32[128,128]{1,0:T(8,128)S(1)}, bf16[4,2,256,2048]{3,2,1,0:T(8,128)(2,1)S(1)}) custom-call(f32[16,24,128]{2,1,0:T(8,128)S(1)} %all_to_all.48.got_mine, f32[16,24,128]{2,1,0:T(8,128)S(1)} %collective-permute-done.5.got_other, ...), custom_call_target="tpu_custom_call" | custom-call | tf_op jit(solution)/shard_map/factor_and_expand/pallas_call | solution.py:430
  113.0 2.5 %collective-permute-start.6 = (f32[128,128]{1,0:T(8,128)S(1)}, f32[128,128]{1,0:T(8,128)S(1)}, u32[]{:S(2)}, u32[]{:S(2)}) collective-permute-start(f32[128,128]{1,0:T(8,128)S(1)} %get-tuple-element.49), channel_id=1, source_target_pairs={{0,8},{8,16},{16,24},{24,32},{32,40},{40,48},{48,56},{56,64},{64,7... | collective-permute-start | bytes 196616 | tf_op jit(solution)/shard_map/ppermute | solution.py:582
  115.4 2.2 %collective-permute-start.7 = (f32[128,128]{1,0:T(8,128)S(1)}, f32[128,128]{1,0:T(8,128)S(1)}, u32[]{:S(2)}, u32[]{:S(2)}) collective-permute-start(f32[128,128]{1,0:T(8,128)S(1)} %get-tuple-element.50), channel_id=1, source_target_pairs={{0,1},{1,2},{2,3},{3,4},{4,5},{5,6},{6,7},{8,9},{9,10},{10,11},{11... | collective-permute-start | bytes 196616 | tf_op jit(solution)/shard_map/ppermute | solution.py:582
  117.6 2.6 %project.1.base = f32[2,16,24,128]{3,2,1,0:T(8,128)S(1)} custom-call(bf16[4,2,256,2048]{3,2,1,0:T(8,128)(2,1)S(1)} %get-tuple-element.51.held, f32[64,2048]{1,0:T(8,128)S(1)} %get-tuple-element.48.field), custom_call_target="tpu_custom_call" | custom-call | tf_op jit(solution)/shard_map/project/pallas_call | solution.py:460
  120.2 0.9 roughness_products.1
  121.5 1.2 collective-permute-done.8
  122.7 12.4 %all_to_all.49 = f32[16,24,128]{2,1,0:T(8,128)S(1)} all-to-all(f32[16,24,128]{2,1,0:T(8,128)S(1)} %add.11), channel_id=1, replica_groups=mesh['y'=4,'x'=4,'core'=2,'z'=8] {'y','x'}, dimensions={0} | all-to-all | bytes 393216 | tf_op jit(solution)/shard_map/all_to_all | solution.py:551
  135.2 10.3 %all_to_all.50 = f32[8,24,128]{2,1,0:T(8,128)S(1)} all-to-all(f32[8,24,128]{2,1,0:T(8,128)S(1)} %broadcast_in_dim.70), channel_id=1, replica_groups=mesh['y'=4,'x'=4,'core'=2,'z'=8] {'z'}, dimensions={0} | all-to-all | bytes 196608 | tf_op jit(solution)/shard_map/all_to_all | solution.py:551
  145.5 9.8 %all_to_all.51.got_mine = f32[16,24,128]{2,1,0:T(8,128)S(1)} all-to-all(f32[16,24,128]{2,1,0:T(8,128)S(1)} %broadcast_in_dim.71), channel_id=1, replica_groups=mesh['y'=4,'x'=4,'core'=2,'z'=8] {'y','x'}, dimensions={0} | all-to-all | bytes 393216 | tf_op jit(solution)/shard_map/all_to_all | solution.py:551
  155.3 4.2 %collective-permute-start.9 = (f32[16,24,128]{2,1,0:T(8,128)S(1)}, f32[16,24,128]{2,1,0:T(8,128)S(1)}, u32[]{:S(2)}, u32[]{:S(2)}) collective-permute-start(f32[16,24,128]{2,1,0:T(8,128)S(1)} %all_to_all.51.got_mine), channel_id=1, source_target_pairs={{0,8},{8,0},{1,9},{9,1},{2,10},{10,2},{3,11},{11,3},{4,12},{12,4},... | collective-permute-start | bytes 589832 | tf_op jit(solution)/shard_map/ppermute | solution.py:575
  159.6 1.1 collective-permute-done.9.got_other
  160.6 3.2 %factor_and_finish.1 = (f32[1024,128]{1,0:T(8,128)}, f32[64,64]{1,0:T(8,128)}) custom-call(f32[16,24,128]{2,1,0:T(8,128)S(1)} %all_to_all.51.got_mine, f32[16,24,128]{2,1,0:T(8,128)S(1)} %collective-permute-done.9.got_other, f32[64,2048]{1,0:T(8,128)S(1)} %get-tuple-element.48.field), custom_call_target="tpu_custom_call" | custom-call | tf_op jit(solution)/shard_map/factor_and_finish/pallas_call | solution.py:532
  (37 shorter events, 4.1 us)
Async XLA Ops:
  0.6 0.7 copy-start
  1.3 58.0 %copy-start.1 = (s32[16,128]{1,0:T(8,128)S(1)}, s32[16,128]{1,0:T(8,128)}, u32[]{:S(2)}) copy-start(s32[16,128]{1,0:T(8,128)} %sea.3) | copy-start | bytes 24580
  1.3 58.0 %copy-start.2 = (f32[16,128]{1,0:T(8,128)S(1)}, f32[16,128]{1,0:T(8,128)}, u32[]{:S(2)}) copy-start(f32[16,128]{1,0:T(8,128)} %pen.5) | copy-start | bytes 24580
  9.7 4.3 %collective-permute-start = (f32[320,128]{1,0:T(8,128)S(1)}, f32[320,128]{1,0:T(8,128)S(1)}, u32[]{:S(2)}, u32[]{:S(2)}) collective-permute-start(f32[320,128]{1,0:T(8,128)S(1)} %get-tuple-element.30), channel_id=1, source_target_pairs={{0,8},{8,0},{1,9},{9,1},{2,10},{10,2},{3,11},{11,3},{4,12},{12,4},... | collective-permute-start | bytes 491528 | tf_op jit(solution)/shard_map/ppermute | solution.py:560
  14.8 11.9 %all-to-all-start = ((f32[16,16,128]{2,1,0:T(8,128)}), f32[16,16,128]{2,1,0:T(8,128)S(1)}, u32[]{:S(2)}, u32[]{:S(2)}) async-start(f32[16,16,128]{2,1,0:T(8,128)} %add.9), calls=%async_computation | async-start | bytes 262144 | tf_op jit(solution)/shard_map/all_to_all | solution.py:551
  19.8 6.0 %collective-permute-start.1 = (f32[64,128]{1,0:T(8,128)S(1)}, f32[64,128]{1,0:T(8,128)S(1)}, u32[]{:S(2)}, u32[]{:S(2)}) collective-permute-start(f32[64,128]{1,0:T(8,128)S(1)} %get-tuple-element.33), channel_id=1, source_target_pairs={{8,16},{16,8},{24,32},{32,24},{40,48},{48,40},{56,64},{64,56},{72,... | collective-permute-start | bytes 98312 | tf_op jit(solution)/shard_map/ppermute | solution.py:565
  56.5 2.8 %collective-permute-start.2 = (f32[16,16,128]{2,1,0:T(8,128)S(1)}, f32[16,16,128]{2,1,0:T(8,128)S(1)}, u32[]{:S(2)}, u32[]{:S(2)}) collective-permute-start(f32[16,16,128]{2,1,0:T(8,128)S(1)} %all_to_all.46.got_mine), channel_id=1, source_target_pairs={{0,8},{8,0},{1,9},{9,1},{2,10},{10,2},{3,11},{11,3},{4,12},{12,4},... | collective-permute-start | bytes 393224 | tf_op jit(solution)/shard_map/ppermute | solution.py:575
  66.4 1.6 collective-permute-start.3
  68.7 11.4 %all-to-all-start.3 = ((f32[16,24,128]{2,1,0:T(8,128)}), f32[16,24,128]{2,1,0:T(8,128)S(1)}, u32[]{:S(2)}, u32[]{:S(2)}) async-start(f32[16,24,128]{2,1,0:T(8,128)} %add.10), calls=%async_computation.3 | async-start | bytes 393216 | tf_op jit(solution)/shard_map/all_to_all | solution.py:551
  72.4 5.6 %collective-permute-start.4 = (f32[64,128]{1,0:T(8,128)S(1)}, f32[64,128]{1,0:T(8,128)S(1)}, u32[]{:S(2)}, u32[]{:S(2)}) collective-permute-start(f32[64,128]{1,0:T(8,128)S(1)} %get-tuple-element.43), channel_id=1, source_target_pairs={{8,16},{16,8},{24,32},{32,24},{40,48},{48,40},{56,64},{64,56},{72,... | collective-permute-start | bytes 98312 | tf_op jit(solution)/shard_map/ppermute | solution.py:565
  104.3 2.3 %collective-permute-start.5 = (f32[16,24,128]{2,1,0:T(8,128)S(1)}, f32[16,24,128]{2,1,0:T(8,128)S(1)}, u32[]{:S(2)}, u32[]{:S(2)}) collective-permute-start(f32[16,24,128]{2,1,0:T(8,128)S(1)} %all_to_all.48.got_mine), channel_id=1, source_target_pairs={{0,8},{8,0},{1,9},{9,1},{2,10},{10,2},{3,11},{11,3},{4,12},{12,4},... | collective-permute-start | bytes 589832 | tf_op jit(solution)/shard_map/ppermute | solution.py:575
  113.0 7.2 %collective-permute-start.6 = (f32[128,128]{1,0:T(8,128)S(1)}, f32[128,128]{1,0:T(8,128)S(1)}, u32[]{:S(2)}, u32[]{:S(2)}) collective-permute-start(f32[128,128]{1,0:T(8,128)S(1)} %get-tuple-element.49), channel_id=1, source_target_pairs={{0,8},{8,16},{16,24},{24,32},{32,40},{40,48},{48,56},{56,64},{64,7... | collective-permute-start | bytes 196616 | tf_op jit(solution)/shard_map/ppermute | solution.py:582
  115.4 4.8 %collective-permute-start.7 = (f32[128,128]{1,0:T(8,128)S(1)}, f32[128,128]{1,0:T(8,128)S(1)}, u32[]{:S(2)}, u32[]{:S(2)}) collective-permute-start(f32[128,128]{1,0:T(8,128)S(1)} %get-tuple-element.50), channel_id=1, source_target_pairs={{0,1},{1,2},{2,3},{3,4},{4,5},{5,6},{6,7},{8,9},{9,10},{10,11},{11... | collective-permute-start | bytes 196616 | tf_op jit(solution)/shard_map/ppermute | solution.py:582
  121.1 1.5 collective-permute-start.8
  155.3 5.3 %collective-permute-start.9 = (f32[16,24,128]{2,1,0:T(8,128)S(1)}, f32[16,24,128]{2,1,0:T(8,128)S(1)}, u32[]{:S(2)}, u32[]{:S(2)}) collective-permute-start(f32[16,24,128]{2,1,0:T(8,128)S(1)} %all_to_all.51.got_mine), channel_id=1, source_target_pairs={{0,8},{8,0},{1,9},{9,1},{2,10},{10,2},{3,11},{11,3},{4,12},{12,4},... | collective-permute-start | bytes 589832 | tf_op jit(solution)/shard_map/ppermute | solution.py:575
